TPU v7x, 256 devices: a whole 4x4x8 slice. The times are simulated.
256 devices in a mesh: px: 16 (over z_lo, y, core), py: 16 (over x, z_hi).
Axes of the slice: x: 4, y: 4, z: 8 (z_hi: 4, z_lo: 2; z = z_hi * 2 + z_lo), core: 2. Of those that a mesh axis runs over, the one named last changes fastest.
Arguments:
- base_flow: bfloat16 [3, 512, 384, 256], P(None, 'px', 'py'), may hold values from -3 to 3
- adjoint_start: float32 [3, 512, 384, 256], P(None, 'px', 'py'), may hold values from -2 to 3
- source: bfloat16 [3, 512, 384, 256], P(None, 'px', 'py'), may hold values from -6 to 6
- solid_mask: int32 [512, 384, 256], P('px', 'py'), may hold values 0 or 1
- outlet_ids: int32 [512, 384], P('px', 'py'), may hold values from 0 to 8
- resist: float32 [8, 8], replicated, may hold values from 5 to 20
- tile_owner: int32 [65536, 1], P(('px', 'py')), may hold values from 0 to 255; in each aligned block of 256 rows (0 to 255, 256 to 511, ...) at most 2 rows name the same one
- tile_slot: int32 [65536], P(('px', 'py')), may hold values from 0 to 31
- tile_column: int32 [65536], P(('px', 'py')), may hold values from 0 to 1535
- control_basis: float32 [8192, 128], P(('px', 'py')), may hold values from -0.0390625 to 0.0390625
Outputs:
- adjoint: float32 [3, 512, 384, 256], P(None, 'px', 'py')
- control_grad: float32 [8192], P(('px', 'py'))
Inputs may be any that keep to these rules, and one draw needn't show every extreme that they name: `tile_owner`: among the tiles of one device, at most 2 share an owner.
All inputs are finite; a program needn't handle non-finite values. No bound on the sum of `solid_mask` on one device may be relied on, other than what follows from the above.
Results may differ from a plain program's by a relative error of at most 0.00035.
Values may be sent and summed in bfloat16 or wider, within the bound.
A program may use at most 64 MiB of HBM per device.

v0:
```python
import math

import jax
import jax.numpy as jnp
from jax import lax
from jax.sharding import PartitionSpec as P

NX = 512
NY = 384
NZ = 256
SEG = 128
OUTLETS = 8
TILES_DEV = 256


DT = 0.1
NU = 0.5
ALPHA = 5.0


def padded_2(cells, sides, width):
    for axis, dim in sides:
        count = lax.axis_size(axis)
        ends = count - 1
        head = lax.slice_in_dim(cells, 0, width, axis=dim)
        tail = lax.slice_in_dim(cells, cells.shape[dim] - width, cells.shape[dim], axis=dim)
        cells = jnp.concatenate(
            [
                lax.ppermute(tail, axis, [(i, (i + 1) % count) for i in range(ends)]),
                cells,
                lax.ppermute(head, axis, [((i + 1) % count, i) for i in range(ends)]),
            ],
            axis=dim,
        )
    return cells


def shifted(padded, axis_num, offset):
    window = [slice(1, -1), slice(1, -1), slice(1, -1)]
    extent = padded.shape[padded.ndim - 3 + axis_num]
    window[axis_num] = slice(1 + offset, extent - 1 + offset)
    return padded[(slice(None),) * (padded.ndim - 3) + tuple(window)]


def central(padded, axis_num):
    return 0.5 * (shifted(padded, axis_num, 1) - shifted(padded, axis_num, -1))


def laplace(padded):
    total = -6.0 * shifted(padded, 0, 0)
    for axis_num in range(3):
        total = total + shifted(padded, axis_num, 1) + shifted(padded, axis_num, -1)
    return total


def depth_pad(field):
    return jnp.pad(field, [(0, 0)] * (field.ndim - 1) + [(1, 1)])


def cosine_table(count):
    order = jnp.arange(count).astype(jnp.float32)
    modes = order[:, None]
    points = order[None, :]
    weights = jnp.where(modes == 0.0, math.sqrt(1.0 / count), math.sqrt(2.0 / count))
    return weights * jnp.cos(jnp.pi * (points + 0.5) * modes / count)


def eigen_at(modes, count):
    return 2.0 * jnp.cos(jnp.pi * modes.astype(jnp.float32) / count) - 2.0


def divide_modes(
    coeffs, modes_first, modes_second, modes_third, count_first, count_second, count_third
):
    lam = (
        eigen_at(modes_first, count_first)[:, None, None]
        + eigen_at(modes_second, count_second)[None, :, None]
        + eigen_at(modes_third, count_third)[None, None, :]
    )
    anchor = (
        (modes_first[:, None, None] == 0)
        & (modes_second[None, :, None] == 0)
        & (modes_third[None, None, :] == 0)
    )
    return jnp.where(anchor, jnp.float32(0.0), coeffs / jnp.where(anchor, jnp.float32(-1.0), lam))


def solve_pressure(div):
    high = lax.Precision.HIGHEST
    table_rows = cosine_table(NX)
    table_cols = cosine_table(NY)
    table_depth = cosine_table(NZ)
    row_index = lax.axis_index("px")
    col_index = lax.axis_index("py")
    depth_coeffs = jnp.einsum("cz,xyz->ycx", table_depth, div, precision=high)
    middle = jnp.einsum(
        "ax,yzx->yza",
        table_rows,
        lax.all_to_all(depth_coeffs, "px", split_axis=1, concat_axis=2, tiled=True),
        precision=high,
    )
    spectrum = jnp.einsum(
        "by,yza->bza",
        table_cols,
        lax.all_to_all(middle, "py", split_axis=1, concat_axis=0, tiled=True),
        precision=high,
    )
    depth_part = spectrum.shape[1]
    modes_depth = (
        row_index * middle.shape[1]
        + col_index * depth_part
        + jnp.arange(depth_part, dtype=jnp.int32)
    )
    modes_cols = jnp.arange(NY, dtype=jnp.int32)
    modes_rows = jnp.arange(NX, dtype=jnp.int32)
    solved = divide_modes(spectrum, modes_cols, modes_depth, modes_rows, NY, NZ, NX)
    cols_back = jnp.einsum("by,bza->yza", table_cols, solved, precision=high)
    middle_back = lax.all_to_all(cols_back, "py", split_axis=0, concat_axis=1, tiled=True)
    rows_spatial = jnp.einsum("ax,yza->yzx", table_rows, middle_back, precision=high)
    return jnp.einsum(
        "cz,ycx->xyz",
        table_depth,
        lax.all_to_all(rows_spatial, "px", split_axis=2, concat_axis=1, tiled=True),
        precision=high,
    )


def mirror_edges(padded, axis_num, at_start, at_end):
    first = lax.slice_in_dim(padded, 0, 1, axis=axis_num)
    second = lax.slice_in_dim(padded, 1, 2, axis=axis_num)
    extent = padded.shape[axis_num]
    before_last = lax.slice_in_dim(padded, extent - 2, extent - 1, axis=axis_num)
    last = lax.slice_in_dim(padded, extent - 1, extent, axis=axis_num)
    inner = lax.slice_in_dim(padded, 1, extent - 1, axis=axis_num)
    return jnp.concatenate(
        [jnp.where(at_start, second, first), inner, jnp.where(at_end, before_last, last)],
        axis=axis_num,
    )


def local(
    base_flow,
    adjoint_start,
    source,
    solid_mask,
    outlet_ids,
    resist,
    tile_owner,
    tile_slot,
    tile_column,
    control_basis,
):
    rows_here, cols_here, depth = (
        adjoint_start.shape[1],
        adjoint_start.shape[2],
        adjoint_start.shape[3],
    )
    row_index = lax.axis_index("px")
    col_index = lax.axis_index("py")
    rows_count = lax.axis_size("px")
    cols_count = lax.axis_size("py")
    flow = base_flow.astype(jnp.float32)
    forcing = source.astype(jnp.float32)
    flow_halo = padded_2(base_flow, (("px", 1), ("py", 2)), 1)
    flow_pad = depth_pad(flow_halo.astype(jnp.float32))
    flow_grads = jnp.stack(
        [
            jnp.stack([central(flow_pad[source_axis], target) for source_axis in range(3)])
            for target in range(3)
        ]
    )
    damping = 1.0 + DT * ALPHA * solid_mask.astype(jnp.float32)
    outlet_onehot = (
        outlet_ids[None] == jnp.arange(OUTLETS, dtype=jnp.int32)[:, None, None]
    ).astype(jnp.float32)
    velocity = adjoint_start
    padded = depth_pad(padded_2(velocity, (("px", 1), ("py", 2)), 1))
    convect = (
        flow[0][None] * central(padded, 0)
        + flow[1][None] * central(padded, 1)
        + flow[2][None] * central(padded, 2)
    )
    transpose_term = jnp.sum(velocity[None] * flow_grads, axis=1)
    predicted = (
        velocity + DT * (convect - transpose_term + NU * laplace(padded) + forcing)
    ) / damping[None]
    partial_flux = jnp.sum(outlet_onehot * predicted[2, :, :, -1][None], axis=(1, 2))
    flux = lax.psum(partial_flux, ("px", "py")) / (NX * NY)
    press = jnp.dot(resist, flux, precision=lax.Precision.HIGHEST)
    predicted = predicted.at[2, :, :, -1].add(
        -DT * jnp.sum(outlet_onehot * press[:, None, None], axis=0)
    )
    wall_pad = depth_pad(padded_2(predicted, (("px", 1), ("py", 2)), 1))
    div = central(wall_pad[0], 0) + central(wall_pad[1], 1) + central(wall_pad[2], 2)
    pressure = solve_pressure(div)
    pressure_halo = padded_2(pressure, (("px", 0), ("py", 1)), 1)
    pressure_halo = mirror_edges(pressure_halo, 0, row_index == 0, row_index == rows_count - 1)
    pressure_halo = mirror_edges(pressure_halo, 1, col_index == 0, col_index == cols_count - 1)
    pressure_pad = jnp.pad(pressure_halo, ((0, 0), (0, 0), (1, 1)), mode="edge")
    velocity = predicted - jnp.stack([central(pressure_pad, target) for target in range(3)])
    sigma = -ALPHA * jnp.sum(flow * velocity, axis=0)
    segment_rows = sigma.reshape(rows_here * cols_here * (depth // SEG), SEG)
    picked = segment_rows[tile_column]
    devices = rows_count * cols_count
    capacity = max(2, 2 * TILES_DEV // devices)
    owners = tile_owner[:, 0]
    owner_onehot = (owners[:, None] == jnp.arange(devices, dtype=jnp.int32)[None, :]).astype(
        jnp.int32
    )
    ranking = jnp.sum(jnp.cumsum(owner_onehot, axis=0) * owner_onehot, axis=1) - 1
    target_slot = owners * capacity + ranking
    packed = jnp.zeros((devices * capacity, SEG), jnp.float32).at[target_slot].set(picked)
    labels = jnp.full((devices * capacity,), -1, jnp.int32).at[target_slot].set(tile_slot)
    packed = packed.reshape(rows_count, cols_count, capacity, SEG)
    labels = labels.reshape(rows_count, cols_count, capacity)
    got_rows, got_labels = (
        lax.all_to_all(
            lax.all_to_all(packed, "px", split_axis=0, concat_axis=0, tiled=True),
            "py",
            split_axis=1,
            concat_axis=1,
            tiled=True,
        ),
        lax.all_to_all(
            lax.all_to_all(labels, "px", split_axis=0, concat_axis=0, tiled=True),
            "py",
            split_axis=1,
            concat_axis=1,
            tiled=True,
        ),
    )
    got_rows = got_rows.reshape(devices * capacity, SEG)
    got_labels = got_labels.reshape(devices * capacity)
    scores = jnp.dot(
        got_rows,
        control_basis.T,
        precision=lax.Precision.HIGHEST,
        preferred_element_type=jnp.float32,
    )
    chosen = got_labels[:, None] == jnp.arange(control_basis.shape[0], dtype=jnp.int32)[None, :]
    grad = jnp.sum(jnp.where(chosen, scores, jnp.float32(0.0)), axis=0)
    return (velocity, grad)


def solution(mesh):
    in_specs = (
        P(None, "px", "py", None),
        P(None, "px", "py", None),
        P(None, "px", "py", None),
        P("px", "py", None),
        P("px", "py"),
        P(),
        P(("px", "py"), None),
        P(("px", "py")),
        P(("px", "py")),
        P(("px", "py"), None),
    )
    out_specs = (P(None, "px", "py", None), P(("px", "py")))
    return jax.shard_map(local, mesh=mesh, in_specs=in_specs, out_specs=out_specs, check_vma=False)
```

profile of v0, /device:TPU:1, one launch (start us, length us, event | category | flops | bytes accessed | tf_op | source)
XLA Modules:
  0.0 412.7 jit_solution(1627980985705549458)
XLA Ops:
  2.6 4.6 %collective-permute-start.4 = (bf16[3,1,24,256]{3,1,2,0:T(2,128)(2,1)S(1)}, bf16[3,1,24,256]{3,1,2,0:T(2,128)(2,1)S(1)}, u32[]{:S(2)}, u32[]{:S(2)}) collective-permute-start(bf16[3,1,24,256]{3,1,2,0:T(2,128)(2,1)S(1)} %get-tuple-element.58), channel_id=1, source_target_pairs={{0,16},{16,32},{32,48},{48,64},{64,80},{80,96},{96,112},{112,128},... | collective-permute-start | bytes 110600 | tf_op jit(solution)/shard_map/ppermute | solution.py:29
  17.2 4.9 %collective-permute-start.6 = (bf16[3,34,1,256]{3,1,2,0:T(8,128)(2,1)S(1)}, bf16[3,34,1,256]{3,1,2,0:T(8,128)(2,1)S(1)}, u32[]{:S(2)}, u32[]{:S(2)}) collective-permute-start(bf16[3,34,1,256]{3,1,2,0:T(8,128)(2,1)S(1)} %get-tuple-element.54), channel_id=1, source_target_pairs={{0,1},{1,2},{2,3},{3,4},{4,5},{5,6},{6,7},{7,8},{8,9},{9,10},{10,1... | collective-permute-start | bytes 156680 | tf_op jit(solution)/shard_map/ppermute | solution.py:29
  25.5 7.6 %collective-permute-start.3 = (f32[3,34,1,256]{3,1,2,0:T(8,128)}, f32[3,34,1,256]{3,1,2,0:T(8,128)S(1)}, u32[]{:S(2)}, u32[]{:S(2)}) collective-permute-start(f32[3,34,1,256]{3,1,2,0:T(8,128)} %get-tuple-element.36), channel_id=1, source_target_pairs={{0,1},{1,2},{2,3},{3,4},{4,5},{5,6},{6,7},{7,8},{8,9},{9,10},{10,1... | collective-permute-start | bytes 313352 | tf_op jit(solution)/shard_map/ppermute | solution.py:29
  48.5 4.5 %add_divide_fusion = f32[3,32,24,256]{3,1,2,0:T(8,128)S(1)} fusion(f32[3,32,24,256]{3,1,2,0:T(8,128)S(1)} %copy.178, f32[3,32,24,256]{3,1,2,0:T(8,128)S(1)} %fusion, f32[3,34,26,258]{3,1,2,0:T(8,128)S(1)} %select_maximum_fusion.4, f32[3,34,1,256]{3,1,2,0:T(8,128)S(1)} %collective-permute-done.2, f32[3,1,24,256]{3,1,2,0:T(1,128)S(1)} %collective-permute-done, ...), kind=kLoop, calls=%fused_computation.34 | loop fusion | flops 18284544 | bytes 16478208 | tf_op jit(solution)/shard_map/div | solution.py:184
  53.5 79.2 %psum.7 = f32[8]{0:T(128)S(1)} all-reduce(f32[8]{0:T(128)S(1)} %select_reduce_fusion.1), channel_id=1, replica_groups=mesh['px'=16,'py'=16] {'px','py'}, use_global_device_ids=true, to_apply=%region_2.3 | all-reduce | flops 8 | bytes 64 | tf_op jit(solution)/shard_map/psum | solution.py:188
  133.3 4.5 %scatter-add.4 = f32[3,32,24,256]{3,1,2,0:T(8,128)S(1)} dynamic-update-slice(f32[3,32,24,256]{3,1,2,0:T(8,128)S(1)} %add_divide_fusion, f32[1,32,24,1]{3,1,2,0:T(8,128)S(1)} %slice_add_fusion, s32[]{:T(128)} %constant.118.clone.1, s32[]{:T(128)} %constant.119.clone.1, s32[]{:T(128)} %constant.119.clone.1, s32[]{:T(128)} %constant.120.clone.1) | dynamic-update-slice | bytes 6148 | tf_op jit(solution)/shard_map/scatter-add | solution.py:190
  150.5 4.9 %collective-permute-done.11 = f32[3,34,1,256]{3,1,2,0:T(8,128)S(1)} collective-permute-done((f32[3,34,1,256]{3,1,2,0:T(8,128)S(1)}, f32[3,34,1,256]{3,1,2,0:T(8,128)S(1)}, u32[]{:S(2)}, u32[]{:S(2)}) %collective-permute-start.11) | collective-permute-done | bytes 104480 | tf_op jit(solution)/shard_map/ppermute | solution.py:31
  169.1 9.6 %all-to-all-start = ((f32[16,1,12288]{2,1,0:T(1,128)}), f32[16,1,12288]{2,1,0:T(1,128)S(1)}, u32[]{:S(2)}, u32[]{:S(2)}) async-start(f32[16,1,12288]{2,1,0:T(1,128)} %reshape.267), calls=%async_computation | async-start | bytes 1572864 | tf_op jit(solution)/shard_map/all_to_all | solution.py:99
  178.7 12.9 %all-to-all-done = f32[16,1,12288]{2,1,0:T(1,128)S(1)} async-done(((f32[16,1,12288]{2,1,0:T(1,128)}), f32[16,1,12288]{2,1,0:T(1,128)S(1)}, u32[]{:S(2)}, u32[]{:S(2)}) %all-to-all-start) | async-done | bytes 786464 | tf_op jit(solution)/shard_map/all_to_all | solution.py:99
  199.5 5.4 %copy.204 = f32[24,16,16,32]{3,2,0,1:T(8,128)} copy(f32[24,16,16,32]{3,0,1,2:T(8,128)} %bitcast.124) | data formatting | bytes 1572864 | tf_op jit(solution)/shard_map/all_to_all | solution.py:99
  207.5 6.3 %fusion.7 = f32[24,16,512]{2,0,1:T(8,128)} fusion(f32[24,16,512]{2,0,1:T(8,128)S(1)} %reshape.257, f32[512]{0:T(512)S(1)} %iota_convert_fusion, f32[512]{0:T(512)S(1)} %get-tuple-element.75, f32[512]{0:T(512)S(1)} %get-tuple-element.76), kind=kOutput, calls=%fused_computation.54 | convolution fusion | flops 1208745984 | bytes 1579008 | tf_op jit(solution)/shard_map/ax,yzx->yza/dot_general | solution.py:96
  213.8 7.6 %all-to-all-start.1 = ((f32[24,16,512]{2,0,1:T(8,128)}), f32[24,16,512]{2,0,1:T(8,128)S(1)}, u32[]{:S(2)}, u32[]{:S(2)}) async-start(f32[24,16,512]{2,0,1:T(8,128)} %fusion.7), calls=%async_computation.1 | async-start | bytes 1572864 | tf_op jit(solution)/shard_map/all_to_all | solution.py:105
  221.6 21.8 %all-to-all-done.1 = f32[24,16,512]{2,0,1:T(8,128)S(1)} async-done(((f32[24,16,512]{2,0,1:T(8,128)}), f32[24,16,512]{2,0,1:T(8,128)S(1)}, u32[]{:S(2)}, u32[]{:S(2)}) %all-to-all-start.1) | async-done | bytes 786464 | tf_op jit(solution)/shard_map/all_to_all | solution.py:105
  251.2 29.0 %all_to_all.89 = f32[384,1,512]{2,1,0:T(1,128)S(1)} all-to-all(f32[384,1,512]{2,1,0:T(1,128)S(1)} %copy.186), channel_id=1, replica_groups=mesh['px'=16,'py'=16] {'py'}, dimensions={0} | all-to-all | bytes 1572864 | tf_op jit(solution)/shard_map/all_to_all | solution.py:118
  280.3 5.4 %fusion.5 = f32[24,16,512]{2,1,0:T(8,128)S(1)} fusion(f32[16,24,1,512]{3,1,0,2:T(8,128)S(1)} %bitcast.130, f32[512]{0:T(512)S(1)} %iota_convert_fusion, f32[512]{0:T(512)S(1)} %get-tuple-element.75, f32[512]{0:T(512)S(1)} %get-tuple-element.76), kind=kOutput, calls=%fused_computation.52 | convolution fusion | flops 1208745984 | bytes 1579008 | tf_op jit(solution)/shard_map/ax,yza->yzx/dot_general | solution.py:119
  289.4 5.4 %reshape.269 = f32[16,1,12288]{2,1,0:T(1,128)} reshape(f32[512,16,24]{2,1,0:T(8,128)} %bitcast.122) | data formatting | bytes 1572864
  302.2 9.9 %all-to-all-done.3 = f32[16,1,12288]{2,1,0:T(1,128)S(1)} async-done(((f32[16,1,12288]{2,1,0:T(1,128)}), f32[16,1,12288]{2,1,0:T(1,128)S(1)}, u32[]{:S(2)}, u32[]{:S(2)}) %all-to-all-start.3) | async-done | bytes 786464 | tf_op jit(solution)/shard_map/all_to_all | solution.py:123
  325.5 6.1 %copy.189 = f32[24,16,16,32]{3,1,2,0:T(8,128)} copy(f32[24,16,16,32]{0,1,3,2:T(8,128)} %bitcast.121) | data formatting | bytes 1572864 | tf_op jit(solution)/shard_map/all_to_all | solution.py:123
  331.6 7.8 %convolution_bitcast_fusion = f32[32,24,256]{2,0,1:T(8,128)S(1)} fusion(f32[24,256,32]{2,1,0:T(8,128)} %bitcast.123, f32[256]{0:T(256)S(1)} %iota_convert_fusion.2, f32[256]{0:T(256)S(1)} %get-tuple-element.74, f32[256]{0:T(256)S(1)} %get-tuple-element.73), kind=kOutput, calls=%fused_computation.41 | convolution fusion | flops 604176384 | bytes 1575936 | tf_op jit(solution)/shard_map/cz,ycx->xyz/dot_general | solution.py:120
  367.0 6.7 %all-to-all-start.6 = ((f32[16,16,2,128]{3,2,1,0:T(2,128)}), f32[16,16,2,128]{3,2,1,0:T(2,128)S(1)}, u32[]{:S(2)}, u32[]{:S(2)}) async-start(f32[16,16,2,128]{3,2,1,0:T(2,128)} %bitcast.50), calls=%async_computation.6 | async-start | bytes 524288 | tf_op jit(solution)/shard_map/all_to_all | solution.py:218
  374.4 6.5 %all-to-all-done.6 = f32[16,16,2,128]{3,2,1,0:T(2,128)S(1)} async-done(((f32[16,16,2,128]{3,2,1,0:T(2,128)}), f32[16,16,2,128]{3,2,1,0:T(2,128)S(1)}, u32[]{:S(2)}, u32[]{:S(2)}) %all-to-all-start.6) | async-done | bytes 262176 | tf_op jit(solution)/shard_map/all_to_all | solution.py:218
  380.9 6.4 %all-to-all-start.5 = ((s32[16,16,2]{0,2,1:T(2,128)}), s32[16,16,2]{0,2,1:T(2,128)S(1)}, u32[]{:S(2)}, u32[]{:S(2)}) async-start(s32[16,16,2]{0,2,1:T(2,128)} %copy.194), calls=%async_computation.5 | async-start | bytes 32768 | tf_op jit(solution)/shard_map/all_to_all | solution.py:224
  388.1 7.9 %all-to-all-done.5 = s32[16,16,2]{0,2,1:T(2,128)S(1)} async-done(((s32[16,16,2]{0,2,1:T(2,128)}), s32[16,16,2]{0,2,1:T(2,128)S(1)}, u32[]{:S(2)}, u32[]{:S(2)}) %all-to-all-start.5) | async-done | bytes 2080 | tf_op jit(solution)/shard_map/all_to_all | solution.py:224
  402.6 8.5 %all-to-all-done.7 = f32[16,16,2,128]{3,2,0,1:T(2,128)S(1)} async-done(((f32[16,16,2,128]{3,2,0,1:T(2,128)}), f32[16,16,2,128]{3,2,0,1:T(2,128)S(1)}, u32[]{:S(2)}, u32[]{:S(2)}) %all-to-all-start.7) | async-done | bytes 262176 | tf_op jit(solution)/shard_map/all_to_all | solution.py:217
  (152 shorter events, 137.5 us)
Async XLA Ops:
  0.6 410.6 %copy-start = (f32[32,128]{1,0:T(8,128)S(1)}, f32[32,128]{1,0:T(8,128)}, u32[]{:S(2)}) copy-start(f32[32,128]{1,0:T(8,128)} %param.21) | copy-start | bytes 49156
  2.6 14.5 %collective-permute-start.4 = (bf16[3,1,24,256]{3,1,2,0:T(2,128)(2,1)S(1)}, bf16[3,1,24,256]{3,1,2,0:T(2,128)(2,1)S(1)}, u32[]{:S(2)}, u32[]{:S(2)}) collective-permute-start(bf16[3,1,24,256]{3,1,2,0:T(2,128)(2,1)S(1)} %get-tuple-element.58), channel_id=1, source_target_pairs={{0,16},{16,32},{32,48},{48,64},{64,80},{80,96},{96,112},{112,128},... | collective-permute-start | bytes 110600 | tf_op jit(solution)/shard_map/ppermute | solution.py:29
  7.3 9.9 %collective-permute-start.5 = (bf16[3,1,24,256]{3,1,2,0:T(2,128)(2,1)S(1)}, bf16[3,1,24,256]{3,1,2,0:T(2,128)(2,1)S(1)}, u32[]{:S(2)}, u32[]{:S(2)}) collective-permute-start(bf16[3,1,24,256]{3,1,2,0:T(2,128)(2,1)S(1)} %get-tuple-element.59), channel_id=1, source_target_pairs={{16,0},{32,16},{48,32},{64,48},{80,64},{96,80},{112,96},{128,112},... | collective-permute-start | bytes 110600 | tf_op jit(solution)/shard_map/ppermute | solution.py:31
  9.3 14.2 %collective-permute-start = (f32[3,1,24,256]{3,1,2,0:T(1,128)S(1)}, f32[3,1,24,256]{3,1,2,0:T(1,128)S(1)}, u32[]{:S(2)}, u32[]{:S(2)}) collective-permute-start(f32[3,1,24,256]{3,1,2,0:T(1,128)S(1)} %copy.166), channel_id=1, source_target_pairs={{16,0},{32,16},{48,32},{64,48},{80,64},{96,80},{112,96},{128,112},... | collective-permute-start | bytes 221192 | tf_op jit(solution)/shard_map/ppermute | solution.py:31
  11.3 12.2 %collective-permute-start.1 = (f32[3,1,24,256]{3,1,2,0:T(1,128)S(1)}, f32[3,1,24,256]{3,1,2,0:T(1,128)S(1)}, u32[]{:S(2)}, u32[]{:S(2)}) collective-permute-start(f32[3,1,24,256]{3,1,2,0:T(1,128)S(1)} %copy.168), channel_id=1, source_target_pairs={{0,16},{16,32},{32,48},{48,64},{64,80},{80,96},{96,112},{112,128},... | collective-permute-start | bytes 221192 | tf_op jit(solution)/shard_map/ppermute | solution.py:29
  17.2 15.8 %collective-permute-start.6 = (bf16[3,34,1,256]{3,1,2,0:T(8,128)(2,1)S(1)}, bf16[3,34,1,256]{3,1,2,0:T(8,128)(2,1)S(1)}, u32[]{:S(2)}, u32[]{:S(2)}) collective-permute-start(bf16[3,34,1,256]{3,1,2,0:T(8,128)(2,1)S(1)} %get-tuple-element.54), channel_id=1, source_target_pairs={{0,1},{1,2},{2,3},{3,4},{4,5},{5,6},{6,7},{7,8},{8,9},{9,10},{10,1... | collective-permute-start | bytes 156680 | tf_op jit(solution)/shard_map/ppermute | solution.py:29
  22.2 10.9 %collective-permute-start.7 = (bf16[3,34,1,256]{3,1,2,0:T(8,128)(2,1)S(1)}, bf16[3,34,1,256]{3,1,2,0:T(8,128)(2,1)S(1)}, u32[]{:S(2)}, u32[]{:S(2)}) collective-permute-start(bf16[3,34,1,256]{3,1,2,0:T(8,128)(2,1)S(1)} %get-tuple-element.55), channel_id=1, source_target_pairs={{1,0},{2,1},{3,2},{4,3},{5,4},{6,5},{7,6},{8,7},{9,8},{10,9},{11,1... | collective-permute-start | bytes 156680 | tf_op jit(solution)/shard_map/ppermute | solution.py:31
  24.2 20.1 %collective-permute-start.2 = (f32[3,34,1,256]{3,1,2,0:T(8,128)}, f32[3,34,1,256]{3,1,2,0:T(8,128)S(1)}, u32[]{:S(2)}, u32[]{:S(2)}) collective-permute-start(f32[3,34,1,256]{3,1,2,0:T(8,128)} %get-tuple-element.37), channel_id=1, source_target_pairs={{1,0},{2,1},{3,2},{4,3},{5,4},{6,5},{7,6},{8,7},{9,8},{10,9},{11,1... | collective-permute-start | bytes 313352 | tf_op jit(solution)/shard_map/ppermute | solution.py:31
  25.5 18.8 %collective-permute-start.3 = (f32[3,34,1,256]{3,1,2,0:T(8,128)}, f32[3,34,1,256]{3,1,2,0:T(8,128)S(1)}, u32[]{:S(2)}, u32[]{:S(2)}) collective-permute-start(f32[3,34,1,256]{3,1,2,0:T(8,128)} %get-tuple-element.36), channel_id=1, source_target_pairs={{0,1},{1,2},{2,3},{3,4},{4,5},{5,6},{6,7},{7,8},{8,9},{9,10},{10,1... | collective-permute-start | bytes 313352 | tf_op jit(solution)/shard_map/ppermute | solution.py:29
  137.9 4.9 %collective-permute-start.8 = (f32[3,1,24,256]{3,1,2,0:T(1,128)S(1)}, f32[3,1,24,256]{3,1,2,0:T(1,128)S(1)}, u32[]{:S(2)}, u32[]{:S(2)}) collective-permute-start(f32[3,1,24,256]{3,1,2,0:T(1,128)S(1)} %get-tuple-element.38), channel_id=1, source_target_pairs={{0,16},{16,32},{32,48},{48,64},{64,80},{80,96},{96,112},{112,128},... | collective-permute-start | bytes 221192 | tf_op jit(solution)/shard_map/ppermute | solution.py:29
  140.8 5.7 %collective-permute-start.9 = (f32[3,1,24,256]{3,1,2,0:T(1,128)S(1)}, f32[3,1,24,256]{3,1,2,0:T(1,128)S(1)}, u32[]{:S(2)}, u32[]{:S(2)}) collective-permute-start(f32[3,1,24,256]{3,1,2,0:T(1,128)S(1)} %get-tuple-element.39), channel_id=1, source_target_pairs={{16,0},{32,16},{48,32},{64,48},{80,64},{96,80},{112,96},{128,112},... | collective-permute-start | bytes 221192 | tf_op jit(solution)/shard_map/ppermute | solution.py:31
  146.5 4.0 collective-permute-start.10
  148.7 6.8 %collective-permute-start.11 = (f32[3,34,1,256]{3,1,2,0:T(8,128)S(1)}, f32[3,34,1,256]{3,1,2,0:T(8,128)S(1)}, u32[]{:S(2)}, u32[]{:S(2)}) collective-permute-start(f32[3,34,1,256]{3,1,2,0:T(8,128)S(1)} %get-tuple-element.35), channel_id=1, source_target_pairs={{1,0},{2,1},{3,2},{4,3},{5,4},{6,5},{7,6},{8,7},{9,8},{10,9},{11,1... | collective-permute-start | bytes 313352 | tf_op jit(solution)/shard_map/ppermute | solution.py:31
  169.1 22.5 %all-to-all-start = ((f32[16,1,12288]{2,1,0:T(1,128)}), f32[16,1,12288]{2,1,0:T(1,128)S(1)}, u32[]{:S(2)}, u32[]{:S(2)}) async-start(f32[16,1,12288]{2,1,0:T(1,128)} %reshape.267), calls=%async_computation | async-start | bytes 1572864 | tf_op jit(solution)/shard_map/all_to_all | solution.py:99
  213.8 29.6 %all-to-all-start.1 = ((f32[24,16,512]{2,0,1:T(8,128)}), f32[24,16,512]{2,0,1:T(8,128)S(1)}, u32[]{:S(2)}, u32[]{:S(2)}) async-start(f32[24,16,512]{2,0,1:T(8,128)} %fusion.7), calls=%async_computation.1 | async-start | bytes 1572864 | tf_op jit(solution)/shard_map/all_to_all | solution.py:105
  294.8 17.3 %all-to-all-start.3 = ((f32[16,1,12288]{2,1,0:T(1,128)}), f32[16,1,12288]{2,1,0:T(1,128)S(1)}, u32[]{:S(2)}, u32[]{:S(2)}) async-start(f32[16,1,12288]{2,1,0:T(1,128)} %reshape.269), calls=%async_computation.3 | async-start | bytes 1572864 | tf_op jit(solution)/shard_map/all_to_all | solution.py:123
  313.0 54.0 %all-to-all-start.4 = ((s32[16,16,2]{1,2,0:T(2,128)}), s32[16,16,2]{1,2,0:T(2,128)S(1)}, u32[]{:S(2)}, u32[]{:S(2)}) async-start(s32[16,16,2]{1,2,0:T(2,128)} %copy.193), calls=%async_computation.4 | async-start | bytes 32768 | tf_op jit(solution)/shard_map/all_to_all | solution.py:225
  339.4 5.5 %collective-permute-start.12 = (f32[1,24,256]{2,0,1:T(1,128)S(1)}, f32[1,24,256]{2,0,1:T(1,128)S(1)}, u32[]{:S(2)}, u32[]{:S(2)}) collective-permute-start(f32[1,24,256]{2,0,1:T(1,128)S(1)} %get-tuple-element.68), channel_id=1, source_target_pairs={{0,16},{16,32},{32,48},{48,64},{64,80},{80,96},{96,112},{112,128},... | collective-permute-start | bytes 73736 | tf_op jit(solution)/shard_map/ppermute | solution.py:29
  343.0 5.1 %collective-permute-start.13 = (f32[1,24,256]{2,0,1:T(1,128)S(1)}, f32[1,24,256]{2,0,1:T(1,128)S(1)}, u32[]{:S(2)}, u32[]{:S(2)}) collective-permute-start(f32[1,24,256]{2,0,1:T(1,128)S(1)} %get-tuple-element.69), channel_id=1, source_target_pairs={{16,0},{32,16},{48,32},{64,48},{80,64},{96,80},{112,96},{128,112},... | collective-permute-start | bytes 73736 | tf_op jit(solution)/shard_map/ppermute | solution.py:31
  348.1 5.0 %collective-permute-start.14 = (f32[34,1,256]{2,0,1:T(8,128)S(1)}, f32[34,1,256]{2,0,1:T(8,128)S(1)}, u32[]{:S(2)}, u32[]{:S(2)}) collective-permute-start(f32[34,1,256]{2,0,1:T(8,128)S(1)} %get-tuple-element.66), channel_id=1, source_target_pairs={{0,1},{1,2},{2,3},{3,4},{4,5},{5,6},{6,7},{7,8},{8,9},{9,10},{10,1... | collective-permute-start | bytes 104456 | tf_op jit(solution)/shard_map/ppermute | solution.py:29
  351.5 5.6 %collective-permute-start.15 = (f32[34,1,256]{2,0,1:T(8,128)S(1)}, f32[34,1,256]{2,0,1:T(8,128)S(1)}, u32[]{:S(2)}, u32[]{:S(2)}) collective-permute-start(f32[34,1,256]{2,0,1:T(8,128)S(1)} %get-tuple-element.67), channel_id=1, source_target_pairs={{1,0},{2,1},{3,2},{4,3},{5,4},{6,5},{7,6},{8,7},{9,8},{10,9},{11,1... | collective-permute-start | bytes 104456 | tf_op jit(solution)/shard_map/ppermute | solution.py:31
  367.0 13.9 %all-to-all-start.6 = ((f32[16,16,2,128]{3,2,1,0:T(2,128)}), f32[16,16,2,128]{3,2,1,0:T(2,128)S(1)}, u32[]{:S(2)}, u32[]{:S(2)}) async-start(f32[16,16,2,128]{3,2,1,0:T(2,128)} %bitcast.50), calls=%async_computation.6 | async-start | bytes 524288 | tf_op jit(solution)/shard_map/all_to_all | solution.py:218
  380.9 15.1 %all-to-all-start.5 = ((s32[16,16,2]{0,2,1:T(2,128)}), s32[16,16,2]{0,2,1:T(2,128)S(1)}, u32[]{:S(2)}, u32[]{:S(2)}) async-start(s32[16,16,2]{0,2,1:T(2,128)} %copy.194), calls=%async_computation.5 | async-start | bytes 32768 | tf_op jit(solution)/shard_map/all_to_all | solution.py:224
  396.0 15.1 %all-to-all-start.7 = ((f32[16,16,2,128]{3,2,0,1:T(2,128)}), f32[16,16,2,128]{3,2,0,1:T(2,128)S(1)}, u32[]{:S(2)}, u32[]{:S(2)}) async-start(f32[16,16,2,128]{3,2,0,1:T(2,128)} %copy.197), calls=%async_computation.7 | async-start | bytes 524288 | tf_op jit(solution)/shard_map/all_to_all | solution.py:217
  (11 other events, 167.6 us)
where the time goes:
time: 417 us; the launch traced here: 413 us
  blocking collectives  108 us (26%)
  starting transfers between devices  88.6 us (21%)
  waiting for transfers between devices  83.5 us (20%)
  local copies, waits for them, and re-layouts  60.7 us (15%)
  other arithmetic  40 us (10%)
  matrix products  29.7 us (7%)
    psum x1, blocking collectives, local(): flux = lax.psum(partial_flux, ('px', 'py')) / (NX * NY)  79.2 us
    ppermute x8, starting transfers between devices, padded_2(): lax.ppermute(tail, axis, [(i, (i + 1) % count) for i in range(ends)])  32.6 us
    all_to_all x1, blocking collectives, solve_pressure(): lax.all_to_all(cols_back, 'py', split_axis=0, concat_axis=1, tiled=True)  29 us
    unnamed x32, local copies, waits for them, and re-layouts  23.3 us
    all_to_all x1, waiting for transfers between devices, solve_pressure(): lax.all_to_all(middle, 'py', split_axis=1, concat_axis=0, tiled=True)  21.8 us
    ppermute x8, waiting for transfers between devices, padded_2(): lax.ppermute(head, axis, [((i + 1) % count, i) for i in range(ends)])  15.9 us
    ppermute x8, starting transfers between devices, padded_2(): lax.ppermute(head, axis, [((i + 1) % count, i) for i in range(ends)])  13.4 us
    all_to_all x1, waiting for transfers between devices, solve_pressure(): lax.all_to_all(depth_coeffs, 'px', split_axis=1, concat_axis=2, tiled=True)  12.9 us
  transfers between devices with their start and end apart: 23, of which 11 were waited for; matrix products, arithmetic and copies ran while one was open for 13% of the time, Pallas kernels for 0%

commit v1 on v0

v1 whole, which is shorter than its diff:
```python
import functools
import math

import jax
import jax.numpy as jnp
import numpy as np
from jax import lax
from jax.experimental import pallas as pl
from jax.experimental.pallas import tpu as pltpu
from jax.sharding import PartitionSpec as P

SEG = 128
OUTLETS = 8
DT = 0.1
NU = 0.5
ALPHA = 5.0
HALF = 128
MESH = pl.DeviceIdType.MESH
F32 = jnp.float32
BF16 = jnp.bfloat16


def table_np(count):
    order = np.arange(count).astype(np.float32)
    modes = order[:, None]
    points = order[None, :]
    weights = np.where(modes == 0.0, math.sqrt(1.0 / count), math.sqrt(2.0 / count)).astype(np.float32)
    angle = np.float32(np.pi) * (points + np.float32(0.5)) * modes / np.float32(count)
    return (weights * np.cos(angle.astype(np.float32))).astype(np.float32)


def eigen_np(count):
    order = np.arange(count).astype(np.float32)
    angle = (np.float32(np.pi) * order / np.float32(count)).astype(np.float32)
    return (np.float32(2.0) * np.cos(angle) - np.float32(2.0)).astype(np.float32)


def split_np(table, count):
    parts = []
    for _ in range(count):
        parts.append(table.astype(jnp.bfloat16))
        table = table - parts[-1].astype(np.float32)
    return tuple(parts)


def split(value, count):
    parts = []
    for _ in range(count):
        parts.append(value.astype(BF16))
        value = value - parts[-1].astype(F32)
    return tuple(parts)


def dot_parts(a_parts, b_parts, contract):
    dims = ((contract[0], contract[1]), ((), ()))
    dot = functools.partial(lax.dot_general, dimension_numbers=dims, preferred_element_type=F32)
    total = None
    for order in range(len(a_parts) - 1, -1, -1):
        for i in range(order + 1):
            term = dot(a_parts[i], b_parts[order - i])
            total = term if total is None else total + term
    return total


def swap_groups(tiles):
    lane = lax.broadcasted_iota(jnp.int32, tiles[0].shape, 1)
    odd = (lane // 32) % 2 == 1
    far = lane >= 64
    t0, t1, t2, t3 = tiles
    a0 = jnp.where(odd, pltpu.roll(t1, 32, 1), t0)
    a1 = jnp.where(odd, t1, pltpu.roll(t0, 96, 1))
    a2 = jnp.where(odd, pltpu.roll(t3, 32, 1), t2)
    a3 = jnp.where(odd, t3, pltpu.roll(t2, 96, 1))
    return (
        jnp.where(far, pltpu.roll(a2, 64, 1), a0),
        jnp.where(far, pltpu.roll(a3, 64, 1), a1),
        jnp.where(far, a2, pltpu.roll(a0, 64, 1)),
        jnp.where(far, a3, pltpu.roll(a1, 64, 1)),
    )


def z_shift(field, edge_low, edge_high):
    depth = field.shape[1]
    lane = lax.broadcasted_iota(jnp.int32, field.shape, 1)
    below = jnp.where(lane == 0, edge_low, pltpu.roll(field, 1, 1))
    above = jnp.where(lane == depth - 1, edge_high, pltpu.roll(field, depth - 1, 1))
    return below, above


def main_kernel(
    dims,
    v_hbm, u_hbm, s_hbm, m_hbm, ids, resb, tz_hbm, tx_hbm, tt_hbm, mu, muo,
    w_out, q_out,
    vp, up, ub, sb, mk, w0, w1, w2, snd_y, rcv_y, wy_snd, wy_rcv, fsum, fr1, fr2,
    div, msg, got, got2, cols, tau, kap, owner_inv, owner_phi,
    isnd, ircv, jsnd, jrcv, back, qp, qy_snd, qy_rcv, tz, tx, tt,
    load_sem, x_send, x_recv, y_send, y_recv, f_send, f_recv, a_send, a_recv, i_send, i_recv, out_sem,
):
    npx, npy, nxl, nyl, nz = dims
    nx = npx * nxl
    kzl = nz // npx
    kown = kzl // npy
    halves = nz // HALF
    me_x = lax.axis_index("px")
    me_y = lax.axis_index("py")
    right_x, left_x = lax.rem(me_x + 1, npx), lax.rem(me_x + npx - 1, npx)
    right_y, left_y = lax.rem(me_y + 1, npy), lax.rem(me_y + npy - 1, npy)
    first_x, last_x = me_x == 0, me_x == npx - 1
    first_y, last_y = me_y == 0, me_y == npy - 1
    top = 8 + nyl

    loads = []
    for c in range(3):
        for h in range(halves):
            loads.append(
                pltpu.make_async_copy(
                    v_hbm.at[c, :, :, pl.ds(h * HALF, HALF)],
                    vp.at[c, h, pl.ds(1, nxl), pl.ds(8, nyl), :],
                    load_sem.at[c * halves + h],
                )
            )
    base = 3 * halves
    load_u = pltpu.make_async_copy(u_hbm, ub, load_sem.at[base])
    load_s = pltpu.make_async_copy(s_hbm, sb, load_sem.at[base + 1])
    load_m = pltpu.make_async_copy(m_hbm, mk, load_sem.at[base + 2])
    hbm_tables = (tz_hbm, tx_hbm, tt_hbm)
    vmem_tables = (tz, tx, tt)
    load_t = [
        pltpu.make_async_copy(a, b, load_sem.at[base + 3 + n]) for n, (a, b) in enumerate(zip(hbm_tables, vmem_tables))
    ]
    load_u.start()
    for copy in loads:
        copy.start()
    load_s.start()
    load_m.start()
    for copy in load_t:
        copy.start()

    barrier = pltpu.get_barrier_semaphore()

    def greet_x(r, carry):
        pl.semaphore_signal(barrier, inc=1, device_id=(lax.rem(me_x + r, npx), me_y), device_id_type=MESH)
        return carry

    def greet_y(r, carry):
        pl.semaphore_signal(barrier, inc=1, device_id=(me_x, lax.rem(me_y + r, npy)), device_id_type=MESH)
        return carry

    lax.fori_loop(1, npx, greet_x, 0)
    lax.fori_loop(1, npy, greet_y, 0)

    load_u.wait()

    def widen(i, carry):
        for a in range(3):
            pair = ub[a, pl.ds(pl.multiple_of(i * 2 * nyl, 2 * nyl), 2 * nyl), :].astype(F32)
            for s in range(2):
                for h in range(halves):
                    up[a, h, 1 + 2 * i + s, 8:top, :] = pair[s * nyl:(s + 1) * nyl, h * HALF:(h + 1) * HALF]
        return carry

    lax.fori_loop(0, nxl // 2, widen, 0)
    for copy in loads:
        copy.wait()

    pl.semaphore_wait(barrier, npx - 1 + npy - 1)

    def remote(src, dst, send, recv, target):
        return pltpu.make_async_remote_copy(
            src_ref=src, dst_ref=dst, send_sem=send, recv_sem=recv, device_id=target, device_id_type=MESH
        )

    def x_pair(field, at, number):
        return (
            remote(at(field, nxl), at(field, 0), x_send.at[number], x_recv.at[number], (right_x, me_y)),
            remote(at(field, 1), at(field, nxl + 1), x_send.at[number + 1], x_recv.at[number + 1], (left_x, me_y)),
        )

    def at_plane(field, x):
        return field.at[:, :, x, pl.ds(8, nyl), :]

    def y_pair(send, recv, number):
        return (
            remote(send.at[0], recv.at[0], y_send.at[number], y_recv.at[number], (me_x, right_y)),
            remote(send.at[1], recv.at[1], y_send.at[number + 1], y_recv.at[number + 1], (me_x, left_y)),
        )

    for c in range(3):
        for h in range(halves):
            snd_y[0, c, h] = vp[c, h, 1:nxl + 1, top - 1, :].astype(BF16)
            snd_y[1, c, h] = vp[c, h, 1:nxl + 1, 8, :].astype(BF16)
            snd_y[0, 3 + c, h] = up[c, h, 1:nxl + 1, top - 1, :].astype(BF16)
            snd_y[1, 3 + c, h] = up[c, h, 1:nxl + 1, 8, :].astype(BF16)
    halo = y_pair(snd_y, rcv_y, 0) + x_pair(vp, at_plane, 0) + x_pair(up, at_plane, 2)
    for copy in halo:
        copy.start()

    def reduce_cell(c, g, right):
        inv = 1.0 / (c + right + g)
        return inv, c * inv

    def table_cell(i, carry):
        c, g = carry
        right = jnp.where((i == nyl - 1) & last_y, 0.0, 1.0)
        inv, k = reduce_cell(c, g, right)
        tau[i] = inv
        kap[i] = k
        return k, mu[...] + g * inv

    lax.fori_loop(1, nyl, table_cell, (jnp.ones_like(mu[...]), mu[...]))

    def owner_cell(i, carry):
        c, g, ground = carry
        inv, k = reduce_cell(c, g, 1.0)
        return k, muo[...] + g * inv, ground + k * g

    one = jnp.ones_like(muo[...])
    c, g, ground = lax.fori_loop(1, nyl - 1, owner_cell, (one, muo[...], jnp.zeros_like(one)))
    inv, link = reduce_cell(c, g, 1.0)
    from_left = g * inv
    end_ground = muo[...] + from_left + (ground + c * (g / (c + g)))
    ground = ground + link * g
    held = muo[...] + ground
    for b in range(npy - 1):
        inv = 1.0 / (link + held)
        phi = link * inv
        owner_inv[b] = inv
        owner_phi[b] = phi
        nxt = end_ground if b == npy - 2 else muo[...] + ground + from_left
        held = nxt + phi * held
    positive = held > 0.0
    owner_inv[npy - 1] = jnp.where(positive, 1.0 / jnp.where(positive, held, 1.0), 0.0)

    load_s.wait()
    load_m.wait()
    for copy in halo:
        copy.wait()

    for c in range(3):
        for h in range(halves):
            low_v, low_u = rcv_y[0, c, h].astype(F32), rcv_y[0, 3 + c, h].astype(F32)
            high_v, high_u = rcv_y[1, c, h].astype(F32), rcv_y[1, 3 + c, h].astype(F32)
            vp[c, h, 1:nxl + 1, 7, :] = jnp.where(first_y, 0.0, low_v)
            up[c, h, 1:nxl + 1, 7, :] = jnp.where(first_y, 0.0, low_u)
            vp[c, h, 1:nxl + 1, top, :] = jnp.where(last_y, 0.0, high_v)
            up[c, h, 1:nxl + 1, top, :] = jnp.where(last_y, 0.0, high_u)
    edge = jnp.zeros((nyl, HALF), F32)

    @pl.when(first_x)
    def _():
        for c in range(3):
            for h in range(halves):
                vp[c, h, 0, 8:top, :] = edge
                up[c, h, 0, 8:top, :] = edge

    @pl.when(last_x)
    def _():
        for c in range(3):
            for h in range(halves):
                vp[c, h, nxl + 1, 8:top, :] = edge
                up[c, h, nxl + 1, 8:top, :] = edge

    def whole(field, c, x):
        return jnp.concatenate([field[c, h, x] for h in range(halves)], axis=1)

    def middle(field, c, x):
        return jnp.concatenate([field[c, h, x, 8:top, :] for h in range(halves)], axis=1)

    def predict(i, carry):
        rows = pl.ds(pl.multiple_of(i * 2 * nyl, 2 * nyl), 2 * nyl)
        forcing = [sb[b, rows, :].astype(F32) for b in range(3)]
        for s in range(2):
            x = 2 * i + s
            scale = 1.0 / (1.0 + (DT * ALPHA) * mk[x].astype(F32))
            u, v = [], []
            slopes = [None] * 3
            for a in range(3):
                tall = whole(up, a, x + 1)
                u.append(tall[8:top])
                v.append(middle(vp, a, x + 1))
                below, above = z_shift(u[a], 0.0, 0.0)
                diffs = (
                    middle(up, a, x + 2) - middle(up, a, x),
                    tall[9:top + 1] - tall[7:top - 1],
                    above - below,
                )
                for b in range(3):
                    term = v[a] * diffs[b]
                    slopes[b] = term if slopes[b] is None else slopes[b] + term
            for b in range(3):
                tall = whole(vp, b, x + 1)
                xm, xp = middle(vp, b, x), middle(vp, b, x + 2)
                ym, yp = tall[7:top - 1], tall[9:top + 1]
                zm, zp = z_shift(v[b], 0.0, 0.0)
                convect = u[0] * (xp - xm) + u[1] * (yp - ym) + u[2] * (zp - zm)
                lap = (xp + xm) + (yp + ym) + (zp + zm) - 6.0 * v[b]
                change = 0.5 * (convect - slopes[b]) + NU * lap + forcing[b][s * nyl:(s + 1) * nyl]
                w = (v[b] + DT * change) * scale
                for h in range(halves):
                    part = w[:, h * HALF:(h + 1) * HALF]
                    if b == 0:
                        w0[h, x + 1] = part
                    elif b == 1:
                        w1[h, x, 8:top, :] = part
                    else:
                        w2[h, x] = part
        return carry

    lax.fori_loop(0, nxl // 2, predict, 0)

    for h in range(halves):
        wy_snd[0, h] = w1[h, :, top - 1, :]
        wy_snd[1, h] = w1[h, :, 8, :]
    halo = y_pair(wy_snd, wy_rcv, 2) + x_pair(w0, lambda field, x: field.at[:, x], 4)
    for copy in halo:
        copy.start()

    lane = lax.broadcasted_iota(jnp.int32, (nyl, HALF), 1)

    def flux_plane(x, carry):
        face = jnp.where(lane == HALF - 1, w2[halves - 1, x], 0.0)
        which = jnp.broadcast_to(ids[x], (nyl, HALF))
        return tuple(total + jnp.where(which == k, face, 0.0) for k, total in enumerate(carry))

    zero = jnp.zeros((nyl, HALF), F32)
    totals = lax.fori_loop(0, nxl, flux_plane, (zero,) * OUTLETS)
    fsum[0] = jnp.concatenate([jnp.sum(t, axis=0, keepdims=True) for t in totals], axis=0)

    def flux_x(r):
        return remote(fsum.at[0], fr1.at[me_x], f_send.at[r], f_recv.at[r], (lax.rem(me_x + r, npx), me_y))

    def flux_y(r):
        return remote(fsum.at[1], fr2.at[me_y], f_send.at[npx + r], f_recv.at[npx + r], (me_x, lax.rem(me_y + r, npy)))

    def run(first, last, action):
        def body(r, carry):
            action(r)
            return carry

        lax.fori_loop(first, last, body, 0)

    run(1, npx, lambda r: flux_x(r).start())
    fr1[me_x] = fsum[0]

    for copy in halo:
        copy.wait()
    for h in range(halves):
        w1[h, :, 7, :] = jnp.where(first_y, 0.0, wy_rcv[0, h])
        w1[h, :, top, :] = jnp.where(last_y, 0.0, wy_rcv[1, h])

    @pl.when(first_x)
    def _():
        for h in range(halves):
            w0[h, 0] = edge

    @pl.when(last_x)
    def _():
        for h in range(halves):
            w0[h, nxl + 1] = edge

    def diverge(x, carry):
        deep = jnp.concatenate([w2[h, x] for h in range(halves)], axis=1)
        below, above = z_shift(deep, 0.0, 0.0)
        for h in range(halves):
            cut = slice(h * HALF, (h + 1) * HALF)
            tall = w1[h, x]
            total = (w0[h, x + 2] - w0[h, x]) + (tall[9:top + 1] - tall[7:top - 1]) + (above - below)[:, cut]
            div[h, pl.ds(x, nyl, stride=nxl), :] = 0.5 * total
        return carry

    lax.fori_loop(0, nxl // 2, diverge, 0)
    run(1, npx, lambda r: flux_x(r).wait())
    fsum[1] = jnp.sum(fr1[...], axis=0)
    run(1, npy, lambda r: flux_y(r).start())
    fr2[me_y] = fsum[1]
    lax.fori_loop(nxl // 2, nxl, diverge, 0)
    run(1, npy, lambda r: flux_y(r).wait())
    flux = jnp.sum(fr2[...], axis=0) * (1.0 / (nx * npy * nyl))
    press = [jnp.sum(resb[k] * flux, axis=0, keepdims=True) for k in range(OUTLETS)]

    def lower(x, carry):
        which = jnp.broadcast_to(ids[x], (nyl, HALF))
        drop = jnp.zeros((nyl, HALF), F32)
        for k in range(OUTLETS):
            drop = jnp.where(which == k, jnp.broadcast_to(press[k], (nyl, HALF)), drop)
        drop = DT * jnp.where(lane == HALF - 1, drop, 0.0)
        w2[halves - 1, x] = w2[halves - 1, x] - drop
        here = pl.ds(x, nyl, stride=nxl)
        div[halves - 1, here, :] = div[halves - 1, here, :] - 0.5 * pltpu.roll(drop, HALF - 1, 1)
        return carry

    lax.fori_loop(0, nxl, lower, 0)

    outs = []
    for h in range(halves):
        cut = pl.ds(h * HALF, HALF)
        outs.append(pltpu.make_async_copy(w0.at[h, pl.ds(1, nxl)], w_out.at[0, :, :, cut], out_sem.at[3 * h]))
        outs.append(
            pltpu.make_async_copy(w1.at[h, :, pl.ds(8, nyl), :], w_out.at[1, :, :, cut], out_sem.at[3 * h + 1])
        )
        outs.append(pltpu.make_async_copy(w2.at[h], w_out.at[2, :, :, cut], out_sem.at[3 * h + 2]))
    for copy in outs:
        copy.start()

    for copy in load_t:
        copy.wait()
    cells = nxl * nyl

    def depth_chunk(j, carry):
        here = pl.ds(pl.multiple_of(j * 256, 256), 256)
        value = jnp.concatenate([div[h, here, :] for h in range(halves)], axis=1)
        out = dot_parts((tz[0], tz[1]), split(value, 2), ((1,), (1,)))
        for p in range(npx):
            msg[p, :, here] = out[p * kzl:(p + 1) * kzl]
        return carry

    lax.fori_loop(0, cells // 256, depth_chunk, 0)

    def forth(r):
        p = lax.rem(me_x + r, npx)
        return remote(msg.at[p], got.at[me_x], a_send.at[r], a_recv.at[r], (p, me_y))

    run(1, npx, lambda r: forth(r).start())
    got[me_x] = msg[me_x]
    run(1, npx, lambda r: forth(r).wait())

    groups = nyl // 4
    wides = npx // 4

    def gather(j, carry):
        yg = j // wides
        sg = lax.rem(j, wides)
        lanes = pl.ds(pl.multiple_of(yg * HALF, HALF), HALF)
        out = swap_groups([got[4 * sg + a, :, lanes] for a in range(4)])
        for b in range(4):
            rows = pl.ds(pl.multiple_of((4 * yg + b) * kzl, kzl), kzl)
            cols[rows, pl.ds(pl.multiple_of(sg * HALF, HALF), HALF)] = out[b]
        return carry

    lax.fori_loop(0, groups * wides, gather, 0)

    total_rows = nyl * kzl
    chunk = 128

    def x_transform(parts):
        def body(j, carry):
            rows = pl.ds(pl.multiple_of(j * chunk, chunk), chunk)
            cols[rows, :] = dot_parts(split(cols[rows, :], len(parts)), parts, ((1,), (0,)))
            return carry

        lax.fori_loop(0, total_rows // chunk, body, 0)

    x_transform((tt[0], tt[1]))

    def row_of(i):
        return pl.ds(pl.multiple_of(i * kzl, kzl), kzl)

    def down(i, carry):
        r, ends = carry
        ends = ends + kap[i] * r
        nxt = cols[row_of(i + 1), :] + tau[i] * r
        cols[row_of(i + 1), :] = nxt
        return nxt, ends

    r, ends = lax.fori_loop(1, nyl - 1, down, (cols[row_of(1), :], cols[row_of(0), :]))
    ends = ends + kap[nyl - 1] * r
    over = tau[nyl - 1] * r
    for j in range(npy):
        isnd[j, 0:kown, :] = ends[j * kown:(j + 1) * kown]
        isnd[j, kown:2 * kown, :] = over[j * kown:(j + 1) * kown]

    def collect(r):
        j = lax.rem(me_y + r, npy)
        return remote(isnd.at[j], ircv.at[me_y], i_send.at[r], i_recv.at[r], (me_x, j))

    run(1, npy, lambda r: collect(r).start())
    ircv[me_y] = isnd[me_y]
    run(1, npy, lambda r: collect(r).wait())

    rho = []
    for b in range(npy):
        value = ircv[b, 0:kown, :]
        if b > 0:
            value = value + ircv[b - 1, kown:2 * kown, :]
        rho.append(value)
    depth_mode = lax.broadcasted_iota(jnp.int32, (kown, nx), 0) + me_x * kzl + me_y * kown
    row_mode = lax.broadcasted_iota(jnp.int32, (kown, nx), 1)
    mean = sum(rho[1:], rho[0]) * (1.0 / (npy * nyl))
    mean = jnp.where((depth_mode == 0) & (row_mode == 0), mean, 0.0)
    half_sum = (nyl - 1) / 2.0
    for b in range(npy):
        weight = 1.0 + (0.0 if b == 0 else half_sum) + (2.0 * half_sum if b == npy - 1 else half_sum)
        rho[b] = rho[b] - weight * mean
    for b in range(npy - 1):
        rho[b + 1] = rho[b + 1] + owner_phi[b] * rho[b]
    value = -owner_inv[npy - 1] * rho[npy - 1]
    jsnd[npy - 1, 0:kown, :] = value
    jsnd[npy - 1, kown:2 * kown, :] = jnp.zeros_like(value)
    jsnd[npy - 1, 2 * kown:3 * kown, :] = mean
    for b in range(npy - 2, -1, -1):
        jsnd[b, kown:2 * kown, :] = value
        value = owner_phi[b] * value - owner_inv[b] * rho[b]
        jsnd[b, 0:kown, :] = value
        jsnd[b, 2 * kown:3 * kown, :] = mean

    def hand_back(r):
        j = lax.rem(me_y + r, npy)
        return remote(jsnd.at[j], jrcv.at[me_y], i_send.at[npy + r], i_recv.at[npy + r], (me_x, j))

    run(1, npy, lambda r: hand_back(r).start())
    jrcv[me_y] = jsnd[me_y]
    run(1, npy, lambda r: hand_back(r).wait())
    for j in range(npy):
        for part in range(3):
            back[part, j * kown:(j + 1) * kown, :] = jrcv[j, part * kown:(part + 1) * kown, :]
    first_value, mean_rows = back[0], back[2]

    def up_again(n, q):
        i = nyl - 1 - n
        share = 0.5 * (i + 1).astype(F32)
        q = tau[i] * (q - cols[row_of(i), :] + mean_rows * share) + kap[i] * first_value
        cols[row_of(i), :] = q
        return q

    lax.fori_loop(0, nyl - 1, up_again, back[1])
    cols[row_of(0), :] = first_value

    x_transform((tx[0], tx[1], tx[2]))

    def scatter(j, carry):
        yg = j // wides
        sg = lax.rem(j, wides)
        lanes = pl.ds(pl.multiple_of(sg * HALF, HALF), HALF)
        tiles = []
        for b in range(4):
            rows = pl.ds(pl.multiple_of((4 * yg + b) * kzl, kzl), kzl)
            tiles.append(cols[rows, lanes])
        out = swap_groups(tiles)
        for a in range(4):
            msg[4 * sg + a, :, pl.ds(pl.multiple_of(yg * HALF, HALF), HALF)] = out[a]
        return carry

    lax.fori_loop(0, groups * wides, scatter, 0)


    def home(r):
        p = lax.rem(me_x + r, npx)
        return remote(msg.at[p], got2.at[me_x], a_send.at[npx + r], a_recv.at[npx + r], (p, me_y))

    run(1, npx, lambda r: home(r).start())
    got2[me_x] = msg[me_x]
    run(1, npx, lambda r: home(r).wait())

    per = 256 // nxl
    for j in range(cells // 256):
        value = got2[:, :, j * 256:(j + 1) * 256].reshape(nz, 256)
        out = dot_parts(split(value.T, 3), (tz[0], tz[1], tz[2]), ((1,), (0,)))
        for y in range(per):
            for h in range(halves):
                qp[h, 1:nxl + 1, 8 + j * per + y, :] = out[y * nxl:(y + 1) * nxl, h * HALF:(h + 1) * HALF]

    for h in range(halves):
        qy_snd[0, h] = qp[h, 1:nxl + 1, top - 1, :]
        qy_snd[1, h] = qp[h, 1:nxl + 1, 8, :]
    halo = y_pair(qy_snd, qy_rcv, 4) + x_pair(qp, lambda field, x: field.at[:, x, pl.ds(8, nyl), :], 6)
    for copy in halo:
        copy.start()
    for copy in halo:
        copy.wait()
    for h in range(halves):
        qp[h, 1:nxl + 1, 7, :] = jnp.where(first_y, qy_snd[1, h], qy_rcv[0, h])
        qp[h, 1:nxl + 1, top, :] = jnp.where(last_y, qy_snd[0, h], qy_rcv[1, h])

    @pl.when(first_x)
    def _():
        for h in range(halves):
            qp[h, 0, 8:top, :] = qp[h, 1, 8:top, :]

    @pl.when(last_x)
    def _():
        for h in range(halves):
            qp[h, nxl + 1, 8:top, :] = qp[h, nxl, 8:top, :]

    give = pltpu.make_async_copy(qp, q_out, out_sem.at[3 * halves])
    give.start()
    for copy in outs:
        copy.wait()
    give.wait()


def main_call(dims, v, u, s, m, ids, resb, tables, mu, muo):
    npx, npy, nxl, nyl, nz = dims
    nx = npx * nxl
    kzl = nz // npx
    kown = kzl // npy
    halves = nz // HALF
    wide = nyl + 16
    cells = nxl * nyl
    vmem = pltpu.VMEM
    anywhere = pl.BlockSpec(memory_space=pl.ANY)
    here = pl.BlockSpec(memory_space=pltpu.VMEM)
    dma = pltpu.SemaphoreType.DMA
    scratch = [
        vmem((3, halves, nxl + 2, wide, HALF), F32),
        vmem((3, halves, nxl + 2, wide, HALF), F32),
        vmem((3, cells, nz), BF16),
        vmem((3, cells, nz), BF16),
        vmem((nxl, nyl, nz), jnp.int32),
        vmem((halves, nxl + 2, nyl, HALF), F32),
        vmem((halves, nxl, wide, HALF), F32),
        vmem((halves, nxl, nyl, HALF), F32),
        vmem((2, 6, halves, nxl, HALF), BF16),
        vmem((2, 6, halves, nxl, HALF), BF16),
        vmem((2, halves, nxl, HALF), F32),
        vmem((2, halves, nxl, HALF), F32),
        vmem((2, OUTLETS, HALF), F32),
        vmem((npx, OUTLETS, HALF), F32),
        vmem((npy, OUTLETS, HALF), F32),
        vmem((halves, cells, HALF), F32),
        vmem((npx, kzl, cells), F32),
        vmem((npx, kzl, cells), F32),
        vmem((npx, kzl, cells), F32),
        vmem((nyl * kzl, nx), F32),
        vmem((nyl, kzl, nx), F32),
        vmem((nyl, kzl, nx), F32),
        vmem((npy, kown, nx), F32),
        vmem((npy, kown, nx), F32),
        vmem((npy, 2 * kown, nx), F32),
        vmem((npy, 2 * kown, nx), F32),
        vmem((npy, 3 * kown, nx), F32),
        vmem((npy, 3 * kown, nx), F32),
        vmem((3, kzl, nx), F32),
        vmem((halves, nxl + 2, wide, HALF), F32),
        vmem((2, halves, nxl, HALF), F32),
        vmem((2, halves, nxl, HALF), F32),
    ]
    scratch += [vmem(t.shape, BF16) for t in tables]
    scratch += [
        dma((3 * halves + 3 + len(tables),)),
        dma((8,)),
        dma((8,)),
        dma((6,)),
        dma((6,)),
        dma((npx + npy,)),
        dma((npx + npy,)),
        dma((2 * npx,)),
        dma((2 * npx,)),
        dma((2 * npy,)),
        dma((2 * npy,)),
        dma((3 * halves + 1,)),
    ]
    return pl.pallas_call(
        functools.partial(main_kernel, dims),
        out_shape=(
            jax.ShapeDtypeStruct((3, nxl, nyl, nz), F32),
            jax.ShapeDtypeStruct((halves, nxl + 2, wide, HALF), F32),
        ),
        in_specs=[anywhere] * 4 + [here] * 2 + [anywhere] * len(tables) + [here] * 2,
        out_specs=(anywhere, anywhere),
        scratch_shapes=scratch,
        compiler_params=pltpu.CompilerParams(
            collective_id=0, has_side_effects=True, vmem_limit_bytes=56 * 2**20
        ),
        name="project",
    )(v, u, s, m, ids, resb, *tables, mu, muo)


def final_kernel(dims, steps, w, u, qp, slots, v_out, picked, sig):
    npx, npy, nxl, nyl, nz = dims
    halves = nz // HALF
    per = nxl // steps
    step = pl.program_id(0)
    top = 8 + nyl

    def middle(x):
        return jnp.concatenate([qp[h, x, 8:top, :] for h in range(halves)], axis=1)

    for i in range(per // 2):
        pair = [u[a, i * 2 * nyl:(i + 1) * 2 * nyl, :].astype(F32) for a in range(3)]
        for s in range(2):
            n = 2 * i + s
            x = step * per + n
            tall = jnp.concatenate([qp[h, x + 1] for h in range(halves)], axis=1)
            center = tall[8:top]
            lane = lax.broadcasted_iota(jnp.int32, center.shape, 1)
            below = jnp.where(lane == 0, center, pltpu.roll(center, 1, 1))
            above = jnp.where(lane == nz - 1, center, pltpu.roll(center, nz - 1, 1))
            slopes = (middle(x + 2) - middle(x), tall[9:top + 1] - tall[7:top - 1], above - below)
            total = None
            for b in range(3):
                v = w[b, n] - 0.5 * slopes[b]
                v_out[b, n] = v
                term = pair[b][s * nyl:(s + 1) * nyl] * v
                total = term if total is None else total + term
            total = -ALPHA * total
            for h in range(halves):
                sig[h, pl.ds(pl.multiple_of(x * nyl, 8), nyl), :] = total[:, h * HALF:(h + 1) * HALF]

    @pl.when(step == steps - 1)
    def _():
        column = slots[...]
        shape = (column.shape[0], nxl * nyl)
        cell = lax.broadcasted_iota(jnp.int32, shape, 1) * halves
        dot = functools.partial(jnp.dot, preferred_element_type=F32)
        total = None
        for h in range(halves):
            chosen = (jnp.broadcast_to(column, shape) == cell + h).astype(F32).astype(BF16)
            value = sig[h]
            first = value.astype(BF16)
            rest = value - first.astype(F32)
            second = rest.astype(BF16)
            third = (rest - second.astype(F32)).astype(BF16)
            part = dot(chosen, first) + (dot(chosen, second) + dot(chosen, third))
            total = part if total is None else total + part
        picked[...] = total


def final_call(dims, w, u, qp, slots):
    npx, npy, nxl, nyl, nz = dims
    halves = nz // HALF
    steps = 8
    per = nxl // steps
    cells = nxl * nyl
    count = slots.shape[0]
    return pl.pallas_call(
        functools.partial(final_kernel, dims, steps),
        grid=(steps,),
        out_shape=(
            jax.ShapeDtypeStruct((3, nxl, nyl, nz), F32),
            jax.ShapeDtypeStruct((count, SEG), F32),
        ),
        in_specs=[
            pl.BlockSpec((3, per, nyl, nz), lambda i: (0, i, 0, 0)),
            pl.BlockSpec((3, per * nyl, nz), lambda i: (0, i, 0)),
            pl.BlockSpec(qp.shape, lambda i: (0, 0, 0, 0)),
            pl.BlockSpec(slots.shape, lambda i: (0, 0)),
        ],
        out_specs=(
            pl.BlockSpec((3, per, nyl, nz), lambda i: (0, i, 0, 0)),
            pl.BlockSpec((count, SEG), lambda i: (0, 0)),
        ),
        scratch_shapes=[pltpu.VMEM((halves, cells, HALF), F32)],
        compiler_params=pltpu.CompilerParams(vmem_limit_bytes=40 * 2**20),
        name="correct",
    )(w, u, qp, slots)


def route_kernel(npx, npy, rows, labels, rows_out, labels_out, mid_rows, mid_labels, send, recv):
    me_x = lax.axis_index("px")
    me_y = lax.axis_index("py")
    barrier = pltpu.get_barrier_semaphore()

    def loop(count, action):
        def body(r, carry):
            action(r)
            return carry

        lax.fori_loop(1, count, body, 0)

    def at_x(r):
        return (lax.rem(me_x + r, npx), me_y)

    def at_y(r):
        return (me_x, lax.rem(me_y + r, npy))

    loop(npx, lambda r: pl.semaphore_signal(barrier, inc=1, device_id=at_x(r), device_id_type=MESH))
    loop(npy, lambda r: pl.semaphore_signal(barrier, inc=1, device_id=at_y(r), device_id_type=MESH))
    pl.semaphore_wait(barrier, npx - 1 + npy - 1)

    def remote(src, dst, number, target):
        return pltpu.make_async_remote_copy(
            src_ref=src, dst_ref=dst, send_sem=send.at[number], recv_sem=recv.at[number],
            device_id=target, device_id_type=MESH,
        )

    def rows_x(r):
        return remote(rows.at[at_x(r)[0]], mid_rows.at[me_x], r, at_x(r))

    def labels_x(r):
        return remote(labels.at[at_x(r)[0]], mid_labels.at[me_x], npx + r, at_x(r))

    def rows_y(r):
        return remote(mid_rows.at[:, at_y(r)[1]], rows_out.at[me_y], 2 * npx + r, at_y(r))

    def labels_y(r):
        return remote(mid_labels.at[:, at_y(r)[1]], labels_out.at[me_y], 2 * npx + npy + r, at_y(r))

    loop(npx, lambda r: rows_x(r).start())
    loop(npx, lambda r: labels_x(r).start())
    mid_rows[me_x] = rows[me_x]
    mid_labels[me_x] = labels[me_x]
    loop(npx, lambda r: rows_x(r).wait())
    loop(npx, lambda r: labels_x(r).wait())
    loop(npy, lambda r: rows_y(r).start())
    loop(npy, lambda r: labels_y(r).start())
    rows_out[me_y] = mid_rows[:, me_y]
    labels_out[me_y] = mid_labels[:, me_y]
    loop(npy, lambda r: rows_y(r).wait())
    loop(npy, lambda r: labels_y(r).wait())


def route_call(npx, npy, rows, labels):
    here = pl.BlockSpec(memory_space=pltpu.VMEM)
    capacity = rows.shape[2]
    return pl.pallas_call(
        functools.partial(route_kernel, npx, npy),
        out_shape=(
            jax.ShapeDtypeStruct((npy, npx, capacity, SEG), F32),
            jax.ShapeDtypeStruct((npy, npx, 1, SEG), jnp.int32),
        ),
        in_specs=[here, here],
        out_specs=(here, here),
        scratch_shapes=[
            pltpu.VMEM(rows.shape, F32),
            pltpu.VMEM(labels.shape, jnp.int32),
            pltpu.SemaphoreType.DMA((2 * (npx + npy),)),
            pltpu.SemaphoreType.DMA((2 * (npx + npy),)),
        ],
        compiler_params=pltpu.CompilerParams(
            collective_id=1, has_side_effects=True, vmem_limit_bytes=24 * 2**20
        ),
        name="route",
    )(rows, labels)


def local(
    base_flow, adjoint_start, source, solid_mask, outlet_ids, resist,
    tile_owner, tile_slot, tile_column, control_basis,
):
    _, nxl, nyl, nz = adjoint_start.shape
    npx, npy = lax.axis_size("px"), lax.axis_size("py")
    dims = (npx, npy, nxl, nyl, nz)
    nx = npx * nxl
    kzl = nz // npx
    kown = kzl // npy
    devices = npx * npy
    capacity = 2

    owners = tile_owner[:, 0]
    count = owners.shape[0]
    order = jnp.arange(count, dtype=jnp.int32)
    ranks = jnp.sum(
        ((owners[:, None] == owners[None, :]) & (order[None, :] < order[:, None])).astype(jnp.int32), axis=1
    )
    place = owners * capacity + ranks
    match = place[None, :] == jnp.arange(devices * capacity, dtype=jnp.int32)[:, None]
    column_at = jnp.sum(jnp.where(match, tile_column[None, :] + 1, 0), axis=1) - 1
    label_at = jnp.sum(jnp.where(match, tile_slot[None, :] + 1, 0), axis=1) - 1
    labels = jnp.pad(label_at.reshape(npx, npy, 1, capacity), ((0, 0), (0, 0), (0, 0), (0, SEG - capacity)))

    lam_x = jnp.asarray(-eigen_np(nx))
    lam_z = jnp.asarray(-eigen_np(nz))
    at = lax.axis_index("px") * kzl
    mine = lax.dynamic_slice(lam_z, (at,), (kzl,))
    owned = lax.dynamic_slice(lam_z, (at + lax.axis_index("py") * kown,), (kown,))
    mu = lam_x[None, :] + mine[:, None]
    muo = lam_x[None, :] + owned[:, None]
    tz, tx = table_np(nz), table_np(nx)
    tables = [split_np(tz, 3), split_np(tx, 3), split_np(np.ascontiguousarray(tx.T), 2)]
    tables = [jnp.asarray(np.stack(t)) for t in tables]

    ids = outlet_ids.reshape(nxl, nyl, 1)
    resb = jnp.broadcast_to(resist[:, :, None], (OUTLETS, OUTLETS, HALF))
    flow = base_flow.reshape(3, nxl * nyl, nz)
    w, qp = main_call(
        dims, adjoint_start, flow, source.reshape(3, nxl * nyl, nz), solid_mask, ids, resb, tables, mu, muo
    )
    velocity, picked = final_call(dims, w, flow, qp, column_at[:, None])
    rows, got_labels = route_call(npx, npy, picked.reshape(npx, npy, capacity, SEG), labels)
    rows = rows.reshape(devices * capacity, SEG)
    got_labels = got_labels[:, :, 0, :capacity].reshape(devices * capacity)
    scores = jnp.dot(rows, control_basis.T, precision=lax.Precision.HIGHEST, preferred_element_type=F32)
    chosen = got_labels[:, None] == jnp.arange(control_basis.shape[0], dtype=jnp.int32)[None, :]
    grad = jnp.sum(jnp.where(chosen, scores, jnp.float32(0.0)), axis=0)
    return velocity, grad


def solution(mesh):
    in_specs = (
        P(None, "px", "py", None),
        P(None, "px", "py", None),
        P(None, "px", "py", None),
        P("px", "py", None),
        P("px", "py"),
        P(),
        P(("px", "py"), None),
        P(("px", "py")),
        P(("px", "py")),
        P(("px", "py"), None),
    )
    out_specs = (P(None, "px", "py", None), P(("px", "py")))
    return jax.shard_map(local, mesh=mesh, in_specs=in_specs, out_specs=out_specs, check_vma=False)
```

time: 417 us -> 144 us (0.35); the launches traced: 413 us -> 144 us
  Pallas kernels: 0 us -> 130 us
  blocking collectives: 108 us -> 0 us
  starting transfers between devices: 88.6 us -> 0 us
  waiting for transfers between devices: 83.5 us -> 0 us
  local copies, waits for them, and re-layouts: 60.7 us -> 8.92 us
  other arithmetic: 40 us -> 3.74 us
  matrix products: 29.7 us -> 1 us
    pallas_call x0 -> x3, Pallas kernels: none -> 130 us  [the longest x1 97.3 us: main_call(): pl.pallas_call(functools.partial(main_kernel, dims), out_shape=(jax.Shape...]
    psum x1 -> x0, blocking collectives: 79.2 us -> none  [local(): flux = lax.psum(partial_flux, ('px', 'py')) / (NX * NY)]
    all_to_all x7 -> x0, waiting for transfers between devices: 67.3 us -> none  [the longest x1 21.8 us: solve_pressure(): lax.all_to_all(middle, 'py', split_axis=1, concat_axis=0, tiled=True)]
    ppermute x16 -> x0, starting transfers between devices: 46 us -> none  [the longest x8 32.6 us: padded_2(): lax.ppermute(tail, axis, [(i, (i + 1) % count) for i in range(ends)])]
    all_to_all x7 -> x0, starting transfers between devices: 42.6 us -> none  [the longest x1 9.6 us: solve_pressure(): lax.all_to_all(depth_coeffs, 'px', split_axis=1, concat_axis=2, tiled=True)]
    all_to_all x1 -> x0, blocking collectives: 29 us -> none  [solve_pressure(): lax.all_to_all(cols_back, 'py', split_axis=0, concat_axis=1, tiled=True)]
    dot_general x8 -> x1, matrix products: 29.7 us -> 1 us  [local(): jnp.dot(rows, control_basis.T, precision=lax.Precision.HIGHEST, preferred...]
    unnamed x32 -> x14, local copies, waits for them, and re-layouts: 23.3 us -> 3.03 us
  transfers between devices with their start and end apart: 23 -> 0, of which waited for: 11 -> 0; matrix products, arithmetic and copies ran while one was open for 13% -> 0% of each run, Pallas kernels for 0% -> 0%
where the time goes in v1:
time: 144 us
  Pallas kernels  130 us (90%)
  local copies, waits for them, and re-layouts  8.92 us (6%)
  other arithmetic  3.74 us (3%)
    pallas_call x1, Pallas kernels, main_call(): pl.pallas_call(functools.partial(main_kernel, dims), out_shape=(jax.Shape...  97.3 us
    pallas_call x1, Pallas kernels, route_call(): pl.pallas_call(functools.partial(route_kernel, npx, npy), out_shape=(jax....  27.3 us
    pallas_call x1, Pallas kernels, final_call(): pl.pallas_call(functools.partial(final_kernel, dims, steps), grid=(steps,...  5.12 us
    unnamed x14, local copies, waits for them, and re-layouts  3.03 us

profile of v1, /device:TPU:1, one launch (start us, length us, event | category | flops | bytes accessed | tf_op | source)
XLA Modules:
  0.0 144.1 jit_solution(11698112618739314798)
XLA Ops:
  0.6 0.0 copy-start
  0.7 1.3 dynamic_slice.7
  1.9 1.9 %broadcast_add_fusion.3 = f32[512]{0:T(512)} fusion(f32[512]{0:T(512)} %constant.33.clone, f32[]{:T(128)} %bitcast.3), kind=kLoop, calls=%fused_computation.14 | loop fusion | flops 512 | bytes 4100 | tf_op jit(solution)/shard_map/add | solution.py:857
  3.8 0.8 dynamic_slice.6
  4.6 1.4 broadcast_add_fusion.mu
  6.0 1.7 %copy.21.ids = s32[32,24,1]{2,1,0:T(8,128)} copy(s32[32,24,1]{0,1,2:T(8,128)} %bitcast.18) | data formatting | bytes 6144 | tf_op jit(solution)/shard_map/reshape | solution.py:862
  7.6 1.4 broadcast_in_dim.23.resb
  9.0 97.3 %project.1 = (f32[3,32,24,256]{3,2,1,0:T(8,128)}, f32[2,34,40,128]{3,2,1,0:T(8,128)}) custom-call(f32[3,32,24,256]{3,2,1,0:T(8,128)} %v_hbm.1, bf16[3,768,256]{2,1,0:T(8,128)(2,1)} %bitcast.12, bf16[3,768,256]{2,1,0:T(8,128)(2,1)} %bitcast.16, s32[32,24,256]{2,1,0:T(8,128)} %m_hbm.1, s32[32,24,1]{2,1,0:T(8,128)} %copy.21.ids, ...), custom_call_target="tpu_custom_call" | custom-call | tf_op jit(solution)/shard_map/project/pallas_call | solution.py:652
  106.3 0.0 copy-done.4
  106.3 0.2 convert_reduce_fusion
  106.5 0.0 copy-done.5
  106.5 0.0 copy-done.6
  106.5 0.3 select_reduce_fusion
  106.8 0.1 copy.22.slots
  107.0 1.7 %copy-done.2 = f32[3,32,24,256]{3,2,1,0:T(8,128)S(1)} copy-done((f32[3,32,24,256]{3,2,1,0:T(8,128)S(1)}, f32[3,32,24,256]{3,2,1,0:T(8,128)}, u32[]{:S(2)}) %copy-start.2) | copy-done | bytes 2359320
  108.6 1.3 copy-done.3
  110.0 5.1 %correct.1 = (f32[3,32,24,256]{3,2,1,0:T(8,128)}, f32[512,128]{1,0:T(8,128)S(1)}) custom-call(f32[3,32,24,256]{3,2,1,0:T(8,128)S(1)} %copy-done.2, bf16[3,768,256]{2,1,0:T(8,128)(2,1)S(1)} %bitcast.13, f32[2,34,40,128]{3,2,1,0:T(8,128)S(1)} %copy-done.3, s32[512,1]{1,0:T(8,128)S(1)} %copy.22.slots), custom_call_target="tpu_custom_call" | custom-call | tf_op jit(solution)/shard_map/correct/pallas_call | solution.py:725
  115.1 0.1 sub.13
  115.2 0.1 pad.4.labels
  115.3 27.3 %route.1 = (f32[16,16,2,128]{3,2,1,0:T(2,128)S(1)}, s32[16,16,1,128]{3,2,1,0:T(1,128)S(1)}) custom-call(f32[16,16,2,128]{3,2,1,0:T(2,128)S(1)} %bitcast.14, s32[16,16,1,128]{3,2,1,0:T(1,128)S(1)} %pad.4.labels), custom_call_target="tpu_custom_call" | custom-call | tf_op jit(solution)/shard_map/route/pallas_call | solution.py:805
  142.6 0.3 slice_reduce_fusion
  143.0 0.1 eq.47
  143.1 0.0 copy-done
  143.1 1.0 fusion
  (11 shorter events, 0.0 us)
Async XLA Ops:
  0.6 142.5 %copy-start = (f32[32,128]{1,0:T(8,128)S(1)}, f32[32,128]{1,0:T(8,128)}, u32[]{:S(2)}) copy-start(f32[32,128]{1,0:T(8,128)} %param.24) | copy-start | bytes 49156
  9.0 97.3 %copy-start.4 = (s32[256,1]{0,1:T(1,128)S(1)}, s32[256,1]{0,1:T(1,128)}, u32[]{:S(2)}) copy-start(s32[256,1]{0,1:T(1,128)} %param.21) | copy-start | bytes 3076
  9.0 97.5 %copy-start.5 = (s32[256]{0:T(256)S(1)}, s32[256]{0:T(256)}, u32[]{:S(2)}) copy-start(s32[256]{0:T(256)} %param.22) | copy-start | bytes 3076
  9.0 97.5 %copy-start.6 = (s32[256]{0:T(256)S(1)}, s32[256]{0:T(256)}, u32[]{:S(2)}) copy-start(s32[256]{0:T(256)} %param.23) | copy-start | bytes 3076
  9.0 97.9 %copy-start.1 = (bf16[3,32,24,256]{3,2,1,0:T(8,128)(2,1)S(1)}, bf16[3,32,24,256]{3,2,1,0:T(8,128)(2,1)}, u32[]{:S(2)}) copy-start(bf16[3,32,24,256]{3,2,1,0:T(8,128)(2,1)} %param.15) | copy-start | bytes 3538948
  107.0 1.7 %copy-start.2 = (f32[3,32,24,256]{3,2,1,0:T(8,128)S(1)}, f32[3,32,24,256]{3,2,1,0:T(8,128)}, u32[]{:S(2)}) copy-start(f32[3,32,24,256]{3,2,1,0:T(8,128)} %get-tuple-element.8.w) | copy-start | bytes 7077892
  108.6 1.3 copy-start.3

commit v2 on v1

v2 whole, which is shorter than its diff:
```python
import functools
import math

import jax
import jax.numpy as jnp
import numpy as np
from jax import lax
from jax.experimental import pallas as pl
from jax.experimental.pallas import tpu as pltpu
from jax.sharding import PartitionSpec as P

SEG = 128
OUTLETS = 8
DT = 0.1
NU = 0.5
ALPHA = 5.0
HALF = 128
MESH = pl.DeviceIdType.MESH
F32 = jnp.float32
BF16 = jnp.bfloat16


def table_np(count):
    order = np.arange(count).astype(np.float32)
    modes = order[:, None]
    points = order[None, :]
    weights = np.where(modes == 0.0, math.sqrt(1.0 / count), math.sqrt(2.0 / count)).astype(np.float32)
    angle = np.float32(np.pi) * (points + np.float32(0.5)) * modes / np.float32(count)
    return (weights * np.cos(angle.astype(np.float32))).astype(np.float32)


def eigen_np(count):
    order = np.arange(count).astype(np.float32)
    angle = (np.float32(np.pi) * order / np.float32(count)).astype(np.float32)
    return (np.float32(2.0) * np.cos(angle) - np.float32(2.0)).astype(np.float32)


def split_np(table, count):
    parts = []
    for _ in range(count):
        parts.append(table.astype(jnp.bfloat16))
        table = table - parts[-1].astype(np.float32)
    return tuple(parts)


def split(value, count):
    parts = []
    for _ in range(count):
        parts.append(value.astype(BF16))
        value = value - parts[-1].astype(F32)
    return tuple(parts)


def dot_parts(a_parts, b_parts, contract):
    dims = ((contract[0], contract[1]), ((), ()))
    dot = functools.partial(lax.dot_general, dimension_numbers=dims, preferred_element_type=F32)
    total = None
    for order in range(len(a_parts) - 1, -1, -1):
        for i in range(order + 1):
            term = dot(a_parts[i], b_parts[order - i])
            total = term if total is None else total + term
    return total


def swap_groups(tiles):
    lane = lax.broadcasted_iota(jnp.int32, tiles[0].shape, 1)
    odd = (lane // 32) % 2 == 1
    far = lane >= 64
    t0, t1, t2, t3 = tiles
    a0 = jnp.where(odd, pltpu.roll(t1, 32, 1), t0)
    a1 = jnp.where(odd, t1, pltpu.roll(t0, 96, 1))
    a2 = jnp.where(odd, pltpu.roll(t3, 32, 1), t2)
    a3 = jnp.where(odd, t3, pltpu.roll(t2, 96, 1))
    return (
        jnp.where(far, pltpu.roll(a2, 64, 1), a0),
        jnp.where(far, pltpu.roll(a3, 64, 1), a1),
        jnp.where(far, a2, pltpu.roll(a0, 64, 1)),
        jnp.where(far, a3, pltpu.roll(a1, 64, 1)),
    )


def z_shift(field, edge_low, edge_high):
    depth = field.shape[1]
    lane = lax.broadcasted_iota(jnp.int32, field.shape, 1)
    below = jnp.where(lane == 0, edge_low, pltpu.roll(field, 1, 1))
    above = jnp.where(lane == depth - 1, edge_high, pltpu.roll(field, depth - 1, 1))
    return below, above


def main_kernel(
    dims,
    v_hbm, u_hbm, s_hbm, m_hbm, ids, resist, owner_col, owner_row, slot_row, column_row, basis,
    tz_hbm, tx_hbm, tt_hbm, lam_x, lam_z,
    v_out, grad_out,
    vp, up, ub, sb, mk, idb, w0, w1, w2, snd_y, rcv_y, wy_snd, wy_rcv, fsum, fr1, fr2,
    div, msg, got, got2, cols, tau, kap, owner_inv, owner_phi,
    isnd, ircv, jsnd, jrcv, back, qp, qy_snd, qy_rcv, vel, sig,
    pick, ask, asked, asks, wanted, chosen, reply, replies, fetch, fetched, give, given, gives, taken,
    tz, tx, tt,
    load_sem, x_send, x_recv, y_send, y_recv, f_send, f_recv, a_send, a_recv, i_send, i_recv, r_send, r_recv, out_sem,
):
    npx, npy, nxl, nyl, nz = dims
    nx = npx * nxl
    kzl = nz // npx
    kown = kzl // npy
    halves = nz // HALF
    cells = nxl * nyl
    per = 256 // nxl
    pieces = nyl // per
    group = 2 * npy
    places = npx * group
    me_x = lax.axis_index("px")
    me_y = lax.axis_index("py")
    right_x, left_x = lax.rem(me_x + 1, npx), lax.rem(me_x + npx - 1, npx)
    right_y, left_y = lax.rem(me_y + 1, npy), lax.rem(me_y + npy - 1, npy)
    first_x, last_x = me_x == 0, me_x == npx - 1
    first_y, last_y = me_y == 0, me_y == npy - 1
    top = 8 + nyl
    wide = nyl + 16

    def run(first, last, action):
        def body(r, carry):
            action(r)
            return carry

        lax.fori_loop(first, last, body, 0)

    def remote(src, dst, send, recv, target):
        return pltpu.make_async_remote_copy(
            src_ref=src, dst_ref=dst, send_sem=send, recv_sem=recv, device_id=target, device_id_type=MESH
        )

    def at_x(r):
        return (lax.rem(me_x + r, npx), me_y)

    def at_y(r):
        return (me_x, lax.rem(me_y + r, npy))

    loads = []
    for c in range(3):
        for h in range(halves):
            loads.append(
                pltpu.make_async_copy(
                    v_hbm.at[c, :, :, pl.ds(h * HALF, HALF)],
                    vp.at[c, h, pl.ds(1, nxl), pl.ds(8, nyl), :],
                    load_sem.at[c * halves + h],
                )
            )
    base = 3 * halves
    load_u = pltpu.make_async_copy(u_hbm, ub, load_sem.at[base])
    load_s = pltpu.make_async_copy(s_hbm, sb, load_sem.at[base + 1])
    load_m = pltpu.make_async_copy(m_hbm, mk, load_sem.at[base + 2])
    load_t = [
        pltpu.make_async_copy(a, b, load_sem.at[base + 3 + n])
        for n, (a, b) in enumerate(((tz_hbm, tz), (tx_hbm, tx), (tt_hbm, tt)))
    ]
    for copy in loads:
        copy.start()
    load_u.start()
    load_s.start()
    load_m.start()
    for copy in load_t:
        copy.start()

    barrier = pltpu.get_barrier_semaphore()
    run(1, npx, lambda r: pl.semaphore_signal(barrier, inc=1, device_id=at_x(r), device_id_type=MESH))
    run(1, npy, lambda r: pl.semaphore_signal(barrier, inc=1, device_id=at_y(r), device_id_type=MESH))

    count = owner_row.shape[1]
    owners = owner_row[...]
    same = owner_col[...] == owners
    earlier = lax.broadcasted_iota(jnp.int32, (count, count), 0) < lax.broadcasted_iota(
        jnp.int32, (count, count), 1
    )
    rank = jnp.sum(jnp.where(same & earlier, 1, 0), axis=0, keepdims=True)
    owner_x = owners // npy
    place = owner_x * group + rank * npy + (owners - owner_x * npy)
    match = lax.broadcasted_iota(jnp.int32, (places, count), 0) == place
    pick[...] = jnp.sum(jnp.where(match, column_row[...] + 1, 0), axis=1, keepdims=True) - 1
    slots = jnp.broadcast_to((slot_row[...] + 1).astype(F32), (8, count)).astype(BF16)
    requests = (
        lax.dot_general(
            slots, match.astype(F32).astype(BF16), (((1,), (1,)), ((), ())), preferred_element_type=F32
        )
        - 1.0
    )

    def pad_lanes(row):
        if row.shape[1] >= HALF:
            return row
        return jnp.concatenate([row, jnp.zeros((8, HALF - row.shape[1]), F32)], axis=1)

    def by_px(row, ref):
        row = pad_lanes(row)
        lanes = row.shape[1]
        for p in range(npx):
            ref[p] = pltpu.roll(row, (lanes - group * p) % lanes, 1)[:, :HALF]

    def by_py(rows, ref):
        for j in range(npy):
            ref[j] = pltpu.roll(rows, (HALF - j) % HALF, 1)

    by_px(requests, ask)
    seen = ids[...].T
    for x in range(nxl):
        idb[x] = jnp.broadcast_to(seen[:, x:x + 1], (nyl, HALF))

    def row_at(ref, lead, y):
        lines = ref.reshape(*ref.shape[:-3], (nxl + 2) * wide, HALF)
        return lines.at[(*lead, pl.ds(wide + y, nxl, stride=wide), slice(None))]

    def x_pair(field, at, number):
        return (
            remote(at(field, nxl), at(field, 0), x_send.at[number], x_recv.at[number], (right_x, me_y)),
            remote(at(field, 1), at(field, nxl + 1), x_send.at[number + 1], x_recv.at[number + 1], (left_x, me_y)),
        )

    def at_plane(field, x):
        return field.at[:, :, x, pl.ds(8, nyl), :]

    def y_pair(send, recv, number):
        return (
            remote(send.at[0], recv.at[0], y_send.at[number], y_recv.at[number], (me_x, right_y)),
            remote(send.at[1], recv.at[1], y_send.at[number + 1], y_recv.at[number + 1], (me_x, left_y)),
        )

    for copy in loads:
        copy.wait()
    pl.semaphore_wait(barrier, npx - 1 + npy - 1)

    def pack(field, first):
        for c in range(3):
            for h in range(halves):
                snd_y[0, first + c, h] = row_at(field, (c, h), top - 1)[...].astype(BF16)
                snd_y[1, first + c, h] = row_at(field, (c, h), 8)[...].astype(BF16)

    halo_vx = x_pair(vp, at_plane, 0)
    for copy in halo_vx:
        copy.start()

    def ask_x(r):
        return remote(ask.at[at_x(r)[0]], asked.at[me_x], r_send.at[r], r_recv.at[r], at_x(r))

    def ask_y(r):
        n = npx + r
        return remote(asks.at[at_y(r)[1]], wanted.at[me_y], r_send.at[n], r_recv.at[n], at_y(r))

    def reply_y(r):
        n = npx + npy + r
        return remote(reply.at[at_y(r)[1]], replies.at[me_y], r_send.at[n], r_recv.at[n], at_y(r))

    def reply_x(r):
        n = npx + 2 * npy + r
        return remote(fetch.at[at_x(r)[0]], fetched.at[me_x], r_send.at[n], r_recv.at[n], at_x(r))

    def give_x(r):
        n = 2 * npx + 2 * npy + r
        return remote(give.at[at_x(r)[0]], given.at[me_x], r_send.at[n], r_recv.at[n], at_x(r))

    def give_y(r):
        n = 3 * npx + 2 * npy + r
        return remote(gives.at[at_y(r)[1]], taken.at[me_y], r_send.at[n], r_recv.at[n], at_y(r))

    run(1, npx, lambda r: ask_x(r).start())
    asked[me_x] = ask[me_x]
    pack(vp, 0)
    load_u.wait()

    def widen(i, carry):
        for a in range(3):
            pair = ub[a, pl.ds(pl.multiple_of(i * 2 * nyl, 2 * nyl), 2 * nyl), :].astype(F32)
            for s in range(2):
                for h in range(halves):
                    up[a, h, 1 + 2 * i + s, 8:top, :] = pair[s * nyl:(s + 1) * nyl, h * HALF:(h + 1) * HALF]
        return carry

    lax.fori_loop(0, nxl // 2, widen, 0)
    pack(up, 3)
    halo = y_pair(snd_y, rcv_y, 0) + x_pair(up, at_plane, 2)
    for copy in halo:
        copy.start()

    run(1, npx, lambda r: ask_x(r).wait())
    by_py(asked[:, 0, :], asks)
    run(1, npy, lambda r: ask_y(r).start())
    wanted[me_y] = asks[me_y]

    def reduce_cell(c, g, right):
        inv = 1.0 / (c + right + g)
        return inv, c * inv

    mine = lam_z[pl.ds(pl.multiple_of(me_x * kzl, kzl), kzl), 0:1]
    mu = lam_x[...] + mine
    owned = lam_z[pl.ds(me_x * kzl + me_y * kown, kown), 0:1]
    muo = lam_x[...] + owned

    def owner_table():
        def owner_cell(i, carry):
            c, g, ground = carry
            inv, k = reduce_cell(c, g, 1.0)
            return k, muo + g * inv, ground + k * g

        one = jnp.ones_like(muo)
        c, g, ground = lax.fori_loop(1, nyl - 1, owner_cell, (one, muo, jnp.zeros_like(one)))
        inv, link = reduce_cell(c, g, 1.0)
        from_left = g * inv
        end_ground = muo + from_left + (ground + c * (g / (c + g)))
        ground = ground + link * g
        held = muo + ground
        for b in range(npy - 1):
            inv = 1.0 / (link + held)
            phi = link * inv
            owner_inv[b] = inv
            owner_phi[b] = phi
            nxt = end_ground if b == npy - 2 else muo + ground + from_left
            held = nxt + phi * held
        positive = held > 0.0
        owner_inv[npy - 1] = jnp.where(positive, 1.0 / jnp.where(positive, held, 1.0), 0.0)

    owner_table()
    run(1, npy, lambda r: ask_y(r).wait())

    slot_lane = lax.broadcasted_iota(jnp.int32, (npx, HALF), 1).astype(F32)

    def choose(j, carry):
        label = wanted[j]
        for r in range(2):
            hit = jnp.broadcast_to(label[:, r * npy:r * npy + 1], (npx, HALF)) == slot_lane
            chosen[pl.ds(pl.multiple_of((2 * j + r) * npx, npx), npx), :] = hit.astype(F32).astype(BF16)
        return carry

    lax.fori_loop(0, npy, choose, 0)
    controls = basis.shape[0]
    wide_basis = jnp.concatenate([basis[...], jnp.zeros((HALF - controls, SEG), F32)], axis=0)
    rows = sum(
        jnp.dot(chosen[...], part, preferred_element_type=F32) for part in reversed(split(wide_basis, 3))
    )
    for j in range(npy):
        reply[j] = rows[j * 2 * npx:(j + 1) * 2 * npx]
    run(1, npy, lambda r: reply_y(r).start())
    replies[me_y] = reply[me_y]

    load_s.wait()
    load_m.wait()
    for copy in halo_vx + halo:
        copy.wait()

    for c in range(3):
        for h in range(halves):
            for field, first in ((vp, 0), (up, 3)):
                low, high = rcv_y[0, first + c, h].astype(F32), rcv_y[1, first + c, h].astype(F32)
                row_at(field, (c, h), 7)[...] = jnp.where(first_y, 0.0, low)
                row_at(field, (c, h), top)[...] = jnp.where(last_y, 0.0, high)
    edge = jnp.zeros((nyl, HALF), F32)

    @pl.when(first_x)
    def _():
        for c in range(3):
            for h in range(halves):
                vp[c, h, 0, 8:top, :] = edge
                up[c, h, 0, 8:top, :] = edge

    @pl.when(last_x)
    def _():
        for c in range(3):
            for h in range(halves):
                vp[c, h, nxl + 1, 8:top, :] = edge
                up[c, h, nxl + 1, 8:top, :] = edge

    def tall_rows(field, c, x, y):
        return jnp.concatenate([field[c, h, x, y:y + 24, :] for h in range(halves)], axis=1)

    def tile_rows(field, c, x, y):
        return jnp.concatenate([field[c, h, x, y + 8:y + 16, :] for h in range(halves)], axis=1)

    tiles = nyl // 8

    def predict(i, carry):
        for k in range(tiles):
            rows = pl.ds(pl.multiple_of(i * 2 * nyl + 16 * k, 16), 16)
            forcing = [sb[b, rows, :].astype(F32) for b in range(3)]
            for s in range(2):
                n = 2 * k + s
                x = 2 * i + n // tiles
                y = 8 * (n % tiles)
                scale = 1.0 / (1.0 + (DT * ALPHA) * mk[x, y:y + 8, :].astype(F32))
                u, v, tall_v = [], [], []
                slopes = [None] * 3
                for a in range(3):
                    tall = tall_rows(up, a, x + 1, y)
                    tall_v.append(tall_rows(vp, a, x + 1, y))
                    u.append(tall[8:16])
                    v.append(tall_v[a][8:16])
                    below, above = z_shift(u[a], 0.0, 0.0)
                    diffs = (
                        tile_rows(up, a, x + 2, y) - tile_rows(up, a, x, y),
                        tall[9:17] - tall[7:15],
                        above - below,
                    )
                    for b in range(3):
                        term = v[a] * diffs[b]
                        slopes[b] = term if slopes[b] is None else slopes[b] + term
                for b in range(3):
                    tall = tall_v[b]
                    xm, xp = tile_rows(vp, b, x, y), tile_rows(vp, b, x + 2, y)
                    ym, yp = tall[7:15], tall[9:17]
                    zm, zp = z_shift(v[b], 0.0, 0.0)
                    convect = u[0] * (xp - xm) + u[1] * (yp - ym) + u[2] * (zp - zm)
                    lap = (xp + xm) + (yp + ym) + (zp + zm) - 6.0 * v[b]
                    change = 0.5 * (convect - slopes[b]) + NU * lap + forcing[b][8 * s:8 * s + 8]
                    w = (v[b] + DT * change) * scale
                    for h in range(halves):
                        part = w[:, h * HALF:(h + 1) * HALF]
                        if b == 0:
                            w0[h, x + 1, y:y + 8, :] = part
                        elif b == 1:
                            w1[h, x + 1, y + 8:y + 16, :] = part
                        else:
                            w2[h, x, y:y + 8, :] = part
        return carry

    lax.fori_loop(0, nxl // 2, predict, 0)

    for h in range(halves):
        wy_snd[0, h] = row_at(w1, (h,), top - 1)[...]
        wy_snd[1, h] = row_at(w1, (h,), 8)[...]
    halo = y_pair(wy_snd, wy_rcv, 2) + x_pair(w0, lambda field, x: field.at[:, x], 4)
    for copy in halo:
        copy.start()

    lane = lax.broadcasted_iota(jnp.int32, (nyl, HALF), 1)

    def flux_plane(x, carry):
        face = jnp.where(lane == HALF - 1, w2[halves - 1, x], 0.0)
        which = idb[x]
        return tuple(total + jnp.where(which == k, face, 0.0) for k, total in enumerate(carry))

    zero = jnp.zeros((nyl, HALF), F32)
    totals = lax.fori_loop(0, nxl, flux_plane, (zero,) * OUTLETS)
    fsum[0] = jnp.concatenate([jnp.sum(t, axis=0, keepdims=True) for t in totals], axis=0)

    def flux_x(r):
        return remote(fsum.at[0], fr1.at[me_x], f_send.at[r], f_recv.at[r], at_x(r))

    def flux_y(r):
        return remote(fsum.at[1], fr2.at[me_y], f_send.at[npx + r], f_recv.at[npx + r], at_y(r))

    run(1, npx, lambda r: flux_x(r).start())
    fr1[me_x] = fsum[0]

    for copy in halo:
        copy.wait()
    for h in range(halves):
        row_at(w1, (h,), 7)[...] = jnp.where(first_y, 0.0, wy_rcv[0, h])
        row_at(w1, (h,), top)[...] = jnp.where(last_y, 0.0, wy_rcv[1, h])

    @pl.when(first_x)
    def _():
        for h in range(halves):
            w0[h, 0] = edge

    @pl.when(last_x)
    def _():
        for h in range(halves):
            w0[h, nxl + 1] = edge

    def diverge(x, carry):
        deep = jnp.concatenate([w2[h, x] for h in range(halves)], axis=1)
        below, above = z_shift(deep, 0.0, 0.0)
        for h in range(halves):
            cut = slice(h * HALF, (h + 1) * HALF)
            tall = w1[h, x + 1]
            total = (w0[h, x + 2] - w0[h, x]) + (tall[9:top + 1] - tall[7:top - 1]) + (above - below)[:, cut]
            div[h, pl.ds(x, nyl, stride=nxl), :] = 0.5 * total
        return carry

    lax.fori_loop(0, nxl // 2, diverge, 0)
    run(1, npx, lambda r: flux_x(r).wait())
    fsum[1] = jnp.sum(fr1[...], axis=0)
    run(1, npy, lambda r: flux_y(r).start())
    fr2[me_y] = fsum[1]
    lax.fori_loop(nxl // 2, nxl, diverge, 0)

    run(1, npy, lambda r: reply_y(r).wait())
    lines = replies.reshape(npy * 2 * npx, SEG)
    for p in range(npx):
        for r in range(2):
            fetch[p, r * npy:(r + 1) * npy, :] = lines[pl.ds(r * npx + p, npy, stride=2 * npx), :]

    run(1, npy, lambda r: flux_y(r).wait())
    flux = jnp.sum(fr2[...], axis=0) * (1.0 / (nx * npy * nyl))
    press = []
    for k in range(OUTLETS):
        total = resist[k, 0] * flux[0:1]
        for n in range(1, OUTLETS):
            total = total + resist[k, n] * flux[n:n + 1]
        press.append(jnp.broadcast_to(total, (nyl, HALF)))

    def lower(x, carry):
        which = idb[x]
        drop = jnp.zeros((nyl, HALF), F32)
        for k in range(OUTLETS):
            drop = jnp.where(which == k, press[k], drop)
        drop = DT * jnp.where(lane == HALF - 1, drop, 0.0)
        w2[halves - 1, x] = w2[halves - 1, x] - drop
        here = pl.ds(x, nyl, stride=nxl)
        div[halves - 1, here, :] = div[halves - 1, here, :] - 0.5 * pltpu.roll(drop, HALF - 1, 1)
        return carry

    lax.fori_loop(0, nxl, lower, 0)

    for copy in load_t:
        copy.wait()

    def forth(c, r):
        p = at_x(r)[0]
        n = c * npx + r
        return remote(msg.at[p, c], got.at[me_x, c], a_send.at[n], a_recv.at[n], at_x(r))

    def depth_piece(c, carry):
        here = pl.ds(pl.multiple_of(c * 256, 256), 256)
        value = jnp.concatenate([div[h, here, :] for h in range(halves)], axis=1)
        out = dot_parts((tz[0], tz[1]), split(value, 2), ((1,), (1,)))
        for p in range(npx):
            msg[p, c] = out[p * kzl:(p + 1) * kzl]
        run(1, npx, lambda r: forth(c, r).start())
        return carry

    lax.fori_loop(0, pieces, depth_piece, 0)
    run(1, npx, lambda r: reply_x(r).start())
    fetched[me_x] = fetch[me_x]

    def table_cell(i, carry):
        c, g = carry
        right = jnp.where((i == nyl - 1) & last_y, 0.0, 1.0)
        inv, k = reduce_cell(c, g, right)
        tau[i] = inv
        kap[i] = k
        return k, mu + g * inv

    tau[0] = jnp.zeros_like(mu)
    kap[0] = jnp.ones_like(mu)
    lax.fori_loop(1, nyl, table_cell, (jnp.ones_like(mu), mu))

    wides = npx // 4

    def row_of(i):
        return pl.ds(pl.multiple_of(i * kzl, kzl), kzl)

    def piece_rows(c):
        return pl.ds(pl.multiple_of(c * per * kzl, per * kzl), per * kzl)

    def line_piece(c, carry):
        got[me_x, c] = msg[me_x, c]
        run(1, npx, lambda r: forth(c, r).wait())

        def gather(sg, inner):
            for half in range(per // 4):
                out = swap_groups([got[4 * sg + a, c, :, half * HALF:(half + 1) * HALF] for a in range(4)])
                for b in range(4):
                    y = c * per + 4 * half + b
                    cols[row_of(y), pl.ds(pl.multiple_of(sg * HALF, HALF), HALF)] = out[b]
            return inner

        lax.fori_loop(0, wides, gather, 0)
        rows = piece_rows(c)
        cols[rows, :] = dot_parts(split(cols[rows, :], 2), (tt[0], tt[1]), ((1,), (0,)))
        return carry

    lax.fori_loop(0, pieces, line_piece, 0)

    def down(i, carry):
        r, ends = carry
        ends = ends + kap[i] * r
        nxt = cols[row_of(i + 1), :] + tau[i] * r
        cols[row_of(i + 1), :] = nxt
        return nxt, ends

    r, ends = lax.fori_loop(1, nyl - 1, down, (cols[row_of(1), :], cols[row_of(0), :]))
    ends = ends + kap[nyl - 1] * r
    over = tau[nyl - 1] * r
    for j in range(npy):
        isnd[j, 0:kown, :] = ends[j * kown:(j + 1) * kown]
        isnd[j, kown:2 * kown, :] = over[j * kown:(j + 1) * kown]

    def collect(r):
        return remote(isnd.at[at_y(r)[1]], ircv.at[me_y], i_send.at[r], i_recv.at[r], at_y(r))

    run(1, npy, lambda r: collect(r).start())
    ircv[me_y] = isnd[me_y]
    run(1, npy, lambda r: collect(r).wait())

    rho = []
    for b in range(npy):
        value = ircv[b, 0:kown, :]
        if b > 0:
            value = value + ircv[b - 1, kown:2 * kown, :]
        rho.append(value)
    depth_mode = lax.broadcasted_iota(jnp.int32, (kown, nx), 0) + me_x * kzl + me_y * kown
    row_mode = lax.broadcasted_iota(jnp.int32, (kown, nx), 1)
    mean = sum(rho[1:], rho[0]) * (1.0 / (npy * nyl))
    mean = jnp.where((depth_mode == 0) & (row_mode == 0), mean, 0.0)
    half_sum = (nyl - 1) / 2.0
    for b in range(npy):
        weight = 1.0 + (0.0 if b == 0 else half_sum) + (2.0 * half_sum if b == npy - 1 else half_sum)
        rho[b] = rho[b] - weight * mean
    for b in range(npy - 1):
        rho[b + 1] = rho[b + 1] + owner_phi[b] * rho[b]
    value = -owner_inv[npy - 1] * rho[npy - 1]
    jsnd[npy - 1, 0:kown, :] = value
    jsnd[npy - 1, kown:2 * kown, :] = jnp.zeros_like(value)
    jsnd[npy - 1, 2 * kown:3 * kown, :] = mean
    for b in range(npy - 2, -1, -1):
        jsnd[b, kown:2 * kown, :] = value
        value = owner_phi[b] * value - owner_inv[b] * rho[b]
        jsnd[b, 0:kown, :] = value
        jsnd[b, 2 * kown:3 * kown, :] = mean

    def hand_back(r):
        n = npy + r
        return remote(jsnd.at[at_y(r)[1]], jrcv.at[me_y], i_send.at[n], i_recv.at[n], at_y(r))

    run(1, npy, lambda r: hand_back(r).start())
    jrcv[me_y] = jsnd[me_y]
    run(1, npy, lambda r: hand_back(r).wait())
    for j in range(npy):
        for part in range(3):
            back[part, j * kown:(j + 1) * kown, :] = jrcv[j, part * kown:(part + 1) * kown, :]
    first_value, mean_rows = back[0], back[2]

    def home(c, r):
        p = at_x(r)[0]
        n = (pieces + c) * npx + r
        return remote(msg.at[p, c], got2.at[me_x, c], a_send.at[n], a_recv.at[n], at_x(r))

    def up_piece(n, q):
        c = pieces - 1 - n

        def up_again(m, q):
            i = c * per + per - 1 - m
            share = 0.5 * (i + 1).astype(F32)
            q = tau[i] * (q - cols[row_of(i), :] + mean_rows * share) + kap[i] * first_value
            cols[row_of(i), :] = q
            return q

        q = lax.fori_loop(0, per, up_again, q)
        rows = piece_rows(c)
        cols[rows, :] = dot_parts(split(cols[rows, :], 3), (tx[0], tx[1], tx[2]), ((1,), (0,)))

        def scatter(sg, inner):
            for half in range(per // 4):
                parts = []
                for b in range(4):
                    y = c * per + 4 * half + b
                    parts.append(cols[row_of(y), pl.ds(pl.multiple_of(sg * HALF, HALF), HALF)])
                out = swap_groups(parts)
                for a in range(4):
                    msg[4 * sg + a, c, :, half * HALF:(half + 1) * HALF] = out[a]
            return inner

        lax.fori_loop(0, wides, scatter, 0)
        run(1, npx, lambda r: home(c, r).start())
        return q

    lax.fori_loop(0, pieces, up_piece, back[1])

    pressure = qp.reshape(halves, (nxl + 2) * wide, HALF)

    def rise_piece(n, carry):
        c = pieces - 1 - n
        got2[me_x, c] = msg[me_x, c]
        run(1, npx, lambda r: home(c, r).wait())
        value = got2[:, c].reshape(nz, 256)
        out = dot_parts(split(value.T, 3), (tz[0], tz[1], tz[2]), ((1,), (0,)))
        for y in range(per):
            for h in range(halves):
                pressure[h, pl.ds(wide + 8 + c * per + y, nxl, stride=wide), :] = out[
                    y * nxl:(y + 1) * nxl, h * HALF:(h + 1) * HALF
                ]
        return carry

    lax.fori_loop(0, pieces, rise_piece, 0)

    for h in range(halves):
        qy_snd[0, h] = row_at(qp, (h,), top - 1)[...]
        qy_snd[1, h] = row_at(qp, (h,), 8)[...]
    halo = y_pair(qy_snd, qy_rcv, 4) + x_pair(qp, lambda field, x: field.at[:, x, pl.ds(8, nyl), :], 6)
    for copy in halo:
        copy.start()

    def q_rows(x, y, size):
        return jnp.concatenate([qp[h, x, y:y + size, :] for h in range(halves)], axis=1)

    def join(field, x):
        return jnp.concatenate([field[h, x, 0:nyl, :] for h in range(halves)], axis=1)

    def correct_depth(x, carry):
        center = q_rows(x + 1, 8, nyl)
        spot = lax.broadcasted_iota(jnp.int32, center.shape, 1)
        below = jnp.where(spot == 0, center, pltpu.roll(center, 1, 1))
        above = jnp.where(spot == nz - 1, center, pltpu.roll(center, nz - 1, 1))
        vel[2, x] = join(w2, x) - 0.5 * (above - below)
        return carry

    lax.fori_loop(0, nxl, correct_depth, 0)
    outs = [pltpu.make_async_copy(vel.at[b], v_out.at[b], out_sem.at[b]) for b in range(3)]
    outs[2].start()

    for copy in halo:
        copy.wait()
    for h in range(halves):
        row_at(qp, (h,), 7)[...] = jnp.where(first_y, qy_snd[1, h], qy_rcv[0, h])
        row_at(qp, (h,), top)[...] = jnp.where(last_y, qy_snd[0, h], qy_rcv[1, h])

    @pl.when(first_x)
    def _():
        for h in range(halves):
            qp[h, 0, 8:top, :] = qp[h, 1, 8:top, :]

    @pl.when(last_x)
    def _():
        for h in range(halves):
            qp[h, nxl + 1, 8:top, :] = qp[h, nxl, 8:top, :]

    def correct(x, carry):
        tall = q_rows(x + 1, 0, wide)
        v0 = join(w0, x + 1) - 0.5 * (q_rows(x + 2, 8, nyl) - q_rows(x, 8, nyl))
        deep = jnp.concatenate([w1[h, x + 1, 8:top, :] for h in range(halves)], axis=1)
        v1 = deep - 0.5 * (tall[9:top + 1] - tall[7:top - 1])
        vel[0, x] = v0
        vel[1, x] = v1
        u = [jnp.concatenate([up[a, h, x + 1, 8:top, :] for h in range(halves)], axis=1) for a in range(3)]
        total = -ALPHA * (u[0] * v0 + u[1] * v1 + u[2] * vel[2, x])
        for h in range(halves):
            sig[h, pl.ds(pl.multiple_of(x * nyl, 8), nyl), :] = total[:, h * HALF:(h + 1) * HALF]
        return carry

    lax.fori_loop(0, nxl, correct, 0)
    outs[0].start()
    outs[1].start()

    shape = (places, cells)
    cell = lax.broadcasted_iota(jnp.int32, shape, 1) * halves
    picked = None
    for h in range(halves):
        hot = (jnp.broadcast_to(pick[...], shape) == cell + h).astype(F32).astype(BF16)
        for part in reversed(split(sig[h], 3)):
            term = jnp.dot(hot, part, preferred_element_type=F32)
            picked = term if picked is None else picked + term
    run(1, npx, lambda r: reply_x(r).wait())
    products = picked * fetched[...].reshape(places, SEG)
    ones = jnp.ones((8, SEG), BF16)
    totals = sum(
        lax.dot_general(ones, part, (((1,), (1,)), ((), ())), preferred_element_type=F32)
        for part in reversed(split(products, 3))
    )
    by_px(totals, give)
    run(1, npx, lambda r: give_x(r).start())
    given[me_x] = give[me_x]
    run(1, npx, lambda r: give_x(r).wait())
    by_py(given[:, 0, :], gives)
    run(1, npy, lambda r: give_y(r).start())
    taken[me_y] = gives[me_y]
    run(1, npy, lambda r: give_y(r).wait())

    def add_up(j, total):
        label, value = wanted[j], taken[j]
        for r in range(2):
            spot = slice(r * npy, r * npy + 1)
            hit = jnp.broadcast_to(label[:, spot], (npx, HALF)) == slot_lane
            total = total + jnp.where(hit, jnp.broadcast_to(value[:, spot], (npx, HALF)), 0.0)
        return total

    total = lax.fori_loop(0, npy, add_up, jnp.zeros((npx, HALF), F32))
    grad_out[...] = jnp.sum(total, axis=0, keepdims=True)[:, :controls]
    for copy in outs:
        copy.wait()


def main_call(dims, args, owner_rows):
    npx, npy, nxl, nyl, nz = dims
    nx = npx * nxl
    kzl = nz // npx
    kown = kzl // npy
    halves = nz // HALF
    wide = nyl + 16
    cells = nxl * nyl
    pieces = cells // 256
    places = 2 * npx * npy
    vmem = pltpu.VMEM
    anywhere = pl.BlockSpec(memory_space=pl.ANY)
    here = pl.BlockSpec(memory_space=pltpu.VMEM)
    scalar = pl.BlockSpec(memory_space=pltpu.SMEM)
    dma = pltpu.SemaphoreType.DMA
    tables = args[11:14]
    field = vmem((3, halves, nxl + 2, wide, HALF), F32)
    line = vmem((nyl, kzl, nx), F32)
    message = vmem((npx, pieces, kzl, 256), F32)
    scratch = [
        field,
        field,
        vmem((3, cells, nz), BF16),
        vmem((3, cells, nz), BF16),
        vmem((nxl, nyl, nz), jnp.int32),
        vmem((nxl, nyl, HALF), jnp.int32),
        vmem((halves, nxl + 2, nyl, HALF), F32),
        vmem((halves, nxl + 2, wide, HALF), F32),
        vmem((halves, nxl, nyl, HALF), F32),
        vmem((2, 6, halves, nxl, HALF), BF16),
        vmem((2, 6, halves, nxl, HALF), BF16),
        vmem((2, halves, nxl, HALF), F32),
        vmem((2, halves, nxl, HALF), F32),
        vmem((2, OUTLETS, HALF), F32),
        vmem((npx, OUTLETS, HALF), F32),
        vmem((npy, OUTLETS, HALF), F32),
        vmem((halves, cells, HALF), F32),
        message,
        message,
        message,
        vmem((nyl * kzl, nx), F32),
        line,
        line,
        vmem((npy, kown, nx), F32),
        vmem((npy, kown, nx), F32),
        vmem((npy, 2 * kown, nx), F32),
        vmem((npy, 2 * kown, nx), F32),
        vmem((npy, 3 * kown, nx), F32),
        vmem((npy, 3 * kown, nx), F32),
        vmem((3, kzl, nx), F32),
        vmem((halves, nxl + 2, wide, HALF), F32),
        vmem((2, halves, nxl, HALF), F32),
        vmem((2, halves, nxl, HALF), F32),
        vmem((3, nxl, nyl, nz), F32),
        vmem((halves, cells, HALF), F32),
        vmem((places, 1), jnp.int32),
        vmem((npx, 8, HALF), F32),
        vmem((npx, 8, HALF), F32),
        vmem((npy, npx, HALF), F32),
        vmem((npy, npx, HALF), F32),
        vmem((places, HALF), BF16),
        vmem((npy, 2 * npx, SEG), F32),
        vmem((npy, 2 * npx, SEG), F32),
        vmem((npx, 2 * npy, SEG), F32),
        vmem((npx, 2 * npy, SEG), F32),
        vmem((npx, 8, HALF), F32),
        vmem((npx, 8, HALF), F32),
        vmem((npy, npx, HALF), F32),
        vmem((npy, npx, HALF), F32),
    ]
    scratch += [vmem(t.shape, BF16) for t in tables]
    scratch += [
        dma((3 * halves + 3 + len(tables),)),
        dma((8,)),
        dma((8,)),
        dma((6,)),
        dma((6,)),
        dma((npx + npy,)),
        dma((npx + npy,)),
        dma((2 * pieces * npx,)),
        dma((2 * pieces * npx,)),
        dma((2 * npy,)),
        dma((2 * npy,)),
        dma((3 * (npx + npy),)),
        dma((3 * (npx + npy),)),
        dma((3,)),
    ]
    return pl.pallas_call(
        functools.partial(main_kernel, dims),
        out_shape=(
            jax.ShapeDtypeStruct((3, nxl, nyl, nz), F32),
            jax.ShapeDtypeStruct((1, owner_rows), F32),
        ),
        in_specs=[anywhere] * 4 + [here, scalar] + [here] * 5 + [anywhere] * len(tables) + [here] * 2,
        out_specs=(anywhere, here),
        scratch_shapes=scratch,
        compiler_params=pltpu.CompilerParams(
            collective_id=0, has_side_effects=True, vmem_limit_bytes=58 * 2**20
        ),
        name="project",
    )(*args)


def local(
    base_flow, adjoint_start, source, solid_mask, outlet_ids, resist,
    tile_owner, tile_slot, tile_column, control_basis,
):
    _, nxl, nyl, nz = adjoint_start.shape
    npx, npy = lax.axis_size("px"), lax.axis_size("py")
    nx = npx * nxl
    tz, tx = table_np(nz), table_np(nx)
    tables = [split_np(tz, 3), split_np(tx, 3), split_np(np.ascontiguousarray(tx.T), 2)]
    tables = [jnp.asarray(np.stack(t)) for t in tables]
    lam_x = jnp.asarray(-eigen_np(nx)[None, :])
    lam_z = jnp.asarray(np.repeat(-eigen_np(nz)[:, None], HALF, axis=1))
    args = (
        adjoint_start,
        base_flow.reshape(3, nxl * nyl, nz),
        source.reshape(3, nxl * nyl, nz),
        solid_mask,
        outlet_ids,
        resist,
        tile_owner,
        tile_owner.reshape(1, -1),
        tile_slot.reshape(1, -1),
        tile_column.reshape(1, -1),
        control_basis,
        *tables,
        lam_x,
        lam_z,
    )
    velocity, grad = main_call((npx, npy, nxl, nyl, nz), args, control_basis.shape[0])
    return velocity, grad.reshape(-1)


def solution(mesh):
    in_specs = (
        P(None, "px", "py", None),
        P(None, "px", "py", None),
        P(None, "px", "py", None),
        P("px", "py", None),
        P("px", "py"),
        P(),
        P(("px", "py"), None),
        P(("px", "py")),
        P(("px", "py")),
        P(("px", "py"), None),
    )
    out_specs = (P(None, "px", "py", None), P(("px", "py")))
    return jax.shard_map(local, mesh=mesh, in_specs=in_specs, out_specs=out_specs, check_vma=False)
```

time: 144 us -> 118 us (0.82)
  Pallas kernels: 130 us -> 111 us
  other arithmetic: 3.74 us -> 0 us
  local copies, waits for them, and re-layouts: 8.92 us -> 6.6 us
    pallas_call x2 -> x0, Pallas kernels: 32.4 us -> none  [the longest x1 27.3 us: route_call(): pl.pallas_call(functools.partial(route_kernel, npx, npy), out_shape=(jax....]
    pallas_call x1, Pallas kernels: 97.3 us -> 111 us  [main_call(): pl.pallas_call(functools.partial(main_kernel, dims), out_shape=(jax.Shape...]
    unnamed x14 -> x6, local copies, waits for them, and re-layouts: 3.03 us -> 6.6 us
    add x5 -> x0, other arithmetic: 3.3 us -> none  [the longest x1 1.92 us: local(): muo = lam_x[None, :] + owned[:, None]]
    dynamic_slice x2 -> x0, local copies, waits for them, and re-layouts: 2.02 us -> none  [the longest x1 1.27 us: local(): lax.dynamic_slice(lam_z, (at + lax.axis_index('py') * kown,), (kown,))]
    reshape x1 -> x0, local copies, waits for them, and re-layouts: 1.67 us -> none  [local(): ids = outlet_ids.reshape(nxl, nyl, 1)]
where the time goes in v2:
time: 118 us
  Pallas kernels  111 us (94%)
  local copies, waits for them, and re-layouts  6.6 us (6%)
    pallas_call x1, Pallas kernels, main_call(): pl.pallas_call(functools.partial(main_kernel, dims), out_shape=(jax.Shape...  111 us
    unnamed x6, local copies, waits for them, and re-layouts  6.6 us

profile of v2, /device:TPU:1, one launch (start us, length us, event | category | flops | bytes accessed | tf_op | source)
XLA Modules:
  0.0 117.9 jit_solution(16489699465192194584)
XLA Ops:
  0.6 1.4 %copy.17.ids = s32[32,24]{1,0:T(8,128)} copy(s32[32,24]{0,1:T(8,128)} %param.19) | data formatting | bytes 6144 | tf_op args[4]
  2.0 1.5 %copy.18.owner_col = s32[256,1]{1,0:T(8,128)} copy(s32[256,1]{0,1:T(1,128)} %param.21) | data formatting | bytes 2048 | tf_op args[6]
  3.5 110.7 %project.1 = (f32[3,32,24,256]{3,2,1,0:T(8,128)}, f32[1,32]{1,0:T(1,128)}) custom-call(f32[3,32,24,256]{3,2,1,0:T(8,128)} %v_hbm.1, bf16[3,768,256]{2,1,0:T(8,128)(2,1)} %bitcast.6, bf16[3,768,256]{2,1,0:T(8,128)(2,1)} %bitcast.7, s32[32,24,256]{2,1,0:T(8,128)} %m_hbm.1, s32[32,24]{1,0:T(8,128)} %copy.17.ids, f32[8,8]{1,0:T(8,128)} %resist.1, ...), custom_call_target="tpu_custom_call" | custom-call | tf_op jit(solution)/shard_map/project/pallas_call | solution.py:867
  114.2 0.0 copy-start
  114.2 3.2 %copy.21 = f32[3,32,24,256]{3,2,1,0:T(8,128)} copy(f32[3,32,24,256]{3,2,1,0:T(8,128)} %get-tuple-element.8) | data formatting | bytes 4718592
  117.4 0.0 copy-done
  117.4 0.5 copy.22
Async XLA Ops:
  114.2 3.2 %copy-start = (f32[1,32]{1,0:T(1,128)S(1)}, f32[1,32]{1,0:T(1,128)}, u32[]{:S(2)}) copy-start(f32[1,32]{1,0:T(1,128)} %get-tuple-element.5) | copy-start | bytes 388

commit v3 on v2

--- a/solution.py
+++ b/solution.py
@@ -89,13 +89,13 @@
 
 def main_kernel(
     dims,
-    v_hbm, u_hbm, s_hbm, m_hbm, ids, resist, owner_col, owner_row, slot_row, column_row, basis,
+    v_hbm, u_hbm, s_hbm, m_hbm, ids, resist, owner_row, slot_row, column_row, basis,
     tz_hbm, tx_hbm, tt_hbm, lam_x, lam_z,
     v_out, grad_out,
     vp, up, ub, sb, mk, idb, w0, w1, w2, snd_y, rcv_y, wy_snd, wy_rcv, fsum, fr1, fr2,
     div, msg, got, got2, cols, tau, kap, owner_inv, owner_phi,
     isnd, ircv, jsnd, jrcv, back, qp, qy_snd, qy_rcv, vel, sig,
-    pick, ask, asked, asks, wanted, chosen, reply, replies, fetch, fetched, give, given, gives, taken,
+    outlet, hot, pick, ask, asked, asks, wanted, chosen, reply, replies, fetch, fetched, give, given, gives, taken,
     tz, tx, tt,
     load_sem, x_send, x_recv, y_send, y_recv, f_send, f_recv, a_send, a_recv, i_send, i_recv, r_send, r_recv, out_sem,
 ):
@@ -135,6 +135,15 @@
 
     def at_y(r):
         return (me_x, lax.rem(me_y + r, npy))
+
+    def spread(count, target, src, dst, send, recv):
+        run(1, count, lambda r: remote(src(r), dst, send, recv, target(r)).start())
+
+    def settle(like, send, recv):
+        pltpu.make_async_copy(like, like, send).wait()
+        pltpu.make_async_copy(like, like, recv).wait()
+
+    others_x, others_y = pl.ds(0, npx - 1), pl.ds(0, npy - 1)
 
     loads = []
     for c in range(3):
@@ -168,7 +177,7 @@
 
     count = owner_row.shape[1]
     owners = owner_row[...]
-    same = owner_col[...] == owners
+    same = jnp.broadcast_to(owners, (8, count)).T[:, 0:1] == owners
     earlier = lax.broadcasted_iota(jnp.int32, (count, count), 0) < lax.broadcasted_iota(
         jnp.int32, (count, count), 1
     )
@@ -194,14 +203,17 @@
         row = pad_lanes(row)
         lanes = row.shape[1]
         for p in range(npx):
-            ref[p] = pltpu.roll(row, (lanes - group * p) % lanes, 1)[:, :HALF]
+            ref[p, 0:8, :] = pltpu.roll(row, (lanes - group * p) % lanes, 1)[:, :HALF]
 
     def by_py(rows, ref):
         for j in range(npy):
             ref[j] = pltpu.roll(rows, (HALF - j) % HALF, 1)
 
     by_px(requests, ask)
-    seen = ids[...].T
+    seen = ids[...]
+    padded = jnp.concatenate([seen.astype(F32), jnp.zeros((nyl, HALF - nxl), F32)], axis=1)
+    for p in range(npx):
+        ask[p, 8:top, :] = padded
     for x in range(nxl):
         idb[x] = jnp.broadcast_to(seen[:, x:x + 1], (nyl, HALF))
 
@@ -238,31 +250,11 @@
     for copy in halo_vx:
         copy.start()
 
-    def ask_x(r):
-        return remote(ask.at[at_x(r)[0]], asked.at[me_x], r_send.at[r], r_recv.at[r], at_x(r))
-
-    def ask_y(r):
-        n = npx + r
-        return remote(asks.at[at_y(r)[1]], wanted.at[me_y], r_send.at[n], r_recv.at[n], at_y(r))
-
-    def reply_y(r):
-        n = npx + npy + r
-        return remote(reply.at[at_y(r)[1]], replies.at[me_y], r_send.at[n], r_recv.at[n], at_y(r))
-
-    def reply_x(r):
-        n = npx + 2 * npy + r
-        return remote(fetch.at[at_x(r)[0]], fetched.at[me_x], r_send.at[n], r_recv.at[n], at_x(r))
-
-    def give_x(r):
-        n = 2 * npx + 2 * npy + r
-        return remote(give.at[at_x(r)[0]], given.at[me_x], r_send.at[n], r_recv.at[n], at_x(r))
-
-    def give_y(r):
-        n = 3 * npx + 2 * npy + r
-        return remote(gives.at[at_y(r)[1]], taken.at[me_y], r_send.at[n], r_recv.at[n], at_y(r))
-
-    run(1, npx, lambda r: ask_x(r).start())
-    asked[me_x] = ask[me_x]
+    def ask_start():
+        spread(npx, at_x, lambda r: ask.at[at_x(r)[0]], asked.at[me_x], r_send.at[0], r_recv.at[0])
+        asked[me_x] = ask[me_x]
+
+    ask_start()
     pack(vp, 0)
     load_u.wait()
 
@@ -280,9 +272,9 @@
     for copy in halo:
         copy.start()
 
-    run(1, npx, lambda r: ask_x(r).wait())
+    settle(asked.at[others_x], r_send.at[0], r_recv.at[0])
     by_py(asked[:, 0, :], asks)
-    run(1, npy, lambda r: ask_y(r).start())
+    spread(npy, at_y, lambda r: asks.at[at_y(r)[1]], wanted.at[me_y], r_send.at[1], r_recv.at[1])
     wanted[me_y] = asks[me_y]
 
     def reduce_cell(c, g, right):
@@ -318,7 +310,7 @@
         owner_inv[npy - 1] = jnp.where(positive, 1.0 / jnp.where(positive, held, 1.0), 0.0)
 
     owner_table()
-    run(1, npy, lambda r: ask_y(r).wait())
+    settle(wanted.at[others_y], r_send.at[1], r_recv.at[1])
 
     slot_lane = lax.broadcasted_iota(jnp.int32, (npx, HALF), 1).astype(F32)
 
@@ -337,7 +329,7 @@
     )
     for j in range(npy):
         reply[j] = rows[j * 2 * npx:(j + 1) * 2 * npx]
-    run(1, npy, lambda r: reply_y(r).start())
+    spread(npy, at_y, lambda r: reply.at[at_y(r)[1]], replies.at[me_y], r_send.at[2], r_recv.at[2])
     replies[me_y] = reply[me_y]
 
     load_s.wait()
@@ -439,13 +431,7 @@
     totals = lax.fori_loop(0, nxl, flux_plane, (zero,) * OUTLETS)
     fsum[0] = jnp.concatenate([jnp.sum(t, axis=0, keepdims=True) for t in totals], axis=0)
 
-    def flux_x(r):
-        return remote(fsum.at[0], fr1.at[me_x], f_send.at[r], f_recv.at[r], at_x(r))
-
-    def flux_y(r):
-        return remote(fsum.at[1], fr2.at[me_y], f_send.at[npx + r], f_recv.at[npx + r], at_y(r))
-
-    run(1, npx, lambda r: flux_x(r).start())
+    spread(npx, at_x, lambda r: fsum.at[0], fr1.at[me_x], f_send.at[0], f_recv.at[0])
     fr1[me_x] = fsum[0]
 
     for copy in halo:
@@ -474,48 +460,10 @@
             div[h, pl.ds(x, nyl, stride=nxl), :] = 0.5 * total
         return carry
 
-    lax.fori_loop(0, nxl // 2, diverge, 0)
-    run(1, npx, lambda r: flux_x(r).wait())
-    fsum[1] = jnp.sum(fr1[...], axis=0)
-    run(1, npy, lambda r: flux_y(r).start())
-    fr2[me_y] = fsum[1]
-    lax.fori_loop(nxl // 2, nxl, diverge, 0)
-
-    run(1, npy, lambda r: reply_y(r).wait())
-    lines = replies.reshape(npy * 2 * npx, SEG)
-    for p in range(npx):
-        for r in range(2):
-            fetch[p, r * npy:(r + 1) * npy, :] = lines[pl.ds(r * npx + p, npy, stride=2 * npx), :]
-
-    run(1, npy, lambda r: flux_y(r).wait())
-    flux = jnp.sum(fr2[...], axis=0) * (1.0 / (nx * npy * nyl))
-    press = []
-    for k in range(OUTLETS):
-        total = resist[k, 0] * flux[0:1]
-        for n in range(1, OUTLETS):
-            total = total + resist[k, n] * flux[n:n + 1]
-        press.append(jnp.broadcast_to(total, (nyl, HALF)))
-
-    def lower(x, carry):
-        which = idb[x]
-        drop = jnp.zeros((nyl, HALF), F32)
-        for k in range(OUTLETS):
-            drop = jnp.where(which == k, press[k], drop)
-        drop = DT * jnp.where(lane == HALF - 1, drop, 0.0)
-        w2[halves - 1, x] = w2[halves - 1, x] - drop
-        here = pl.ds(x, nyl, stride=nxl)
-        div[halves - 1, here, :] = div[halves - 1, here, :] - 0.5 * pltpu.roll(drop, HALF - 1, 1)
-        return carry
-
-    lax.fori_loop(0, nxl, lower, 0)
+    lax.fori_loop(0, nxl, diverge, 0)
 
     for copy in load_t:
         copy.wait()
-
-    def forth(c, r):
-        p = at_x(r)[0]
-        n = c * npx + r
-        return remote(msg.at[p, c], got.at[me_x, c], a_send.at[n], a_recv.at[n], at_x(r))
 
     def depth_piece(c, carry):
         here = pl.ds(pl.multiple_of(c * 256, 256), 256)
@@ -523,11 +471,21 @@
         out = dot_parts((tz[0], tz[1]), split(value, 2), ((1,), (1,)))
         for p in range(npx):
             msg[p, c] = out[p * kzl:(p + 1) * kzl]
-        run(1, npx, lambda r: forth(c, r).start())
+        spread(npx, at_x, lambda r: msg.at[at_x(r)[0], c], got.at[me_x, c], a_send.at[c], a_recv.at[c])
         return carry
 
     lax.fori_loop(0, pieces, depth_piece, 0)
-    run(1, npx, lambda r: reply_x(r).start())
+
+    settle(fr1.at[others_x], f_send.at[0], f_recv.at[0])
+    fsum[1] = jnp.sum(fr1[...], axis=0)
+    spread(npy, at_y, lambda r: fsum.at[1], fr2.at[me_y], f_send.at[1], f_recv.at[1])
+    fr2[me_y] = fsum[1]
+    settle(replies.at[others_y], r_send.at[2], r_recv.at[2])
+    lines = replies.reshape(npy * 2 * npx, SEG)
+    for p in range(npx):
+        for r in range(2):
+            fetch[p, r * npy:(r + 1) * npy, :] = lines[pl.ds(r * npx + p, npy, stride=2 * npx), :]
+    spread(npx, at_x, lambda r: fetch.at[at_x(r)[0]], fetched.at[me_x], r_send.at[3], r_recv.at[3])
     fetched[me_x] = fetch[me_x]
 
     def table_cell(i, carry):
@@ -542,6 +500,40 @@
     kap[0] = jnp.ones_like(mu)
     lax.fori_loop(1, nyl, table_cell, (jnp.ones_like(mu), mu))
 
+    shape = (places, cells)
+    cell = lax.broadcasted_iota(jnp.int32, shape, 1) * halves
+    for h in range(halves):
+        hot[h] = (jnp.broadcast_to(pick[...], shape) == cell + h).astype(F32).astype(BF16)
+
+    settle(fr2.at[others_y], f_send.at[1], f_recv.at[1])
+    flux = jnp.sum(fr2[...], axis=0) * (1.0 / (nx * npy * nyl))
+    press = []
+    for k in range(OUTLETS):
+        total = resist[k, 0] * flux[0:1]
+        for n in range(1, OUTLETS):
+            total = total + resist[k, n] * flux[n:n + 1]
+        press.append(total[:, HALF - 1:HALF])
+
+    def pressures(which):
+        drop = jnp.zeros(which.shape, F32)
+        for k in range(OUTLETS):
+            drop = jnp.where(which == k, jnp.broadcast_to(press[k], which.shape), drop)
+        return drop
+
+    def lower(x, carry):
+        drop = DT * jnp.where(lane == HALF - 1, pressures(idb[x]), 0.0)
+        w2[halves - 1, x] = w2[halves - 1, x] - drop
+        return carry
+
+    lax.fori_loop(0, nxl, lower, 0)
+    quarter = lane // nxl
+    for n in range(npx // 4):
+        which = asked[4 * n, 8:top, :]
+        for a in range(1, 4):
+            which = jnp.where(quarter == a, pltpu.roll(asked[4 * n + a, 8:top, :], a * nxl, 1), which)
+        outlet[:, n * HALF:(n + 1) * HALF] = pressures(which)
+    weight = jnp.broadcast_to(lam_z[pl.ds(pl.multiple_of(me_x * kzl, kzl), kzl), 1:2], (kzl, nx))
+
     wides = npx // 4
 
     def row_of(i):
@@ -552,7 +544,7 @@
 
     def line_piece(c, carry):
         got[me_x, c] = msg[me_x, c]
-        run(1, npx, lambda r: forth(c, r).wait())
+        settle(got.at[others_x, c], a_send.at[c], a_recv.at[c])
 
         def gather(sg, inner):
             for half in range(per // 4):
@@ -563,6 +555,14 @@
             return inner
 
         lax.fori_loop(0, wides, gather, 0)
+
+        def add_outlet(m, inner):
+            y = c * per + m
+            line = jnp.broadcast_to(outlet[pl.ds(y, 1), :], (kzl, nx))
+            cols[row_of(y), :] = cols[row_of(y), :] + weight * line
+            return inner
+
+        lax.fori_loop(0, per, add_outlet, 0)
         rows = piece_rows(c)
         cols[rows, :] = dot_parts(split(cols[rows, :], 2), (tt[0], tt[1]), ((1,), (0,)))
         return carry
@@ -583,12 +583,9 @@
         isnd[j, 0:kown, :] = ends[j * kown:(j + 1) * kown]
         isnd[j, kown:2 * kown, :] = over[j * kown:(j + 1) * kown]
 
-    def collect(r):
-        return remote(isnd.at[at_y(r)[1]], ircv.at[me_y], i_send.at[r], i_recv.at[r], at_y(r))
-
-    run(1, npy, lambda r: collect(r).start())
+    spread(npy, at_y, lambda r: isnd.at[at_y(r)[1]], ircv.at[me_y], i_send.at[0], i_recv.at[0])
     ircv[me_y] = isnd[me_y]
-    run(1, npy, lambda r: collect(r).wait())
+    settle(ircv.at[others_y], i_send.at[0], i_recv.at[0])
 
     rho = []
     for b in range(npy):
@@ -616,22 +613,13 @@
         jsnd[b, 0:kown, :] = value
         jsnd[b, 2 * kown:3 * kown, :] = mean
 
-    def hand_back(r):
-        n = npy + r
-        return remote(jsnd.at[at_y(r)[1]], jrcv.at[me_y], i_send.at[n], i_recv.at[n], at_y(r))
-
-    run(1, npy, lambda r: hand_back(r).start())
+    spread(npy, at_y, lambda r: jsnd.at[at_y(r)[1]], jrcv.at[me_y], i_send.at[1], i_recv.at[1])
     jrcv[me_y] = jsnd[me_y]
-    run(1, npy, lambda r: hand_back(r).wait())
+    settle(jrcv.at[others_y], i_send.at[1], i_recv.at[1])
     for j in range(npy):
         for part in range(3):
             back[part, j * kown:(j + 1) * kown, :] = jrcv[j, part * kown:(part + 1) * kown, :]
     first_value, mean_rows = back[0], back[2]
-
-    def home(c, r):
-        p = at_x(r)[0]
-        n = (pieces + c) * npx + r
-        return remote(msg.at[p, c], got2.at[me_x, c], a_send.at[n], a_recv.at[n], at_x(r))
 
     def up_piece(n, q):
         c = pieces - 1 - n
@@ -659,7 +647,8 @@
             return inner
 
         lax.fori_loop(0, wides, scatter, 0)
-        run(1, npx, lambda r: home(c, r).start())
+        n = pieces + c
+        spread(npx, at_x, lambda r: msg.at[at_x(r)[0], c], got2.at[me_x, c], a_send.at[n], a_recv.at[n])
         return q
 
     lax.fori_loop(0, pieces, up_piece, back[1])
@@ -669,7 +658,7 @@
     def rise_piece(n, carry):
         c = pieces - 1 - n
         got2[me_x, c] = msg[me_x, c]
-        run(1, npx, lambda r: home(c, r).wait())
+        settle(got2.at[others_x, c], a_send.at[pieces + c], a_recv.at[pieces + c])
         value = got2[:, c].reshape(nz, 256)
         out = dot_parts(split(value.T, 3), (tz[0], tz[1], tz[2]), ((1,), (0,)))
         for y in range(per):
@@ -694,17 +683,25 @@
     def join(field, x):
         return jnp.concatenate([field[h, x, 0:nyl, :] for h in range(halves)], axis=1)
 
-    def correct_depth(x, carry):
+    def flow(a, x):
+        return jnp.concatenate([up[a, h, x + 1, 8:top, :] for h in range(halves)], axis=1)
+
+    def two_parts(x, carry):
         center = q_rows(x + 1, 8, nyl)
         spot = lax.broadcasted_iota(jnp.int32, center.shape, 1)
         below = jnp.where(spot == 0, center, pltpu.roll(center, 1, 1))
         above = jnp.where(spot == nz - 1, center, pltpu.roll(center, nz - 1, 1))
-        vel[2, x] = join(w2, x) - 0.5 * (above - below)
+        v2 = join(w2, x) - 0.5 * (above - below)
+        v0 = join(w0, x + 1) - 0.5 * (q_rows(x + 2, 8, nyl) - q_rows(x, 8, nyl))
+        vel[0, x] = v0
+        vel[2, x] = v2
+        total = flow(0, x) * v0 + flow(2, x) * v2
+        for h in range(halves):
+            sig[h, pl.ds(pl.multiple_of(x * nyl, 8), nyl), :] = total[:, h * HALF:(h + 1) * HALF]
         return carry
 
-    lax.fori_loop(0, nxl, correct_depth, 0)
+    lax.fori_loop(1, nxl - 1, two_parts, 0)
     outs = [pltpu.make_async_copy(vel.at[b], v_out.at[b], out_sem.at[b]) for b in range(3)]
-    outs[2].start()
 
     for copy in halo:
         copy.wait()
@@ -722,32 +719,31 @@
         for h in range(halves):
             qp[h, nxl + 1, 8:top, :] = qp[h, nxl, 8:top, :]
 
-    def correct(x, carry):
+    two_parts(0, 0)
+    two_parts(nxl - 1, 0)
+    outs[0].start()
+    outs[2].start()
+
+    def last_part(x, carry):
         tall = q_rows(x + 1, 0, wide)
-        v0 = join(w0, x + 1) - 0.5 * (q_rows(x + 2, 8, nyl) - q_rows(x, 8, nyl))
         deep = jnp.concatenate([w1[h, x + 1, 8:top, :] for h in range(halves)], axis=1)
         v1 = deep - 0.5 * (tall[9:top + 1] - tall[7:top - 1])
-        vel[0, x] = v0
         vel[1, x] = v1
-        u = [jnp.concatenate([up[a, h, x + 1, 8:top, :] for h in range(halves)], axis=1) for a in range(3)]
-        total = -ALPHA * (u[0] * v0 + u[1] * v1 + u[2] * vel[2, x])
+        rows = pl.ds(pl.multiple_of(x * nyl, 8), nyl)
+        part = flow(1, x) * v1
         for h in range(halves):
-            sig[h, pl.ds(pl.multiple_of(x * nyl, 8), nyl), :] = total[:, h * HALF:(h + 1) * HALF]
+            sig[h, rows, :] = -ALPHA * (sig[h, rows, :] + part[:, h * HALF:(h + 1) * HALF])
         return carry
 
-    lax.fori_loop(0, nxl, correct, 0)
-    outs[0].start()
+    lax.fori_loop(0, nxl, last_part, 0)
     outs[1].start()
 
-    shape = (places, cells)
-    cell = lax.broadcasted_iota(jnp.int32, shape, 1) * halves
     picked = None
     for h in range(halves):
-        hot = (jnp.broadcast_to(pick[...], shape) == cell + h).astype(F32).astype(BF16)
-        for part in reversed(split(sig[h], 3)):
-            term = jnp.dot(hot, part, preferred_element_type=F32)
+        for part in reversed(split(sig[h], 2)):
+            term = jnp.dot(hot[h], part, preferred_element_type=F32)
             picked = term if picked is None else picked + term
-    run(1, npx, lambda r: reply_x(r).wait())
+    settle(fetched.at[others_x], r_send.at[3], r_recv.at[3])
     products = picked * fetched[...].reshape(places, SEG)
     ones = jnp.ones((8, SEG), BF16)
     totals = sum(
@@ -755,13 +751,13 @@
         for part in reversed(split(products, 3))
     )
     by_px(totals, give)
-    run(1, npx, lambda r: give_x(r).start())
+    spread(npx, at_x, lambda r: give.at[at_x(r)[0]], given.at[me_x], r_send.at[4], r_recv.at[4])
     given[me_x] = give[me_x]
-    run(1, npx, lambda r: give_x(r).wait())
+    settle(given.at[others_x], r_send.at[4], r_recv.at[4])
     by_py(given[:, 0, :], gives)
-    run(1, npy, lambda r: give_y(r).start())
+    spread(npy, at_y, lambda r: gives.at[at_y(r)[1]], taken.at[me_y], r_send.at[5], r_recv.at[5])
     taken[me_y] = gives[me_y]
-    run(1, npy, lambda r: give_y(r).wait())
+    settle(taken.at[others_y], r_send.at[5], r_recv.at[5])
 
     def add_up(j, total):
         label, value = wanted[j], taken[j]
@@ -792,7 +788,7 @@
     here = pl.BlockSpec(memory_space=pltpu.VMEM)
     scalar = pl.BlockSpec(memory_space=pltpu.SMEM)
     dma = pltpu.SemaphoreType.DMA
-    tables = args[11:14]
+    tables = args[10:13]
     field = vmem((3, halves, nxl + 2, wide, HALF), F32)
     line = vmem((nyl, kzl, nx), F32)
     message = vmem((npx, pieces, kzl, 256), F32)
@@ -832,9 +828,11 @@
         vmem((2, halves, nxl, HALF), F32),
         vmem((3, nxl, nyl, nz), F32),
         vmem((halves, cells, HALF), F32),
+        vmem((nyl, nx), F32),
+        vmem((halves, places, cells), BF16),
         vmem((places, 1), jnp.int32),
-        vmem((npx, 8, HALF), F32),
-        vmem((npx, 8, HALF), F32),
+        vmem((npx, 8 + nyl, HALF), F32),
+        vmem((npx, 8 + nyl, HALF), F32),
         vmem((npy, npx, HALF), F32),
         vmem((npy, npx, HALF), F32),
         vmem((places, HALF), BF16),
@@ -854,14 +852,14 @@
         dma((8,)),
         dma((6,)),
         dma((6,)),
-        dma((npx + npy,)),
-        dma((npx + npy,)),
-        dma((2 * pieces * npx,)),
-        dma((2 * pieces * npx,)),
-        dma((2 * npy,)),
-        dma((2 * npy,)),
-        dma((3 * (npx + npy),)),
-        dma((3 * (npx + npy),)),
+        dma((2,)),
+        dma((2,)),
+        dma((2 * pieces,)),
+        dma((2 * pieces,)),
+        dma((2,)),
+        dma((2,)),
+        dma((6,)),
+        dma((6,)),
         dma((3,)),
     ]
     return pl.pallas_call(
@@ -870,7 +868,7 @@
             jax.ShapeDtypeStruct((3, nxl, nyl, nz), F32),
             jax.ShapeDtypeStruct((1, owner_rows), F32),
         ),
-        in_specs=[anywhere] * 4 + [here, scalar] + [here] * 5 + [anywhere] * len(tables) + [here] * 2,
+        in_specs=[anywhere] * 4 + [here, scalar] + [here] * 4 + [anywhere] * len(tables) + [here] * 2,
         out_specs=(anywhere, here),
         scratch_shapes=scratch,
         compiler_params=pltpu.CompilerParams(
@@ -891,22 +889,24 @@
     tables = [split_np(tz, 3), split_np(tx, 3), split_np(np.ascontiguousarray(tx.T), 2)]
     tables = [jnp.asarray(np.stack(t)) for t in tables]
     lam_x = jnp.asarray(-eigen_np(nx)[None, :])
-    lam_z = jnp.asarray(np.repeat(-eigen_np(nz)[:, None], HALF, axis=1))
+    depth = np.zeros((nz, HALF), np.float32)
+    depth[:, 0] = -eigen_np(nz)
+    depth[:, 1] = -0.5 * DT * tz[:, nz - 2]
+    depth = jnp.asarray(depth)
     args = (
         adjoint_start,
         base_flow.reshape(3, nxl * nyl, nz),
         source.reshape(3, nxl * nyl, nz),
         solid_mask,
-        outlet_ids,
+        outlet_ids.T,
         resist,
-        tile_owner,
         tile_owner.reshape(1, -1),
         tile_slot.reshape(1, -1),
         tile_column.reshape(1, -1),
         control_basis,
         *tables,
         lam_x,
-        lam_z,
+        depth,
     )
     velocity, grad = main_call((npx, npy, nxl, nyl, nz), args, control_basis.shape[0])
     return velocity, grad.reshape(-1)

time: 118 us -> 111 us (0.941)
  Pallas kernels: 111 us -> 107 us
  local copies, waits for them, and re-layouts: 6.6 us -> 3.75 us
    pallas_call x1, Pallas kernels: 111 us -> 107 us  [main_call(): pl.pallas_call(functools.partial(main_kernel, dims), out_shape=(jax.Shape...]
    unnamed x6 -> x4, local copies, waits for them, and re-layouts: 6.6 us -> 3.75 us
where the time goes in v3:
time: 111 us
  Pallas kernels  107 us (96%)
  local copies, waits for them, and re-layouts  3.75 us (3%)
    pallas_call x1, Pallas kernels, main_call(): pl.pallas_call(functools.partial(main_kernel, dims), out_shape=(jax.Shape...  107 us
    unnamed x4, local copies, waits for them, and re-layouts  3.75 us

profile of v3, /device:TPU:1, one launch (start us, length us, event | category | flops | bytes accessed | tf_op | source)
XLA Modules:
  0.0 111.2 jit_solution(15726298635483370817)
XLA Ops:
  0.6 106.8 %project.1 = (f32[3,32,24,256]{3,2,1,0:T(8,128)}, f32[1,32]{1,0:T(1,128)}) custom-call(f32[3,32,24,256]{3,2,1,0:T(8,128)} %v_hbm.1, bf16[3,768,256]{2,1,0:T(8,128)(2,1)} %bitcast.7, bf16[3,768,256]{2,1,0:T(8,128)(2,1)} %bitcast.8, s32[32,24,256]{2,1,0:T(8,128)} %m_hbm.1, s32[24,32]{1,0:T(8,128)} %bitcast.9, f32[8,8]{1,0:T(8,128)} %resist.1, ...), custom_call_target="tpu_custom_call" | custom-call | tf_op jit(solution)/shard_map/project/pallas_call | solution.py:865
  107.5 0.0 copy-start
  107.5 3.2 %copy.19 = f32[3,32,24,256]{3,2,1,0:T(8,128)} copy(f32[3,32,24,256]{3,2,1,0:T(8,128)} %get-tuple-element.8) | data formatting | bytes 4718592
  110.7 0.0 copy-done
  110.7 0.5 copy.20
Async XLA Ops:
  107.5 3.2 %copy-start = (f32[1,32]{1,0:T(1,128)S(1)}, f32[1,32]{1,0:T(1,128)}, u32[]{:S(2)}) copy-start(f32[1,32]{1,0:T(1,128)} %get-tuple-element.5) | copy-start | bytes 388

commit v4 on v3

--- a/solution.py
+++ b/solution.py
@@ -93,11 +93,11 @@
     tz_hbm, tx_hbm, tt_hbm, lam_x, lam_z,
     v_out, grad_out,
     vp, up, ub, sb, mk, idb, w0, w1, w2, snd_y, rcv_y, wy_snd, wy_rcv, fsum, fr1, fr2,
-    div, msg, got, got2, cols, tau, kap, owner_inv, owner_phi,
+    div, msg, got, got2, relay, relay2, cols, tau, kap, owner_inv, owner_phi,
     isnd, ircv, jsnd, jrcv, back, qp, qy_snd, qy_rcv, vel, sig,
     outlet, hot, pick, ask, asked, asks, wanted, chosen, reply, replies, fetch, fetched, give, given, gives, taken,
     tz, tx, tt,
-    load_sem, x_send, x_recv, y_send, y_recv, f_send, f_recv, a_send, a_recv, i_send, i_recv, r_send, r_recv, out_sem,
+    load_sem, x_send, x_recv, y_send, y_recv, f_send, f_recv, a_send, a_recv, b_send, b_recv, c_send, i_send, i_recv, r_send, r_recv, out_sem,
 ):
     npx, npy, nxl, nyl, nz = dims
     nx = npx * nxl
@@ -144,6 +144,47 @@
         pltpu.make_async_copy(like, like, recv).wait()
 
     others_x, others_y = pl.ds(0, npx - 1), pl.ds(0, npy - 1)
+
+    ring = npx // 2
+    ring_at = lax.rem(me_x, ring)
+    before_x = me_x - ring_at + lax.rem(ring_at + ring - 2, ring)
+    after_x = me_x - ring_at + lax.rem(ring_at + 2, ring)
+    far_same = ring // 2
+    far_other = jnp.where(lax.rem(me_x, 2) == 0, far_same + 1, far_same - 1)
+    hops = ((before_x, after_x, far_same), (after_x, before_x, far_other))
+    direct_x = pl.ds(0, npx - 5)
+
+    def exchange(c, source, relay, sink, n):
+        for way, (through, _, far) in enumerate(hops):
+            for k in range(2):
+                p = lax.rem(me_x + far + k * ring, npx)
+                remote(
+                    source.at[p, c], relay.at[2 * way + k, c], b_send.at[n], b_recv.at[n], (through, me_y)
+                ).start()
+
+        def start(r):
+            step = lax.rem(r, ring)
+
+            @pl.when((step != far_same) & (step != far_other))
+            def _():
+                remote(source.at[at_x(r)[0], c], sink.at[me_x, c], a_send.at[n], a_recv.at[n], at_x(r)).start()
+
+        run(1, npx, start)
+
+    def forward(c, relay, sink, n):
+        pltpu.make_async_copy(relay.at[:, c], relay.at[:, c], b_recv.at[n]).wait()
+        for way, (_, origin, far) in enumerate(hops):
+            for k in range(2):
+                p = lax.rem(origin + far + k * ring, npx)
+                remote(
+                    relay.at[2 * way + k, c], sink.at[origin, c], c_send.at[n], a_recv.at[n], (p, me_y)
+                ).start()
+
+    def complete(c, relay, sink, n):
+        pltpu.make_async_copy(sink.at[direct_x, c], sink.at[direct_x, c], a_send.at[n]).wait()
+        pltpu.make_async_copy(relay.at[:, c], relay.at[:, c], b_send.at[n]).wait()
+        pltpu.make_async_copy(relay.at[:, c], relay.at[:, c], c_send.at[n]).wait()
+        pltpu.make_async_copy(sink.at[others_x, c], sink.at[others_x, c], a_recv.at[n]).wait()
 
     loads = []
     for c in range(3):
@@ -175,6 +216,52 @@
     run(1, npx, lambda r: pl.semaphore_signal(barrier, inc=1, device_id=at_x(r), device_id_type=MESH))
     run(1, npy, lambda r: pl.semaphore_signal(barrier, inc=1, device_id=at_y(r), device_id_type=MESH))
 
+    def row_at(ref, lead, y):
+        lines = ref.reshape(*ref.shape[:-3], (nxl + 2) * wide, HALF)
+        return lines.at[(*lead, pl.ds(wide + y, nxl, stride=wide), slice(None))]
+
+    def x_pair(field, at, number):
+        return (
+            remote(at(field, nxl), at(field, 0), x_send.at[number], x_recv.at[number], (right_x, me_y)),
+            remote(at(field, 1), at(field, nxl + 1), x_send.at[number + 1], x_recv.at[number + 1], (left_x, me_y)),
+        )
+
+    def at_plane(field, x):
+        return field.at[:, :, x, pl.ds(8, nyl), :]
+
+    def y_pair(send, recv, number):
+        return (
+            remote(send.at[0], recv.at[0], y_send.at[number], y_recv.at[number], (me_x, right_y)),
+            remote(send.at[1], recv.at[1], y_send.at[number + 1], y_recv.at[number + 1], (me_x, left_y)),
+        )
+
+    for copy in loads:
+        copy.wait()
+
+    def pack(field, first):
+        for c in range(3):
+            for h in range(halves):
+                snd_y[0, first + c, h] = row_at(field, (c, h), top - 1)[...].astype(BF16)
+                snd_y[1, first + c, h] = row_at(field, (c, h), 8)[...].astype(BF16)
+
+    pack(vp, 0)
+    load_u.wait()
+
+    def widen(i, carry):
+        for a in range(3):
+            pair = ub[a, pl.ds(pl.multiple_of(i * 2 * nyl, 2 * nyl), 2 * nyl), :].astype(F32)
+            for s in range(2):
+                for h in range(halves):
+                    up[a, h, 1 + 2 * i + s, 8:top, :] = pair[s * nyl:(s + 1) * nyl, h * HALF:(h + 1) * HALF]
+        return carry
+
+    lax.fori_loop(0, nxl // 2, widen, 0)
+    pack(up, 3)
+    pl.semaphore_wait(barrier, npx - 1 + npy - 1)
+    halo = y_pair(snd_y, rcv_y, 0) + x_pair(vp, at_plane, 0) + x_pair(up, at_plane, 2)
+    for copy in halo:
+        copy.start()
+
     count = owner_row.shape[1]
     owners = owner_row[...]
     same = jnp.broadcast_to(owners, (8, count)).T[:, 0:1] == owners
@@ -217,65 +304,11 @@
     for x in range(nxl):
         idb[x] = jnp.broadcast_to(seen[:, x:x + 1], (nyl, HALF))
 
-    def row_at(ref, lead, y):
-        lines = ref.reshape(*ref.shape[:-3], (nxl + 2) * wide, HALF)
-        return lines.at[(*lead, pl.ds(wide + y, nxl, stride=wide), slice(None))]
-
-    def x_pair(field, at, number):
-        return (
-            remote(at(field, nxl), at(field, 0), x_send.at[number], x_recv.at[number], (right_x, me_y)),
-            remote(at(field, 1), at(field, nxl + 1), x_send.at[number + 1], x_recv.at[number + 1], (left_x, me_y)),
-        )
-
-    def at_plane(field, x):
-        return field.at[:, :, x, pl.ds(8, nyl), :]
-
-    def y_pair(send, recv, number):
-        return (
-            remote(send.at[0], recv.at[0], y_send.at[number], y_recv.at[number], (me_x, right_y)),
-            remote(send.at[1], recv.at[1], y_send.at[number + 1], y_recv.at[number + 1], (me_x, left_y)),
-        )
-
-    for copy in loads:
-        copy.wait()
-    pl.semaphore_wait(barrier, npx - 1 + npy - 1)
-
-    def pack(field, first):
-        for c in range(3):
-            for h in range(halves):
-                snd_y[0, first + c, h] = row_at(field, (c, h), top - 1)[...].astype(BF16)
-                snd_y[1, first + c, h] = row_at(field, (c, h), 8)[...].astype(BF16)
-
-    halo_vx = x_pair(vp, at_plane, 0)
-    for copy in halo_vx:
-        copy.start()
-
     def ask_start():
         spread(npx, at_x, lambda r: ask.at[at_x(r)[0]], asked.at[me_x], r_send.at[0], r_recv.at[0])
         asked[me_x] = ask[me_x]
 
     ask_start()
-    pack(vp, 0)
-    load_u.wait()
-
-    def widen(i, carry):
-        for a in range(3):
-            pair = ub[a, pl.ds(pl.multiple_of(i * 2 * nyl, 2 * nyl), 2 * nyl), :].astype(F32)
-            for s in range(2):
-                for h in range(halves):
-                    up[a, h, 1 + 2 * i + s, 8:top, :] = pair[s * nyl:(s + 1) * nyl, h * HALF:(h + 1) * HALF]
-        return carry
-
-    lax.fori_loop(0, nxl // 2, widen, 0)
-    pack(up, 3)
-    halo = y_pair(snd_y, rcv_y, 0) + x_pair(up, at_plane, 2)
-    for copy in halo:
-        copy.start()
-
-    settle(asked.at[others_x], r_send.at[0], r_recv.at[0])
-    by_py(asked[:, 0, :], asks)
-    spread(npy, at_y, lambda r: asks.at[at_y(r)[1]], wanted.at[me_y], r_send.at[1], r_recv.at[1])
-    wanted[me_y] = asks[me_y]
 
     def reduce_cell(c, g, right):
         inv = 1.0 / (c + right + g)
@@ -310,31 +343,13 @@
         owner_inv[npy - 1] = jnp.where(positive, 1.0 / jnp.where(positive, held, 1.0), 0.0)
 
     owner_table()
-    settle(wanted.at[others_y], r_send.at[1], r_recv.at[1])
-
-    slot_lane = lax.broadcasted_iota(jnp.int32, (npx, HALF), 1).astype(F32)
-
-    def choose(j, carry):
-        label = wanted[j]
-        for r in range(2):
-            hit = jnp.broadcast_to(label[:, r * npy:r * npy + 1], (npx, HALF)) == slot_lane
-            chosen[pl.ds(pl.multiple_of((2 * j + r) * npx, npx), npx), :] = hit.astype(F32).astype(BF16)
-        return carry
-
-    lax.fori_loop(0, npy, choose, 0)
-    controls = basis.shape[0]
-    wide_basis = jnp.concatenate([basis[...], jnp.zeros((HALF - controls, SEG), F32)], axis=0)
-    rows = sum(
-        jnp.dot(chosen[...], part, preferred_element_type=F32) for part in reversed(split(wide_basis, 3))
-    )
-    for j in range(npy):
-        reply[j] = rows[j * 2 * npx:(j + 1) * 2 * npx]
-    spread(npy, at_y, lambda r: reply.at[at_y(r)[1]], replies.at[me_y], r_send.at[2], r_recv.at[2])
-    replies[me_y] = reply[me_y]
-
+    settle(asked.at[others_x], r_send.at[0], r_recv.at[0])
+    by_py(asked[:, 0, :], asks)
+    spread(npy, at_y, lambda r: asks.at[at_y(r)[1]], wanted.at[me_y], r_send.at[1], r_recv.at[1])
+    wanted[me_y] = asks[me_y]
     load_s.wait()
     load_m.wait()
-    for copy in halo_vx + halo:
+    for copy in halo:
         copy.wait()
 
     for c in range(3):
@@ -420,6 +435,28 @@
     for copy in halo:
         copy.start()
 
+    settle(wanted.at[others_y], r_send.at[1], r_recv.at[1])
+
+    slot_lane = lax.broadcasted_iota(jnp.int32, (npx, HALF), 1).astype(F32)
+
+    def choose(j, carry):
+        label = wanted[j]
+        for r in range(2):
+            hit = jnp.broadcast_to(label[:, r * npy:r * npy + 1], (npx, HALF)) == slot_lane
+            chosen[pl.ds(pl.multiple_of((2 * j + r) * npx, npx), npx), :] = hit.astype(F32).astype(BF16)
+        return carry
+
+    lax.fori_loop(0, npy, choose, 0)
+    controls = basis.shape[0]
+    wide_basis = jnp.concatenate([basis[...], jnp.zeros((HALF - controls, SEG), F32)], axis=0)
+    rows = sum(
+        jnp.dot(chosen[...], part, preferred_element_type=F32) for part in reversed(split(wide_basis, 3))
+    )
+    for j in range(npy):
+        reply[j] = rows[j * 2 * npx:(j + 1) * 2 * npx]
+    spread(npy, at_y, lambda r: reply.at[at_y(r)[1]], replies.at[me_y], r_send.at[2], r_recv.at[2])
+    replies[me_y] = reply[me_y]
+
     lane = lax.broadcasted_iota(jnp.int32, (nyl, HALF), 1)
 
     def flux_plane(x, carry):
@@ -471,10 +508,11 @@
         out = dot_parts((tz[0], tz[1]), split(value, 2), ((1,), (1,)))
         for p in range(npx):
             msg[p, c] = out[p * kzl:(p + 1) * kzl]
-        spread(npx, at_x, lambda r: msg.at[at_x(r)[0], c], got.at[me_x, c], a_send.at[c], a_recv.at[c])
+        exchange(c, msg, relay, got, c)
         return carry
 
     lax.fori_loop(0, pieces, depth_piece, 0)
+    run(0, pieces, lambda c: forward(c, relay, got, c))
 
     settle(fr1.at[others_x], f_send.at[0], f_recv.at[0])
     fsum[1] = jnp.sum(fr1[...], axis=0)
@@ -544,7 +582,7 @@
 
     def line_piece(c, carry):
         got[me_x, c] = msg[me_x, c]
-        settle(got.at[others_x, c], a_send.at[c], a_recv.at[c])
+        complete(c, relay, got, c)
 
         def gather(sg, inner):
             for half in range(per // 4):
@@ -647,18 +685,23 @@
             return inner
 
         lax.fori_loop(0, wides, scatter, 0)
-        n = pieces + c
-        spread(npx, at_x, lambda r: msg.at[at_x(r)[0], c], got2.at[me_x, c], a_send.at[n], a_recv.at[n])
+        exchange(c, msg, relay2, got2, pieces + c)
+
+        @pl.when(n > 0)
+        def _():
+            forward(c + 1, relay2, got2, pieces + c + 1)
+
         return q
 
     lax.fori_loop(0, pieces, up_piece, back[1])
+    forward(0, relay2, got2, pieces)
 
     pressure = qp.reshape(halves, (nxl + 2) * wide, HALF)
 
     def rise_piece(n, carry):
         c = pieces - 1 - n
         got2[me_x, c] = msg[me_x, c]
-        settle(got2.at[others_x, c], a_send.at[pieces + c], a_recv.at[pieces + c])
+        complete(c, relay2, got2, pieces + c)
         value = got2[:, c].reshape(nz, 256)
         out = dot_parts(split(value.T, 3), (tz[0], tz[1], tz[2]), ((1,), (0,)))
         for y in range(per):
@@ -813,6 +856,8 @@
         message,
         message,
         message,
+        vmem((4, pieces, kzl, 256), F32),
+        vmem((4, pieces, kzl, 256), F32),
         vmem((nyl * kzl, nx), F32),
         line,
         line,
@@ -856,6 +901,9 @@
         dma((2,)),
         dma((2 * pieces,)),
         dma((2 * pieces,)),
+        dma((2 * pieces,)),
+        dma((2 * pieces,)),
+        dma((2 * pieces,)),
         dma((2,)),
         dma((2,)),
         dma((6,)),
@@ -872,7 +920,7 @@
         out_specs=(anywhere, here),
         scratch_shapes=scratch,
         compiler_params=pltpu.CompilerParams(
-            collective_id=0, has_side_effects=True, vmem_limit_bytes=58 * 2**20
+            collective_id=0, has_side_effects=True, vmem_limit_bytes=36 * 2**20
         ),
         name="project",
     )(*args)

time: 111 us -> 124 us (1.12)
  local copies, waits for them, and re-layouts: 3.75 us -> 16.6 us
    unnamed x4 -> x32, local copies, waits for them, and re-layouts: 3.75 us -> 16.6 us
where the time goes in v4:
time: 124 us; the launch traced here: 123 us
  Pallas kernels  106 us (85%)
  local copies, waits for them, and re-layouts  16.6 us (13%)
    pallas_call x1, Pallas kernels, main_call(): pl.pallas_call(functools.partial(main_kernel, dims), out_shape=(jax.Shape...  106 us
    unnamed x32, local copies, waits for them, and re-layouts  16.6 us

profile of v4, /device:TPU:1, one launch (start us, length us, event | category | flops | bytes accessed | tf_op | source)
XLA Modules:
  0.0 123.1 jit_solution(15193363746261542718)
XLA Ops:
  0.6 0.0 copy-start
  0.6 1.7 %copy-done = f32[3,32,24,256]{3,2,1,0:T(8,128)S(1)} copy-done((f32[3,32,24,256]{3,2,1,0:T(8,128)S(1)}, f32[3,32,24,256]{3,2,1,0:T(8,128)}, u32[]{:S(2)}) %copy-start) | copy-done | bytes 2359320
  2.3 0.0 copy-start.1
  2.3 1.4 %copy-done.1 = bf16[3,512,512]{2,1,0:T(8,128)(2,1)S(1)} copy-done((bf16[3,512,512]{2,1,0:T(8,128)(2,1)S(1)}, bf16[3,512,512]{2,1,0:T(8,128)(2,1)}, u32[]{:S(2)}) %copy-start.1) | copy-done | bytes 1572888
  3.7 0.0 copy-start.2
  3.7 1.3 %copy-done.2 = bf16[3,32,24,256]{3,2,1,0:T(8,128)(2,1)S(1)} copy-done((bf16[3,32,24,256]{3,2,1,0:T(8,128)(2,1)S(1)}, bf16[3,32,24,256]{3,2,1,0:T(8,128)(2,1)}, u32[]{:S(2)}) %copy-start.2) | copy-done | bytes 1179672
  5.0 0.0 copy-start.3
  5.0 1.3 %copy-done.3 = bf16[3,32,24,256]{3,2,1,0:T(8,128)(2,1)S(1)} copy-done((bf16[3,32,24,256]{3,2,1,0:T(8,128)(2,1)S(1)}, bf16[3,32,24,256]{3,2,1,0:T(8,128)(2,1)}, u32[]{:S(2)}) %copy-start.3) | copy-done | bytes 1179672
  6.3 0.0 copy-start.4
  6.3 1.2 copy-done.4
  7.5 0.0 copy-start.5
  7.5 1.1 copy-done.5
  8.6 1.0 copy-done.6
  9.6 0.9 copy-done.7
  10.5 0.7 copy-done.8
  11.2 0.7 copy-done.9
  11.9 0.7 copy-done.10
  12.6 0.7 copy-done.11
  13.3 0.7 copy-done.12
  14.0 0.7 copy-done.13
  14.7 0.7 copy-done.14
  15.3 105.8 %project.1 = (f32[3,32,24,256]{3,2,1,0:T(8,128)S(1)}, f32[1,32]{1,0:T(1,128)S(1)}) custom-call(f32[3,32,24,256]{3,2,1,0:T(8,128)S(1)} %copy-done, bf16[3,768,256]{2,1,0:T(8,128)(2,1)S(1)} %bitcast.7, bf16[3,768,256]{2,1,0:T(8,128)(2,1)S(1)} %bitcast.8, s32[32,24,256]{2,1,0:T(8,128)S(1)} %copy-done.5, s32[24,32]{1,0:T(8,128)S(1)} %bitcast.9, ...), custom_call_target="tpu_custom_call" | custom-call | tf_op jit(solution)/shard_map/project/pallas_call | solution.py:913
  121.2 1.4 %copy.19 = f32[3,32,24,256]{3,2,1,0:T(8,128)} copy(f32[3,32,24,256]{3,2,1,0:T(8,128)S(1)} %get-tuple-element.8) | data formatting | bytes 4718592
  122.6 0.5 copy.20
  (9 shorter events, 0.0 us)
Async XLA Ops:
  0.6 1.7 %copy-start = (f32[3,32,24,256]{3,2,1,0:T(8,128)S(1)}, f32[3,32,24,256]{3,2,1,0:T(8,128)}, u32[]{:S(2)}) copy-start(f32[3,32,24,256]{3,2,1,0:T(8,128)} %v_hbm.1) | copy-start | bytes 7077892
  2.3 1.4 %copy-start.1 = (bf16[3,512,512]{2,1,0:T(8,128)(2,1)S(1)}, bf16[3,512,512]{2,1,0:T(8,128)(2,1)}, u32[]{:S(2)}) copy-start(bf16[3,512,512]{2,1,0:T(8,128)(2,1)} %constant.11.clone.tx_hbm) | copy-start | bytes 4718596
  3.7 1.3 %copy-start.2 = (bf16[3,32,24,256]{3,2,1,0:T(8,128)(2,1)S(1)}, bf16[3,32,24,256]{3,2,1,0:T(8,128)(2,1)}, u32[]{:S(2)}) copy-start(bf16[3,32,24,256]{3,2,1,0:T(8,128)(2,1)} %param.15) | copy-start | bytes 3538948
  5.0 1.3 %copy-start.3 = (bf16[3,32,24,256]{3,2,1,0:T(8,128)(2,1)S(1)}, bf16[3,32,24,256]{3,2,1,0:T(8,128)(2,1)}, u32[]{:S(2)}) copy-start(bf16[3,32,24,256]{3,2,1,0:T(8,128)(2,1)} %param.17) | copy-start | bytes 3538948
  6.3 1.2 copy-start.4
  7.5 1.1 copy-start.5
  8.6 1.0 copy-start.6
  9.6 0.9 copy-start.7
  10.5 0.7 copy-start.8
  11.2 0.7 copy-start.9
  11.9 0.7 copy-start.10
  12.6 0.7 copy-start.11
  13.3 0.7 copy-start.12
  14.0 0.7 copy-start.13
  14.7 0.7 copy-start.14

commit v5 on v4

--- a/solution.py
+++ b/solution.py
@@ -53,12 +53,16 @@
 
 def dot_parts(a_parts, b_parts, contract):
     dims = ((contract[0], contract[1]), ((), ()))
-    dot = functools.partial(lax.dot_general, dimension_numbers=dims, preferred_element_type=F32)
+    count, rows = len(a_parts), a_parts[0].shape[0]
+    terms = {}
+    for j in range(count):
+        stacked = jnp.concatenate(a_parts[:count - j], axis=0) if j < count - 1 else a_parts[0]
+        out = lax.dot_general(stacked, b_parts[j], dimension_numbers=dims, preferred_element_type=F32)
+        for i in range(count - j):
+            terms[i, j] = out[i * rows:(i + 1) * rows]
     total = None
-    for order in range(len(a_parts) - 1, -1, -1):
-        for i in range(order + 1):
-            term = dot(a_parts[i], b_parts[order - i])
-            total = term if total is None else total + term
+    for i, j in sorted(terms, key=lambda at: -(at[0] + at[1])):
+        total = terms[i, j] if total is None else total + terms[i, j]
     return total
 
 
@@ -89,15 +93,15 @@
 
 def main_kernel(
     dims,
-    v_hbm, u_hbm, s_hbm, m_hbm, ids, resist, owner_row, slot_row, column_row, basis,
-    tz_hbm, tx_hbm, tt_hbm, lam_x, lam_z,
+    v_hbm, u_hbm, s_hbm, m_hbm, ids_hbm, resist_hbm, owner_hbm, slot_hbm, column_hbm, basis_hbm,
+    tz_hbm, tx_hbm, tt_hbm, lam_x_hbm, lam_z_hbm,
     v_out, grad_out,
     vp, up, ub, sb, mk, idb, w0, w1, w2, snd_y, rcv_y, wy_snd, wy_rcv, fsum, fr1, fr2,
-    div, msg, got, got2, relay, relay2, cols, tau, kap, owner_inv, owner_phi,
+    div, msg, got, got2, cols, tau, kap, owner_inv, owner_phi,
     isnd, ircv, jsnd, jrcv, back, qp, qy_snd, qy_rcv, vel, sig,
     outlet, hot, pick, ask, asked, asks, wanted, chosen, reply, replies, fetch, fetched, give, given, gives, taken,
-    tz, tx, tt,
-    load_sem, x_send, x_recv, y_send, y_recv, f_send, f_recv, a_send, a_recv, b_send, b_recv, c_send, i_send, i_recv, r_send, r_recv, out_sem,
+    tz, tx, tt, ids, resist, owner_row, slot_row, column_row, basis, lam_x, lam_z,
+    load_sem, x_send, x_recv, y_send, y_recv, f_send, f_recv, a_send, a_recv, i_send, i_recv, r_send, r_recv, out_sem,
 ):
     npx, npy, nxl, nyl, nz = dims
     nx = npx * nxl
@@ -117,6 +121,7 @@
     first_y, last_y = me_y == 0, me_y == npy - 1
     top = 8 + nyl
     wide = nyl + 16
+    zero_at = jnp.minimum(me_x, 0)
 
     def run(first, last, action):
         def body(r, carry):
@@ -144,47 +149,6 @@
         pltpu.make_async_copy(like, like, recv).wait()
 
     others_x, others_y = pl.ds(0, npx - 1), pl.ds(0, npy - 1)
-
-    ring = npx // 2
-    ring_at = lax.rem(me_x, ring)
-    before_x = me_x - ring_at + lax.rem(ring_at + ring - 2, ring)
-    after_x = me_x - ring_at + lax.rem(ring_at + 2, ring)
-    far_same = ring // 2
-    far_other = jnp.where(lax.rem(me_x, 2) == 0, far_same + 1, far_same - 1)
-    hops = ((before_x, after_x, far_same), (after_x, before_x, far_other))
-    direct_x = pl.ds(0, npx - 5)
-
-    def exchange(c, source, relay, sink, n):
-        for way, (through, _, far) in enumerate(hops):
-            for k in range(2):
-                p = lax.rem(me_x + far + k * ring, npx)
-                remote(
-                    source.at[p, c], relay.at[2 * way + k, c], b_send.at[n], b_recv.at[n], (through, me_y)
-                ).start()
-
-        def start(r):
-            step = lax.rem(r, ring)
-
-            @pl.when((step != far_same) & (step != far_other))
-            def _():
-                remote(source.at[at_x(r)[0], c], sink.at[me_x, c], a_send.at[n], a_recv.at[n], at_x(r)).start()
-
-        run(1, npx, start)
-
-    def forward(c, relay, sink, n):
-        pltpu.make_async_copy(relay.at[:, c], relay.at[:, c], b_recv.at[n]).wait()
-        for way, (_, origin, far) in enumerate(hops):
-            for k in range(2):
-                p = lax.rem(origin + far + k * ring, npx)
-                remote(
-                    relay.at[2 * way + k, c], sink.at[origin, c], c_send.at[n], a_recv.at[n], (p, me_y)
-                ).start()
-
-    def complete(c, relay, sink, n):
-        pltpu.make_async_copy(sink.at[direct_x, c], sink.at[direct_x, c], a_send.at[n]).wait()
-        pltpu.make_async_copy(relay.at[:, c], relay.at[:, c], b_send.at[n]).wait()
-        pltpu.make_async_copy(relay.at[:, c], relay.at[:, c], c_send.at[n]).wait()
-        pltpu.make_async_copy(sink.at[others_x, c], sink.at[others_x, c], a_recv.at[n]).wait()
 
     loads = []
     for c in range(3):
@@ -204,9 +168,20 @@
         pltpu.make_async_copy(a, b, load_sem.at[base + 3 + n])
         for n, (a, b) in enumerate(((tz_hbm, tz), (tx_hbm, tx), (tt_hbm, tt)))
     ]
+    load_small = [
+        pltpu.make_async_copy(a, b, load_sem.at[base + 6 + n])
+        for n, (a, b) in enumerate(
+            (
+                (ids_hbm, ids), (resist_hbm, resist), (owner_hbm, owner_row), (slot_hbm, slot_row),
+                (column_hbm, column_row), (basis_hbm, basis), (lam_x_hbm, lam_x), (lam_z_hbm, lam_z),
+            )
+        )
+    ]
     for copy in loads:
         copy.start()
     load_u.start()
+    for copy in load_small:
+        copy.start()
     load_s.start()
     load_m.start()
     for copy in load_t:
@@ -261,6 +236,8 @@
     halo = y_pair(snd_y, rcv_y, 0) + x_pair(vp, at_plane, 0) + x_pair(up, at_plane, 2)
     for copy in halo:
         copy.start()
+    for copy in load_small:
+        copy.wait()
 
     count = owner_row.shape[1]
     owners = owner_row[...]
@@ -374,11 +351,8 @@
                 vp[c, h, nxl + 1, 8:top, :] = edge
                 up[c, h, nxl + 1, 8:top, :] = edge
 
-    def tall_rows(field, c, x, y):
-        return jnp.concatenate([field[c, h, x, y:y + 24, :] for h in range(halves)], axis=1)
-
-    def tile_rows(field, c, x, y):
-        return jnp.concatenate([field[c, h, x, y + 8:y + 16, :] for h in range(halves)], axis=1)
+    def rows_at(field, c, x, start, size=8):
+        return jnp.concatenate([field[c, h, x, pl.ds(start, size), :] for h in range(halves)], axis=1)
 
     tiles = nyl // 8
 
@@ -391,26 +365,23 @@
                 x = 2 * i + n // tiles
                 y = 8 * (n % tiles)
                 scale = 1.0 / (1.0 + (DT * ALPHA) * mk[x, y:y + 8, :].astype(F32))
-                u, v, tall_v = [], [], []
+                u = [rows_at(up, a, x + 1, y + 8) for a in range(3)]
+                v = [rows_at(vp, a, x + 1, y + 8) for a in range(3)]
+                low, high = y + 7 + zero_at, y + 9 + zero_at
                 slopes = [None] * 3
                 for a in range(3):
-                    tall = tall_rows(up, a, x + 1, y)
-                    tall_v.append(tall_rows(vp, a, x + 1, y))
-                    u.append(tall[8:16])
-                    v.append(tall_v[a][8:16])
                     below, above = z_shift(u[a], 0.0, 0.0)
                     diffs = (
-                        tile_rows(up, a, x + 2, y) - tile_rows(up, a, x, y),
-                        tall[9:17] - tall[7:15],
+                        rows_at(up, a, x + 2, y + 8) - rows_at(up, a, x, y + 8),
+                        rows_at(up, a, x + 1, high) - rows_at(up, a, x + 1, low),
                         above - below,
                     )
                     for b in range(3):
                         term = v[a] * diffs[b]
                         slopes[b] = term if slopes[b] is None else slopes[b] + term
                 for b in range(3):
-                    tall = tall_v[b]
-                    xm, xp = tile_rows(vp, b, x, y), tile_rows(vp, b, x + 2, y)
-                    ym, yp = tall[7:15], tall[9:17]
+                    xm, xp = rows_at(vp, b, x, y + 8), rows_at(vp, b, x + 2, y + 8)
+                    ym, yp = rows_at(vp, b, x + 1, low), rows_at(vp, b, x + 1, high)
                     zm, zp = z_shift(v[b], 0.0, 0.0)
                     convect = u[0] * (xp - xm) + u[1] * (yp - ym) + u[2] * (zp - zm)
                     lap = (xp + xm) + (yp + ym) + (zp + zm) - 6.0 * v[b]
@@ -492,8 +463,8 @@
         below, above = z_shift(deep, 0.0, 0.0)
         for h in range(halves):
             cut = slice(h * HALF, (h + 1) * HALF)
-            tall = w1[h, x + 1]
-            total = (w0[h, x + 2] - w0[h, x]) + (tall[9:top + 1] - tall[7:top - 1]) + (above - below)[:, cut]
+            rise = w1[h, x + 1, pl.ds(9 + zero_at, nyl), :] - w1[h, x + 1, pl.ds(7 + zero_at, nyl), :]
+            total = (w0[h, x + 2] - w0[h, x]) + rise + (above - below)[:, cut]
             div[h, pl.ds(x, nyl, stride=nxl), :] = 0.5 * total
         return carry
 
@@ -508,11 +479,10 @@
         out = dot_parts((tz[0], tz[1]), split(value, 2), ((1,), (1,)))
         for p in range(npx):
             msg[p, c] = out[p * kzl:(p + 1) * kzl]
-        exchange(c, msg, relay, got, c)
+        spread(npx, at_x, lambda r: msg.at[at_x(r)[0], c], got.at[me_x, c], a_send.at[c], a_recv.at[c])
         return carry
 
     lax.fori_loop(0, pieces, depth_piece, 0)
-    run(0, pieces, lambda c: forward(c, relay, got, c))
 
     settle(fr1.at[others_x], f_send.at[0], f_recv.at[0])
     fsum[1] = jnp.sum(fr1[...], axis=0)
@@ -582,7 +552,7 @@
 
     def line_piece(c, carry):
         got[me_x, c] = msg[me_x, c]
-        complete(c, relay, got, c)
+        settle(got.at[others_x, c], a_send.at[c], a_recv.at[c])
 
         def gather(sg, inner):
             for half in range(per // 4):
@@ -685,23 +655,18 @@
             return inner
 
         lax.fori_loop(0, wides, scatter, 0)
-        exchange(c, msg, relay2, got2, pieces + c)
-
-        @pl.when(n > 0)
-        def _():
-            forward(c + 1, relay2, got2, pieces + c + 1)
-
+        n = pieces + c
+        spread(npx, at_x, lambda r: msg.at[at_x(r)[0], c], got2.at[me_x, c], a_send.at[n], a_recv.at[n])
         return q
 
     lax.fori_loop(0, pieces, up_piece, back[1])
-    forward(0, relay2, got2, pieces)
 
     pressure = qp.reshape(halves, (nxl + 2) * wide, HALF)
 
     def rise_piece(n, carry):
         c = pieces - 1 - n
         got2[me_x, c] = msg[me_x, c]
-        complete(c, relay2, got2, pieces + c)
+        settle(got2.at[others_x, c], a_send.at[pieces + c], a_recv.at[pieces + c])
         value = got2[:, c].reshape(nz, 256)
         out = dot_parts(split(value.T, 3), (tz[0], tz[1], tz[2]), ((1,), (0,)))
         for y in range(per):
@@ -721,7 +686,7 @@
         copy.start()
 
     def q_rows(x, y, size):
-        return jnp.concatenate([qp[h, x, y:y + size, :] for h in range(halves)], axis=1)
+        return jnp.concatenate([qp[h, x, pl.ds(y, size), :] for h in range(halves)], axis=1)
 
     def join(field, x):
         return jnp.concatenate([field[h, x, 0:nyl, :] for h in range(halves)], axis=1)
@@ -768,9 +733,8 @@
     outs[2].start()
 
     def last_part(x, carry):
-        tall = q_rows(x + 1, 0, wide)
         deep = jnp.concatenate([w1[h, x + 1, 8:top, :] for h in range(halves)], axis=1)
-        v1 = deep - 0.5 * (tall[9:top + 1] - tall[7:top - 1])
+        v1 = deep - 0.5 * (q_rows(x + 1, 9 + zero_at, nyl) - q_rows(x + 1, 7 + zero_at, nyl))
         vel[1, x] = v1
         rows = pl.ds(pl.multiple_of(x * nyl, 8), nyl)
         part = flow(1, x) * v1
@@ -783,9 +747,9 @@
 
     picked = None
     for h in range(halves):
-        for part in reversed(split(sig[h], 2)):
-            term = jnp.dot(hot[h], part, preferred_element_type=F32)
-            picked = term if picked is None else picked + term
+        both = jnp.dot(hot[h], jnp.concatenate(split(sig[h], 2), axis=1), preferred_element_type=F32)
+        term = both[:, :SEG] + both[:, SEG:]
+        picked = term if picked is None else picked + term
     settle(fetched.at[others_x], r_send.at[3], r_recv.at[3])
     products = picked * fetched[...].reshape(places, SEG)
     ones = jnp.ones((8, SEG), BF16)
@@ -829,7 +793,7 @@
     vmem = pltpu.VMEM
     anywhere = pl.BlockSpec(memory_space=pl.ANY)
     here = pl.BlockSpec(memory_space=pltpu.VMEM)
-    scalar = pl.BlockSpec(memory_space=pltpu.SMEM)
+    far = pl.BlockSpec(memory_space=pltpu.HBM)
     dma = pltpu.SemaphoreType.DMA
     tables = args[10:13]
     field = vmem((3, halves, nxl + 2, wide, HALF), F32)
@@ -856,8 +820,6 @@
         message,
         message,
         message,
-        vmem((4, pieces, kzl, 256), F32),
-        vmem((4, pieces, kzl, 256), F32),
         vmem((nyl * kzl, nx), F32),
         line,
         line,
@@ -892,16 +854,18 @@
     ]
     scratch += [vmem(t.shape, BF16) for t in tables]
     scratch += [
-        dma((3 * halves + 3 + len(tables),)),
+        pltpu.SMEM(a.shape, a.dtype) if n == 5 else vmem(a.shape, a.dtype)
+        for n, a in enumerate(args)
+        if n > 3 and not 10 <= n < 13
+    ]
+    scratch += [
+        dma((3 * halves + 14,)),
         dma((8,)),
         dma((8,)),
         dma((6,)),
         dma((6,)),
         dma((2,)),
         dma((2,)),
-        dma((2 * pieces,)),
-        dma((2 * pieces,)),
-        dma((2 * pieces,)),
         dma((2 * pieces,)),
         dma((2 * pieces,)),
         dma((2,)),
@@ -916,11 +880,11 @@
             jax.ShapeDtypeStruct((3, nxl, nyl, nz), F32),
             jax.ShapeDtypeStruct((1, owner_rows), F32),
         ),
-        in_specs=[anywhere] * 4 + [here, scalar] + [here] * 4 + [anywhere] * len(tables) + [here] * 2,
+        in_specs=[far] * len(args),
         out_specs=(anywhere, here),
         scratch_shapes=scratch,
         compiler_params=pltpu.CompilerParams(
-            collective_id=0, has_side_effects=True, vmem_limit_bytes=36 * 2**20
+            collective_id=0, has_side_effects=True, vmem_limit_bytes=58 * 2**20
         ),
         name="project",
     )(*args)

time: 124 us -> 105 us (0.85)
  local copies, waits for them, and re-layouts: 16.6 us -> 3.75 us
  Pallas kernels: 106 us -> 100 us
    unnamed x32 -> x4, local copies, waits for them, and re-layouts: 16.6 us -> 3.75 us
    pallas_call x1, Pallas kernels: 106 us -> 100 us  [main_call(): pl.pallas_call(functools.partial(main_kernel, dims), out_shape=(jax.Shape...]
where the time goes in v5:
time: 105 us
  Pallas kernels  100 us (95%)
  local copies, waits for them, and re-layouts  3.75 us (4%)
    pallas_call x1, Pallas kernels, main_call(): pl.pallas_call(functools.partial(main_kernel, dims), out_shape=(jax.Shape...  100 us
    unnamed x4, local copies, waits for them, and re-layouts  3.75 us

profile of v5, /device:TPU:1, one launch (start us, length us, event | category | flops | bytes accessed | tf_op | source)
XLA Modules:
  0.0 104.7 jit_solution(3496602104257921959)
XLA Ops:
  0.6 100.3 %project.1 = (f32[3,32,24,256]{3,2,1,0:T(8,128)}, f32[1,32]{1,0:T(1,128)}) custom-call(f32[3,32,24,256]{3,2,1,0:T(8,128)} %v_hbm.1, bf16[3,768,256]{2,1,0:T(8,128)(2,1)} %bitcast.7, bf16[3,768,256]{2,1,0:T(8,128)(2,1)} %bitcast.8, s32[32,24,256]{2,1,0:T(8,128)} %m_hbm.1, s32[24,32]{1,0:T(8,128)} %bitcast.9, f32[8,8]{1,0:T(8,128)} %resist_hbm.1, ...), custom_call_target="tpu_custom_call" | custom-call | tf_op jit(solution)/shard_map/project/pallas_call | solution.py:877
  100.9 0.0 copy-start
  100.9 3.2 %copy.19 = f32[3,32,24,256]{3,2,1,0:T(8,128)} copy(f32[3,32,24,256]{3,2,1,0:T(8,128)} %get-tuple-element.8) | data formatting | bytes 4718592
  104.2 0.0 copy-done
  104.2 0.5 copy.20
Async XLA Ops:
  100.9 3.2 %copy-start = (f32[1,32]{1,0:T(1,128)S(1)}, f32[1,32]{1,0:T(1,128)}, u32[]{:S(2)}) copy-start(f32[1,32]{1,0:T(1,128)} %get-tuple-element.5) | copy-start | bytes 388

commit v6 on v5

--- a/solution.py
+++ b/solution.py
@@ -142,7 +142,11 @@
         return (me_x, lax.rem(me_y + r, npy))
 
     def spread(count, target, src, dst, send, recv):
-        run(1, count, lambda r: remote(src(r), dst, send, recv, target(r)).start())
+        def start(n):
+            r = lax.rem(n + (count // 2 - 2), count - 1) + 1
+            remote(src(r), dst, send, recv, target(r)).start()
+
+        run(1, count, start)
 
     def settle(like, send, recv):
         pltpu.make_async_copy(like, like, send).wait()
@@ -319,49 +323,31 @@
         positive = held > 0.0
         owner_inv[npy - 1] = jnp.where(positive, 1.0 / jnp.where(positive, held, 1.0), 0.0)
 
-    owner_table()
-    settle(asked.at[others_x], r_send.at[0], r_recv.at[0])
-    by_py(asked[:, 0, :], asks)
-    spread(npy, at_y, lambda r: asks.at[at_y(r)[1]], wanted.at[me_y], r_send.at[1], r_recv.at[1])
-    wanted[me_y] = asks[me_y]
     load_s.wait()
     load_m.wait()
-    for copy in halo:
-        copy.wait()
-
+
+    blank = jnp.zeros((nxl, HALF), F32)
     for c in range(3):
         for h in range(halves):
-            for field, first in ((vp, 0), (up, 3)):
-                low, high = rcv_y[0, first + c, h].astype(F32), rcv_y[1, first + c, h].astype(F32)
-                row_at(field, (c, h), 7)[...] = jnp.where(first_y, 0.0, low)
-                row_at(field, (c, h), top)[...] = jnp.where(last_y, 0.0, high)
-    edge = jnp.zeros((nyl, HALF), F32)
-
-    @pl.when(first_x)
-    def _():
-        for c in range(3):
-            for h in range(halves):
-                vp[c, h, 0, 8:top, :] = edge
-                up[c, h, 0, 8:top, :] = edge
-
-    @pl.when(last_x)
-    def _():
-        for c in range(3):
-            for h in range(halves):
-                vp[c, h, nxl + 1, 8:top, :] = edge
-                up[c, h, nxl + 1, 8:top, :] = edge
+            for field in (vp, up):
+                row_at(field, (c, h), 7)[...] = blank
+                row_at(field, (c, h), top)[...] = blank
 
     def rows_at(field, c, x, start, size=8):
         return jnp.concatenate([field[c, h, x, pl.ds(start, size), :] for h in range(halves)], axis=1)
 
     tiles = nyl // 8
 
-    def predict(i, carry):
+    def predict(i, planes):
         for k in range(tiles):
+            if all((2 * k + s) // tiles not in planes for s in range(2)):
+                continue
             rows = pl.ds(pl.multiple_of(i * 2 * nyl + 16 * k, 16), 16)
             forcing = [sb[b, rows, :].astype(F32) for b in range(3)]
             for s in range(2):
                 n = 2 * k + s
+                if n // tiles not in planes:
+                    continue
                 x = 2 * i + n // tiles
                 y = 8 * (n % tiles)
                 scale = 1.0 / (1.0 + (DT * ALPHA) * mk[x, y:y + 8, :].astype(F32))
@@ -395,9 +381,52 @@
                             w1[h, x + 1, y + 8:y + 16, :] = part
                         else:
                             w2[h, x, y:y + 8, :] = part
-        return carry
-
-    lax.fori_loop(0, nxl // 2, predict, 0)
+
+    pairs = nxl // 2
+    run(1, pairs // 2, lambda i: predict(i, (0, 1)))
+    settle(asked.at[others_x], r_send.at[0], r_recv.at[0])
+    by_py(asked[:, 0, :], asks)
+    spread(npy, at_y, lambda r: asks.at[at_y(r)[1]], wanted.at[me_y], r_send.at[1], r_recv.at[1])
+    wanted[me_y] = asks[me_y]
+    run(pairs // 2, pairs - 1, lambda i: predict(i, (0, 1)))
+    predict(0, (1,))
+    predict(pairs - 1, (0,))
+    for copy in halo:
+        copy.wait()
+    edge = jnp.zeros((nyl, HALF), F32)
+
+    @pl.when(first_x)
+    def _():
+        for c in range(3):
+            for h in range(halves):
+                vp[c, h, 0, 8:top, :] = edge
+                up[c, h, 0, 8:top, :] = edge
+
+    @pl.when(last_x)
+    def _():
+        for c in range(3):
+            for h in range(halves):
+                vp[c, h, nxl + 1, 8:top, :] = edge
+                up[c, h, nxl + 1, 8:top, :] = edge
+    predict(0, (0,))
+    predict(pairs - 1, (1,))
+
+    flat0 = w0.reshape(halves, (nxl + 2) * nyl, HALF)
+    flat2 = w2.reshape(halves, nxl * nyl, HALF)
+    for side, y, inside in ((0, 0, first_y), (1, nyl - 1, last_y)):
+        sign = -0.5 if side == 0 else 0.5
+        for h in range(halves):
+            solid = mk[:, y, h * HALF:(h + 1) * HALF].astype(F32)
+            scale = jnp.where(inside, 0.0, DT / (1.0 + (DT * ALPHA) * solid))
+            beyond = [rcv_y[side, n, h].astype(F32) for n in range(6)]
+            weigh = scale * (NU + sign * row_at(up, (1, h), y + 8)[...])
+            slope = sum(row_at(vp, (a, h), y + 8)[...] * beyond[3 + a] for a in range(3))
+            here = flat0.at[h, pl.ds(nyl + y, nxl, stride=nyl), :]
+            here[...] = here[...] + weigh * beyond[0]
+            here = row_at(w1, (h,), y + 8)
+            here[...] = here[...] + (weigh * beyond[1] - (sign * scale) * slope)
+            here = flat2.at[h, pl.ds(y, nxl, stride=nyl), :]
+            here[...] = here[...] + weigh * beyond[2]
 
     for h in range(halves):
         wy_snd[0, h] = row_at(w1, (h,), top - 1)[...]
@@ -496,6 +525,8 @@
     spread(npx, at_x, lambda r: fetch.at[at_x(r)[0]], fetched.at[me_x], r_send.at[3], r_recv.at[3])
     fetched[me_x] = fetch[me_x]
 
+    owner_table()
+
     def table_cell(i, carry):
         c, g = carry
         right = jnp.where((i == nyl - 1) & last_y, 0.0, 1.0)
@@ -507,11 +538,6 @@
     tau[0] = jnp.zeros_like(mu)
     kap[0] = jnp.ones_like(mu)
     lax.fori_loop(1, nyl, table_cell, (jnp.ones_like(mu), mu))
-
-    shape = (places, cells)
-    cell = lax.broadcasted_iota(jnp.int32, shape, 1) * halves
-    for h in range(halves):
-        hot[h] = (jnp.broadcast_to(pick[...], shape) == cell + h).astype(F32).astype(BF16)
 
     settle(fr2.at[others_y], f_send.at[1], f_recv.at[1])
     flux = jnp.sum(fr2[...], axis=0) * (1.0 / (nx * npy * nyl))
@@ -528,12 +554,6 @@
             drop = jnp.where(which == k, jnp.broadcast_to(press[k], which.shape), drop)
         return drop
 
-    def lower(x, carry):
-        drop = DT * jnp.where(lane == HALF - 1, pressures(idb[x]), 0.0)
-        w2[halves - 1, x] = w2[halves - 1, x] - drop
-        return carry
-
-    lax.fori_loop(0, nxl, lower, 0)
     quarter = lane // nxl
     for n in range(npx // 4):
         which = asked[4 * n, 8:top, :]
@@ -660,6 +680,18 @@
         return q
 
     lax.fori_loop(0, pieces, up_piece, back[1])
+
+    shape = (places, cells)
+    cell = lax.broadcasted_iota(jnp.int32, shape, 1) * halves
+    for h in range(halves):
+        hot[h] = (jnp.broadcast_to(pick[...], shape) == cell + h).astype(F32).astype(BF16)
+
+    def lower(x, carry):
+        drop = DT * jnp.where(lane == HALF - 1, pressures(idb[x]), 0.0)
+        w2[halves - 1, x] = w2[halves - 1, x] - drop
+        return carry
+
+    lax.fori_loop(0, nxl, lower, 0)
 
     pressure = qp.reshape(halves, (nxl + 2) * wide, HALF)
 

time: 105 us -> 103 us (0.981)
  Pallas kernels: 100 us -> 98.2 us
    pallas_call x1, Pallas kernels: 100 us -> 98.2 us  [main_call(): pl.pallas_call(functools.partial(main_kernel, dims), out_shape=(jax.Shape...]
where the time goes in v6:
time: 103 us
  Pallas kernels  98.2 us (95%)
  local copies, waits for them, and re-layouts  3.75 us (4%)
    pallas_call x1, Pallas kernels, main_call(): pl.pallas_call(functools.partial(main_kernel, dims), out_shape=(jax.Shape...  98.2 us
    unnamed x4, local copies, waits for them, and re-layouts  3.75 us

profile of v6, /device:TPU:1, one launch (start us, length us, event | category | flops | bytes accessed | tf_op | source)
XLA Modules:
  0.0 102.7 jit_solution(11940946683371293961)
XLA Ops:
  0.6 98.2 %project.1 = (f32[3,32,24,256]{3,2,1,0:T(8,128)}, f32[1,32]{1,0:T(1,128)}) custom-call(f32[3,32,24,256]{3,2,1,0:T(8,128)} %v_hbm.1, bf16[3,768,256]{2,1,0:T(8,128)(2,1)} %bitcast.7, bf16[3,768,256]{2,1,0:T(8,128)(2,1)} %bitcast.8, s32[32,24,256]{2,1,0:T(8,128)} %m_hbm.1, s32[24,32]{1,0:T(8,128)} %bitcast.9, f32[8,8]{1,0:T(8,128)} %resist_hbm.1, ...), custom_call_target="tpu_custom_call" | custom-call | tf_op jit(solution)/shard_map/project/pallas_call | solution.py:909
  98.9 0.0 copy-start
  98.9 3.2 %copy.19 = f32[3,32,24,256]{3,2,1,0:T(8,128)} copy(f32[3,32,24,256]{3,2,1,0:T(8,128)} %get-tuple-element.8) | data formatting | bytes 4718592
  102.1 0.0 copy-done
  102.1 0.5 copy.20
Async XLA Ops:
  98.9 3.2 %copy-start = (f32[1,32]{1,0:T(1,128)S(1)}, f32[1,32]{1,0:T(1,128)}, u32[]{:S(2)}) copy-start(f32[1,32]{1,0:T(1,128)} %get-tuple-element.5) | copy-start | bytes 388

commit v7 on v6

--- a/solution.py
+++ b/solution.py
@@ -143,10 +143,11 @@
 
     def spread(count, target, src, dst, send, recv):
         def start(n):
-            r = lax.rem(n + (count // 2 - 2), count - 1) + 1
+            r = (n + (count // 2 - 2)) % (count - 1) + 1
             remote(src(r), dst, send, recv, target(r)).start()
 
-        run(1, count, start)
+        for n in range(1, count):
+            start(n)
 
     def settle(like, send, recv):
         pltpu.make_async_copy(like, like, send).wait()
@@ -181,19 +182,21 @@
             )
         )
     ]
+    for copy in load_small:
+        copy.start()
     for copy in loads:
         copy.start()
     load_u.start()
-    for copy in load_small:
-        copy.start()
     load_s.start()
     load_m.start()
     for copy in load_t:
         copy.start()
 
     barrier = pltpu.get_barrier_semaphore()
-    run(1, npx, lambda r: pl.semaphore_signal(barrier, inc=1, device_id=at_x(r), device_id_type=MESH))
-    run(1, npy, lambda r: pl.semaphore_signal(barrier, inc=1, device_id=at_y(r), device_id_type=MESH))
+    for r in range(1, npx):
+        pl.semaphore_signal(barrier, inc=1, device_id=at_x(r), device_id_type=MESH)
+    for r in range(1, npy):
+        pl.semaphore_signal(barrier, inc=1, device_id=at_y(r), device_id_type=MESH)
 
     def row_at(ref, lead, y):
         lines = ref.reshape(*ref.shape[:-3], (nxl + 2) * wide, HALF)
@@ -214,32 +217,6 @@
             remote(send.at[1], recv.at[1], y_send.at[number + 1], y_recv.at[number + 1], (me_x, left_y)),
         )
 
-    for copy in loads:
-        copy.wait()
-
-    def pack(field, first):
-        for c in range(3):
-            for h in range(halves):
-                snd_y[0, first + c, h] = row_at(field, (c, h), top - 1)[...].astype(BF16)
-                snd_y[1, first + c, h] = row_at(field, (c, h), 8)[...].astype(BF16)
-
-    pack(vp, 0)
-    load_u.wait()
-
-    def widen(i, carry):
-        for a in range(3):
-            pair = ub[a, pl.ds(pl.multiple_of(i * 2 * nyl, 2 * nyl), 2 * nyl), :].astype(F32)
-            for s in range(2):
-                for h in range(halves):
-                    up[a, h, 1 + 2 * i + s, 8:top, :] = pair[s * nyl:(s + 1) * nyl, h * HALF:(h + 1) * HALF]
-        return carry
-
-    lax.fori_loop(0, nxl // 2, widen, 0)
-    pack(up, 3)
-    pl.semaphore_wait(barrier, npx - 1 + npy - 1)
-    halo = y_pair(snd_y, rcv_y, 0) + x_pair(vp, at_plane, 0) + x_pair(up, at_plane, 2)
-    for copy in halo:
-        copy.start()
     for copy in load_small:
         copy.wait()
 
@@ -289,8 +266,33 @@
         spread(npx, at_x, lambda r: ask.at[at_x(r)[0]], asked.at[me_x], r_send.at[0], r_recv.at[0])
         asked[me_x] = ask[me_x]
 
+    for copy in loads:
+        copy.wait()
+
+    def pack(field, first):
+        for c in range(3):
+            for h in range(halves):
+                snd_y[0, first + c, h] = row_at(field, (c, h), top - 1)[...].astype(BF16)
+                snd_y[1, first + c, h] = row_at(field, (c, h), 8)[...].astype(BF16)
+
+    pack(vp, 0)
+    load_u.wait()
+
+    def widen(i, carry):
+        for a in range(3):
+            pair = ub[a, pl.ds(pl.multiple_of(i * 2 * nyl, 2 * nyl), 2 * nyl), :].astype(F32)
+            for s in range(2):
+                for h in range(halves):
+                    up[a, h, 1 + 2 * i + s, 8:top, :] = pair[s * nyl:(s + 1) * nyl, h * HALF:(h + 1) * HALF]
+        return carry
+
+    lax.fori_loop(0, nxl // 2, widen, 0)
+    pack(up, 3)
+    pl.semaphore_wait(barrier, npx - 1 + npy - 1)
     ask_start()
-
+    halo = y_pair(snd_y, rcv_y, 0) + x_pair(vp, at_plane, 0) + x_pair(up, at_plane, 2)
+    for copy in halo:
+        copy.start()
     def reduce_cell(c, g, right):
         inv = 1.0 / (c + right + g)
         return inv, c * inv
@@ -350,7 +352,7 @@
                     continue
                 x = 2 * i + n // tiles
                 y = 8 * (n % tiles)
-                scale = 1.0 / (1.0 + (DT * ALPHA) * mk[x, y:y + 8, :].astype(F32))
+                scale = 1.0 - (DT * ALPHA / (1.0 + DT * ALPHA)) * mk[x, y:y + 8, :].astype(F32)
                 u = [rows_at(up, a, x + 1, y + 8) for a in range(3)]
                 v = [rows_at(vp, a, x + 1, y + 8) for a in range(3)]
                 low, high = y + 7 + zero_at, y + 9 + zero_at
@@ -383,58 +385,11 @@
                             w2[h, x, y:y + 8, :] = part
 
     pairs = nxl // 2
-    run(1, pairs // 2, lambda i: predict(i, (0, 1)))
     settle(asked.at[others_x], r_send.at[0], r_recv.at[0])
     by_py(asked[:, 0, :], asks)
     spread(npy, at_y, lambda r: asks.at[at_y(r)[1]], wanted.at[me_y], r_send.at[1], r_recv.at[1])
     wanted[me_y] = asks[me_y]
-    run(pairs // 2, pairs - 1, lambda i: predict(i, (0, 1)))
-    predict(0, (1,))
-    predict(pairs - 1, (0,))
-    for copy in halo:
-        copy.wait()
-    edge = jnp.zeros((nyl, HALF), F32)
-
-    @pl.when(first_x)
-    def _():
-        for c in range(3):
-            for h in range(halves):
-                vp[c, h, 0, 8:top, :] = edge
-                up[c, h, 0, 8:top, :] = edge
-
-    @pl.when(last_x)
-    def _():
-        for c in range(3):
-            for h in range(halves):
-                vp[c, h, nxl + 1, 8:top, :] = edge
-                up[c, h, nxl + 1, 8:top, :] = edge
-    predict(0, (0,))
-    predict(pairs - 1, (1,))
-
-    flat0 = w0.reshape(halves, (nxl + 2) * nyl, HALF)
-    flat2 = w2.reshape(halves, nxl * nyl, HALF)
-    for side, y, inside in ((0, 0, first_y), (1, nyl - 1, last_y)):
-        sign = -0.5 if side == 0 else 0.5
-        for h in range(halves):
-            solid = mk[:, y, h * HALF:(h + 1) * HALF].astype(F32)
-            scale = jnp.where(inside, 0.0, DT / (1.0 + (DT * ALPHA) * solid))
-            beyond = [rcv_y[side, n, h].astype(F32) for n in range(6)]
-            weigh = scale * (NU + sign * row_at(up, (1, h), y + 8)[...])
-            slope = sum(row_at(vp, (a, h), y + 8)[...] * beyond[3 + a] for a in range(3))
-            here = flat0.at[h, pl.ds(nyl + y, nxl, stride=nyl), :]
-            here[...] = here[...] + weigh * beyond[0]
-            here = row_at(w1, (h,), y + 8)
-            here[...] = here[...] + (weigh * beyond[1] - (sign * scale) * slope)
-            here = flat2.at[h, pl.ds(y, nxl, stride=nyl), :]
-            here[...] = here[...] + weigh * beyond[2]
-
-    for h in range(halves):
-        wy_snd[0, h] = row_at(w1, (h,), top - 1)[...]
-        wy_snd[1, h] = row_at(w1, (h,), 8)[...]
-    halo = y_pair(wy_snd, wy_rcv, 2) + x_pair(w0, lambda field, x: field.at[:, x], 4)
-    for copy in halo:
-        copy.start()
-
+    run(1, pairs // 2 + 1, lambda i: predict(i, (0, 1)))
     settle(wanted.at[others_y], r_send.at[1], r_recv.at[1])
 
     slot_lane = lax.broadcasted_iota(jnp.int32, (npx, HALF), 1).astype(F32)
@@ -456,6 +411,52 @@
         reply[j] = rows[j * 2 * npx:(j + 1) * 2 * npx]
     spread(npy, at_y, lambda r: reply.at[at_y(r)[1]], replies.at[me_y], r_send.at[2], r_recv.at[2])
     replies[me_y] = reply[me_y]
+    run(pairs // 2 + 1, pairs - 1, lambda i: predict(i, (0, 1)))
+    predict(0, (1,))
+    predict(pairs - 1, (0,))
+    for copy in halo:
+        copy.wait()
+    edge = jnp.zeros((nyl, HALF), F32)
+
+    @pl.when(first_x)
+    def _():
+        for c in range(3):
+            for h in range(halves):
+                vp[c, h, 0, 8:top, :] = edge
+                up[c, h, 0, 8:top, :] = edge
+
+    @pl.when(last_x)
+    def _():
+        for c in range(3):
+            for h in range(halves):
+                vp[c, h, nxl + 1, 8:top, :] = edge
+                up[c, h, nxl + 1, 8:top, :] = edge
+    predict(0, (0,))
+    predict(pairs - 1, (1,))
+
+    flat0 = w0.reshape(halves, (nxl + 2) * nyl, HALF)
+    flat2 = w2.reshape(halves, nxl * nyl, HALF)
+    for side, y, inside in ((0, 0, first_y), (1, nyl - 1, last_y)):
+        sign = -0.5 if side == 0 else 0.5
+        for h in range(halves):
+            solid = mk[:, y, h * HALF:(h + 1) * HALF].astype(F32)
+            scale = jnp.where(inside, 0.0, DT - (DT * DT * ALPHA / (1.0 + DT * ALPHA)) * solid)
+            beyond = [rcv_y[side, n, h].astype(F32) for n in range(6)]
+            weigh = scale * (NU + sign * row_at(up, (1, h), y + 8)[...])
+            slope = sum(row_at(vp, (a, h), y + 8)[...] * beyond[3 + a] for a in range(3))
+            here = flat0.at[h, pl.ds(nyl + y, nxl, stride=nyl), :]
+            here[...] = here[...] + weigh * beyond[0]
+            here = row_at(w1, (h,), y + 8)
+            here[...] = here[...] + (weigh * beyond[1] - (sign * scale) * slope)
+            here = flat2.at[h, pl.ds(y, nxl, stride=nyl), :]
+            here[...] = here[...] + weigh * beyond[2]
+
+    for h in range(halves):
+        wy_snd[0, h] = row_at(w1, (h,), top - 1)[...]
+        wy_snd[1, h] = row_at(w1, (h,), 8)[...]
+    halo = y_pair(wy_snd, wy_rcv, 2) + x_pair(w0, lambda field, x: field.at[:, x], 4)
+    for copy in halo:
+        copy.start()
 
     lane = lax.broadcasted_iota(jnp.int32, (nyl, HALF), 1)
 
@@ -509,21 +510,17 @@
         for p in range(npx):
             msg[p, c] = out[p * kzl:(p + 1) * kzl]
         spread(npx, at_x, lambda r: msg.at[at_x(r)[0], c], got.at[me_x, c], a_send.at[c], a_recv.at[c])
+
+        @pl.when(c == 0)
+        def _():
+            settle(fr1.at[others_x], f_send.at[0], f_recv.at[0])
+            fsum[1] = jnp.sum(fr1[...], axis=0)
+            spread(npy, at_y, lambda r: fsum.at[1], fr2.at[me_y], f_send.at[1], f_recv.at[1])
+            fr2[me_y] = fsum[1]
+
         return carry
 
     lax.fori_loop(0, pieces, depth_piece, 0)
-
-    settle(fr1.at[others_x], f_send.at[0], f_recv.at[0])
-    fsum[1] = jnp.sum(fr1[...], axis=0)
-    spread(npy, at_y, lambda r: fsum.at[1], fr2.at[me_y], f_send.at[1], f_recv.at[1])
-    fr2[me_y] = fsum[1]
-    settle(replies.at[others_y], r_send.at[2], r_recv.at[2])
-    lines = replies.reshape(npy * 2 * npx, SEG)
-    for p in range(npx):
-        for r in range(2):
-            fetch[p, r * npy:(r + 1) * npy, :] = lines[pl.ds(r * npx + p, npy, stride=2 * npx), :]
-    spread(npx, at_x, lambda r: fetch.at[at_x(r)[0]], fetched.at[me_x], r_send.at[3], r_recv.at[3])
-    fetched[me_x] = fetch[me_x]
 
     owner_table()
 
@@ -613,6 +610,13 @@
 
     spread(npy, at_y, lambda r: isnd.at[at_y(r)[1]], ircv.at[me_y], i_send.at[0], i_recv.at[0])
     ircv[me_y] = isnd[me_y]
+    settle(replies.at[others_y], r_send.at[2], r_recv.at[2])
+    lines = replies.reshape(npy * 2 * npx, SEG)
+    for p in range(npx):
+        for r in range(2):
+            fetch[p, r * npy:(r + 1) * npy, :] = lines[pl.ds(r * npx + p, npy, stride=2 * npx), :]
+    spread(npx, at_x, lambda r: fetch.at[at_x(r)[0]], fetched.at[me_x], r_send.at[3], r_recv.at[3])
+    fetched[me_x] = fetch[me_x]
     settle(ircv.at[others_y], i_send.at[0], i_recv.at[0])
 
     rho = []
@@ -784,26 +788,26 @@
         picked = term if picked is None else picked + term
     settle(fetched.at[others_x], r_send.at[3], r_recv.at[3])
     products = picked * fetched[...].reshape(places, SEG)
-    ones = jnp.ones((8, SEG), BF16)
-    totals = sum(
-        lax.dot_general(ones, part, (((1,), (1,)), ((), ())), preferred_element_type=F32)
-        for part in reversed(split(products, 3))
-    )
-    by_px(totals, give)
+    totals = jnp.broadcast_to(jnp.sum(products, axis=1, keepdims=True), (places, HALF))
+    for p in range(npx):
+        give[p] = totals[p * group:(p + 1) * group]
     spread(npx, at_x, lambda r: give.at[at_x(r)[0]], given.at[me_x], r_send.at[4], r_recv.at[4])
     given[me_x] = give[me_x]
     settle(given.at[others_x], r_send.at[4], r_recv.at[4])
-    by_py(given[:, 0, :], gives)
+    lines = given.reshape(npx * group, HALF)
+    for j in range(npy):
+        for r in range(2):
+            gives[j, r * npx:(r + 1) * npx, :] = lines[pl.ds(r * npy + j, npx, stride=group), :]
     spread(npy, at_y, lambda r: gives.at[at_y(r)[1]], taken.at[me_y], r_send.at[5], r_recv.at[5])
     taken[me_y] = gives[me_y]
     settle(taken.at[others_y], r_send.at[5], r_recv.at[5])
 
     def add_up(j, total):
-        label, value = wanted[j], taken[j]
+        label = wanted[j]
         for r in range(2):
             spot = slice(r * npy, r * npy + 1)
             hit = jnp.broadcast_to(label[:, spot], (npx, HALF)) == slot_lane
-            total = total + jnp.where(hit, jnp.broadcast_to(value[:, spot], (npx, HALF)), 0.0)
+            total = total + jnp.where(hit, taken[j, r * npx:(r + 1) * npx, :], 0.0)
         return total
 
     total = lax.fori_loop(0, npy, add_up, jnp.zeros((npx, HALF), F32))
@@ -879,10 +883,10 @@
         vmem((npy, 2 * npx, SEG), F32),
         vmem((npx, 2 * npy, SEG), F32),
         vmem((npx, 2 * npy, SEG), F32),
-        vmem((npx, 8, HALF), F32),
-        vmem((npx, 8, HALF), F32),
-        vmem((npy, npx, HALF), F32),
-        vmem((npy, npx, HALF), F32),
+        vmem((npx, 2 * npy, HALF), F32),
+        vmem((npx, 2 * npy, HALF), F32),
+        vmem((npy, 2 * npx, HALF), F32),
+        vmem((npy, 2 * npx, HALF), F32),
     ]
     scratch += [vmem(t.shape, BF16) for t in tables]
     scratch += [

time: 103 us -> 107 us (1.039)
  Pallas kernels: 98.2 us -> 102 us
    pallas_call x1, Pallas kernels: 98.2 us -> 102 us  [main_call(): pl.pallas_call(functools.partial(main_kernel, dims), out_shape=(jax.Shape...]
where the time goes in v7:
time: 107 us
  Pallas kernels  102 us (95%)
  local copies, waits for them, and re-layouts  3.75 us (4%)
    pallas_call x1, Pallas kernels, main_call(): pl.pallas_call(functools.partial(main_kernel, dims), out_shape=(jax.Shape...  102 us
    unnamed x4, local copies, waits for them, and re-layouts  3.75 us

profile of v7, /device:TPU:1, one launch (start us, length us, event | category | flops | bytes accessed | tf_op | source)
XLA Modules:
  0.0 106.8 jit_solution(8983737721918848378)
XLA Ops:
  0.6 102.4 %project.1 = (f32[3,32,24,256]{3,2,1,0:T(8,128)}, f32[1,32]{1,0:T(1,128)}) custom-call(f32[3,32,24,256]{3,2,1,0:T(8,128)} %v_hbm.1, bf16[3,768,256]{2,1,0:T(8,128)(2,1)} %bitcast.7, bf16[3,768,256]{2,1,0:T(8,128)(2,1)} %bitcast.8, s32[32,24,256]{2,1,0:T(8,128)} %m_hbm.1, s32[24,32]{1,0:T(8,128)} %bitcast.9, f32[8,8]{1,0:T(8,128)} %resist_hbm.1, ...), custom_call_target="tpu_custom_call" | custom-call | tf_op jit(solution)/shard_map/project/pallas_call | solution.py:913
  103.0 0.0 copy-start
  103.0 3.2 %copy.19 = f32[3,32,24,256]{3,2,1,0:T(8,128)} copy(f32[3,32,24,256]{3,2,1,0:T(8,128)} %get-tuple-element.8) | data formatting | bytes 4718592
  106.3 0.0 copy-done
  106.3 0.5 copy.20
Async XLA Ops:
  103.0 3.2 %copy-start = (f32[1,32]{1,0:T(1,128)S(1)}, f32[1,32]{1,0:T(1,128)}, u32[]{:S(2)}) copy-start(f32[1,32]{1,0:T(1,128)} %get-tuple-element.5) | copy-start | bytes 388

commit v8 on v6

--- a/solution.py
+++ b/solution.py
@@ -99,9 +99,9 @@
     vp, up, ub, sb, mk, idb, w0, w1, w2, snd_y, rcv_y, wy_snd, wy_rcv, fsum, fr1, fr2,
     div, msg, got, got2, cols, tau, kap, owner_inv, owner_phi,
     isnd, ircv, jsnd, jrcv, back, qp, qy_snd, qy_rcv, vel, sig,
-    outlet, hot, pick, ask, asked, asks, wanted, chosen, reply, replies, fetch, fetched, give, given, gives, taken,
+    outlet, hot, pick, ask, asked, asks, wanted, chosen, reply, replies, fetch, fetched, give, given, gives, taken, stack, level,
     tz, tx, tt, ids, resist, owner_row, slot_row, column_row, basis, lam_x, lam_z,
-    load_sem, x_send, x_recv, y_send, y_recv, f_send, f_recv, a_send, a_recv, i_send, i_recv, r_send, r_recv, out_sem,
+    load_sem, x_send, x_recv, y_send, y_recv, f_send, f_recv, a_send, a_recv, i_send, i_recv, l_send, l_recv, r_send, r_recv, out_sem,
 ):
     npx, npy, nxl, nyl, nz = dims
     nx = npx * nxl
@@ -181,11 +181,11 @@
             )
         )
     ]
+    for copy in load_small:
+        copy.start()
     for copy in loads:
         copy.start()
     load_u.start()
-    for copy in load_small:
-        copy.start()
     load_s.start()
     load_m.start()
     for copy in load_t:
@@ -274,8 +274,15 @@
             ref[p, 0:8, :] = pltpu.roll(row, (lanes - group * p) % lanes, 1)[:, :HALF]
 
     def by_py(rows, ref):
+        full = jnp.concatenate([rows, jnp.zeros((HALF - npx, HALF), F32)], axis=0).T
         for j in range(npy):
-            ref[j] = pltpu.roll(rows, (HALF - j) % HALF, 1)
+            for r in range(2):
+                ref[j, r:r + 1, :] = full[r * npy + j:r * npy + j + 1]
+
+    def from_py(ref):
+        for j in range(npy):
+            stack[2 * j:2 * j + 2, :] = ref[j]
+        return stack[...].T[0:npx]
 
     by_px(requests, ask)
     seen = ids[...]
@@ -350,7 +357,7 @@
                     continue
                 x = 2 * i + n // tiles
                 y = 8 * (n % tiles)
-                scale = 1.0 / (1.0 + (DT * ALPHA) * mk[x, y:y + 8, :].astype(F32))
+                scale = 1.0 - (DT * ALPHA / (1.0 + DT * ALPHA)) * mk[x, y:y + 8, :].astype(F32)
                 u = [rows_at(up, a, x + 1, y + 8) for a in range(3)]
                 v = [rows_at(vp, a, x + 1, y + 8) for a in range(3)]
                 low, high = y + 7 + zero_at, y + 9 + zero_at
@@ -417,7 +424,7 @@
         sign = -0.5 if side == 0 else 0.5
         for h in range(halves):
             solid = mk[:, y, h * HALF:(h + 1) * HALF].astype(F32)
-            scale = jnp.where(inside, 0.0, DT / (1.0 + (DT * ALPHA) * solid))
+            scale = jnp.where(inside, 0.0, DT - (DT * DT * ALPHA / (1.0 + DT * ALPHA)) * solid)
             beyond = [rcv_y[side, n, h].astype(F32) for n in range(6)]
             weigh = scale * (NU + sign * row_at(up, (1, h), y + 8)[...])
             slope = sum(row_at(vp, (a, h), y + 8)[...] * beyond[3 + a] for a in range(3))
@@ -439,14 +446,10 @@
 
     slot_lane = lax.broadcasted_iota(jnp.int32, (npx, HALF), 1).astype(F32)
 
-    def choose(j, carry):
-        label = wanted[j]
-        for r in range(2):
-            hit = jnp.broadcast_to(label[:, r * npy:r * npy + 1], (npx, HALF)) == slot_lane
-            chosen[pl.ds(pl.multiple_of((2 * j + r) * npx, npx), npx), :] = hit.astype(F32).astype(BF16)
-        return carry
-
-    lax.fori_loop(0, npy, choose, 0)
+    labels = from_py(wanted)
+    for n in range(2 * npy):
+        hit = jnp.broadcast_to(labels[:, n:n + 1], (npx, HALF)) == slot_lane
+        chosen[n * npx:(n + 1) * npx, :] = hit.astype(F32).astype(BF16)
     controls = basis.shape[0]
     wide_basis = jnp.concatenate([basis[...], jnp.zeros((HALF - controls, SEG), F32)], axis=0)
     rows = sum(
@@ -454,8 +457,6 @@
     )
     for j in range(npy):
         reply[j] = rows[j * 2 * npx:(j + 1) * 2 * npx]
-    spread(npy, at_y, lambda r: reply.at[at_y(r)[1]], replies.at[me_y], r_send.at[2], r_recv.at[2])
-    replies[me_y] = reply[me_y]
 
     lane = lax.broadcasted_iota(jnp.int32, (nyl, HALF), 1)
 
@@ -509,22 +510,20 @@
         for p in range(npx):
             msg[p, c] = out[p * kzl:(p + 1) * kzl]
         spread(npx, at_x, lambda r: msg.at[at_x(r)[0], c], got.at[me_x, c], a_send.at[c], a_recv.at[c])
+
+        @pl.when(c == 0)
+        def _():
+            settle(fr1.at[others_x], f_send.at[0], f_recv.at[0])
+            fsum[1] = jnp.sum(fr1[...], axis=0)
+            spread(npy, at_y, lambda r: fsum.at[1], fr2.at[me_y], f_send.at[1], f_recv.at[1])
+            fr2[me_y] = fsum[1]
+
         return carry
 
     lax.fori_loop(0, pieces, depth_piece, 0)
 
-    settle(fr1.at[others_x], f_send.at[0], f_recv.at[0])
-    fsum[1] = jnp.sum(fr1[...], axis=0)
-    spread(npy, at_y, lambda r: fsum.at[1], fr2.at[me_y], f_send.at[1], f_recv.at[1])
-    fr2[me_y] = fsum[1]
-    settle(replies.at[others_y], r_send.at[2], r_recv.at[2])
-    lines = replies.reshape(npy * 2 * npx, SEG)
-    for p in range(npx):
-        for r in range(2):
-            fetch[p, r * npy:(r + 1) * npy, :] = lines[pl.ds(r * npx + p, npy, stride=2 * npx), :]
-    spread(npx, at_x, lambda r: fetch.at[at_x(r)[0]], fetched.at[me_x], r_send.at[3], r_recv.at[3])
-    fetched[me_x] = fetch[me_x]
-
+    spread(npy, at_y, lambda r: reply.at[at_y(r)[1]], replies.at[me_y], r_send.at[2], r_recv.at[2])
+    replies[me_y] = reply[me_y]
     owner_table()
 
     def table_cell(i, carry):
@@ -634,20 +633,54 @@
     value = -owner_inv[npy - 1] * rho[npy - 1]
     jsnd[npy - 1, 0:kown, :] = value
     jsnd[npy - 1, kown:2 * kown, :] = jnp.zeros_like(value)
-    jsnd[npy - 1, 2 * kown:3 * kown, :] = mean
     for b in range(npy - 2, -1, -1):
         jsnd[b, kown:2 * kown, :] = value
         value = owner_phi[b] * value - owner_inv[b] * rho[b]
         jsnd[b, 0:kown, :] = value
-        jsnd[b, 2 * kown:3 * kown, :] = mean
+
+    level[0] = mean[0:1, 0:HALF]
+    has_mean = (me_x == 0) & first_y
+
+    def tell(r):
+        return remote(level.at[0], level.at[1], l_send.at[r], l_recv.at[0], at_y(r))
+
+    @pl.when(has_mean)
+    def _():
+        run(1, npy, lambda r: tell(r).start())
 
     spread(npy, at_y, lambda r: jsnd.at[at_y(r)[1]], jrcv.at[me_y], i_send.at[1], i_recv.at[1])
     jrcv[me_y] = jsnd[me_y]
+    settle(replies.at[others_y], r_send.at[2], r_recv.at[2])
+    lines = replies.reshape(npy * 2 * npx, SEG)
+    for p in range(npx):
+        for r in range(2):
+            fetch[p, r * npy:(r + 1) * npy, :] = lines[pl.ds(r * npx + p, npy, stride=2 * npx), :]
+    spread(npx, at_x, lambda r: fetch.at[at_x(r)[0]], fetched.at[me_x], r_send.at[3], r_recv.at[3])
+    fetched[me_x] = fetch[me_x]
+
     settle(jrcv.at[others_y], i_send.at[1], i_recv.at[1])
+
+    @pl.when(has_mean)
+    def _():
+        run(1, npy, lambda r: tell(r).wait_send())
+        level[1] = level[0]
+
+    @pl.when((me_x == 0) & (me_y > 0))
+    def _():
+        pltpu.make_async_copy(level.at[1], level.at[1], l_recv.at[0]).wait()
+
+    @pl.when(me_x > 0)
+    def _():
+        level[1] = jnp.zeros((1, HALF), F32)
+
     for j in range(npy):
-        for part in range(3):
+        for part in range(2):
             back[part, j * kown:(j + 1) * kown, :] = jrcv[j, part * kown:(part + 1) * kown, :]
-    first_value, mean_rows = back[0], back[2]
+    first_value = back[0]
+    corner = (lax.broadcasted_iota(jnp.int32, (kzl, nx), 0) == 0) & (
+        lax.broadcasted_iota(jnp.int32, (kzl, nx), 1) == 0
+    )
+    mean_rows = jnp.where(corner, jnp.broadcast_to(level[1, :, 0:1], (kzl, nx)), 0.0)
 
     def up_piece(n, q):
         c = pieces - 1 - n
@@ -784,11 +817,7 @@
         picked = term if picked is None else picked + term
     settle(fetched.at[others_x], r_send.at[3], r_recv.at[3])
     products = picked * fetched[...].reshape(places, SEG)
-    ones = jnp.ones((8, SEG), BF16)
-    totals = sum(
-        lax.dot_general(ones, part, (((1,), (1,)), ((), ())), preferred_element_type=F32)
-        for part in reversed(split(products, 3))
-    )
+    totals = jnp.broadcast_to(jnp.sum(products, axis=1, keepdims=True), (places, HALF)).T[0:8]
     by_px(totals, give)
     spread(npx, at_x, lambda r: give.at[at_x(r)[0]], given.at[me_x], r_send.at[4], r_recv.at[4])
     given[me_x] = give[me_x]
@@ -798,15 +827,11 @@
     taken[me_y] = gives[me_y]
     settle(taken.at[others_y], r_send.at[5], r_recv.at[5])
 
-    def add_up(j, total):
-        label, value = wanted[j], taken[j]
-        for r in range(2):
-            spot = slice(r * npy, r * npy + 1)
-            hit = jnp.broadcast_to(label[:, spot], (npx, HALF)) == slot_lane
-            total = total + jnp.where(hit, jnp.broadcast_to(value[:, spot], (npx, HALF)), 0.0)
-        return total
-
-    total = lax.fori_loop(0, npy, add_up, jnp.zeros((npx, HALF), F32))
+    values = from_py(taken)
+    total = jnp.zeros((npx, HALF), F32)
+    for n in range(2 * npy):
+        hit = jnp.broadcast_to(labels[:, n:n + 1], (npx, HALF)) == slot_lane
+        total = total + jnp.where(hit, jnp.broadcast_to(values[:, n:n + 1], (npx, HALF)), 0.0)
     grad_out[...] = jnp.sum(total, axis=0, keepdims=True)[:, :controls]
     for copy in outs:
         copy.wait()
@@ -859,9 +884,9 @@
         vmem((npy, kown, nx), F32),
         vmem((npy, 2 * kown, nx), F32),
         vmem((npy, 2 * kown, nx), F32),
-        vmem((npy, 3 * kown, nx), F32),
-        vmem((npy, 3 * kown, nx), F32),
-        vmem((3, kzl, nx), F32),
+        vmem((npy, 2 * kown, nx), F32),
+        vmem((npy, 2 * kown, nx), F32),
+        vmem((2, kzl, nx), F32),
         vmem((halves, nxl + 2, wide, HALF), F32),
         vmem((2, halves, nxl, HALF), F32),
         vmem((2, halves, nxl, HALF), F32),
@@ -872,8 +897,8 @@
         vmem((places, 1), jnp.int32),
         vmem((npx, 8 + nyl, HALF), F32),
         vmem((npx, 8 + nyl, HALF), F32),
-        vmem((npy, npx, HALF), F32),
-        vmem((npy, npx, HALF), F32),
+        vmem((npy, 2, HALF), F32),
+        vmem((npy, 2, HALF), F32),
         vmem((places, HALF), BF16),
         vmem((npy, 2 * npx, SEG), F32),
         vmem((npy, 2 * npx, SEG), F32),
@@ -881,8 +906,10 @@
         vmem((npx, 2 * npy, SEG), F32),
         vmem((npx, 8, HALF), F32),
         vmem((npx, 8, HALF), F32),
-        vmem((npy, npx, HALF), F32),
-        vmem((npy, npx, HALF), F32),
+        vmem((npy, 2, HALF), F32),
+        vmem((npy, 2, HALF), F32),
+        vmem((2 * npy, HALF), F32),
+        vmem((2, 1, HALF), F32),
     ]
     scratch += [vmem(t.shape, BF16) for t in tables]
     scratch += [
@@ -902,6 +929,8 @@
         dma((2 * pieces,)),
         dma((2,)),
         dma((2,)),
+        dma((npy,)),
+        dma((1,)),
         dma((6,)),
         dma((6,)),
         dma((3,)),

time: 103 us -> 95.9 us (0.931)
  Pallas kernels: 98.2 us -> 91.4 us
    pallas_call x1, Pallas kernels: 98.2 us -> 91.4 us  [main_call(): pl.pallas_call(functools.partial(main_kernel, dims), out_shape=(jax.Shape...]
where the time goes in v8:
time: 95.9 us; the launch traced here: 95.8 us
  Pallas kernels  91.4 us (95%)
  local copies, waits for them, and re-layouts  3.75 us (4%)
    pallas_call x1, Pallas kernels, main_call(): pl.pallas_call(functools.partial(main_kernel, dims), out_shape=(jax.Shape...  91.4 us
    unnamed x4, local copies, waits for them, and re-layouts  3.75 us

profile of v8, /device:TPU:1, one launch (start us, length us, event | category | flops | bytes accessed | tf_op | source)
XLA Modules:
  0.0 95.8 jit_solution(8776308290695341610)
XLA Ops:
  0.6 91.4 %project.1 = (f32[3,32,24,256]{3,2,1,0:T(8,128)}, f32[1,32]{1,0:T(1,128)}) custom-call(f32[3,32,24,256]{3,2,1,0:T(8,128)} %v_hbm.1, bf16[3,768,256]{2,1,0:T(8,128)(2,1)} %bitcast.7, bf16[3,768,256]{2,1,0:T(8,128)(2,1)} %bitcast.8, s32[32,24,256]{2,1,0:T(8,128)} %m_hbm.1, s32[24,32]{1,0:T(8,128)} %bitcast.9, f32[8,8]{1,0:T(8,128)} %resist_hbm.1, ...), custom_call_target="tpu_custom_call" | custom-call | tf_op jit(solution)/shard_map/project/pallas_call | solution.py:938
  92.0 0.0 copy-start
  92.1 3.2 %copy.19 = f32[3,32,24,256]{3,2,1,0:T(8,128)} copy(f32[3,32,24,256]{3,2,1,0:T(8,128)} %get-tuple-element.8) | data formatting | bytes 4718592
  95.3 0.0 copy-done
  95.3 0.5 copy.20
Async XLA Ops:
  92.0 3.2 %copy-start = (f32[1,32]{1,0:T(1,128)S(1)}, f32[1,32]{1,0:T(1,128)}, u32[]{:S(2)}) copy-start(f32[1,32]{1,0:T(1,128)} %get-tuple-element.5) | copy-start | bytes 388

commit v9 on v8

--- a/solution.py
+++ b/solution.py
@@ -143,10 +143,11 @@
 
     def spread(count, target, src, dst, send, recv):
         def start(n):
-            r = lax.rem(n + (count // 2 - 2), count - 1) + 1
+            r = (n + (count // 2 - 2)) % (count - 1) + 1
             remote(src(r), dst, send, recv, target(r)).start()
 
-        run(1, count, start)
+        for n in range(1, count):
+            start(n)
 
     def settle(like, send, recv):
         pltpu.make_async_copy(like, like, send).wait()
@@ -192,8 +193,10 @@
         copy.start()
 
     barrier = pltpu.get_barrier_semaphore()
-    run(1, npx, lambda r: pl.semaphore_signal(barrier, inc=1, device_id=at_x(r), device_id_type=MESH))
-    run(1, npy, lambda r: pl.semaphore_signal(barrier, inc=1, device_id=at_y(r), device_id_type=MESH))
+    for r in range(1, npx):
+        pl.semaphore_signal(barrier, inc=1, device_id=at_x(r), device_id_type=MESH)
+    for r in range(1, npy):
+        pl.semaphore_signal(barrier, inc=1, device_id=at_y(r), device_id_type=MESH)
 
     def row_at(ref, lead, y):
         lines = ref.reshape(*ref.shape[:-3], (nxl + 2) * wide, HALF)
@@ -267,11 +270,11 @@
             return row
         return jnp.concatenate([row, jnp.zeros((8, HALF - row.shape[1]), F32)], axis=1)
 
-    def by_px(row, ref):
+    def by_px(row, ref, rows=8):
         row = pad_lanes(row)
         lanes = row.shape[1]
         for p in range(npx):
-            ref[p, 0:8, :] = pltpu.roll(row, (lanes - group * p) % lanes, 1)[:, :HALF]
+            ref[p, 0:rows, :] = pltpu.roll(row, (lanes - group * p) % lanes, 1)[0:rows, :HALF]
 
     def by_py(rows, ref):
         full = jnp.concatenate([rows, jnp.zeros((HALF - npx, HALF), F32)], axis=0).T
@@ -818,11 +821,13 @@
     settle(fetched.at[others_x], r_send.at[3], r_recv.at[3])
     products = picked * fetched[...].reshape(places, SEG)
     totals = jnp.broadcast_to(jnp.sum(products, axis=1, keepdims=True), (places, HALF)).T[0:8]
-    by_px(totals, give)
+    by_px(totals, give, 1)
     spread(npx, at_x, lambda r: give.at[at_x(r)[0]], given.at[me_x], r_send.at[4], r_recv.at[4])
     given[me_x] = give[me_x]
     settle(given.at[others_x], r_send.at[4], r_recv.at[4])
-    by_py(given[:, 0, :], gives)
+    for p in range(npx):
+        stack[p:p + 1, :] = given[p]
+    by_py(stack[0:npx, :], gives)
     spread(npy, at_y, lambda r: gives.at[at_y(r)[1]], taken.at[me_y], r_send.at[5], r_recv.at[5])
     taken[me_y] = gives[me_y]
     settle(taken.at[others_y], r_send.at[5], r_recv.at[5])
@@ -904,8 +909,8 @@
         vmem((npy, 2 * npx, SEG), F32),
         vmem((npx, 2 * npy, SEG), F32),
         vmem((npx, 2 * npy, SEG), F32),
-        vmem((npx, 8, HALF), F32),
-        vmem((npx, 8, HALF), F32),
+        vmem((npx, 1, HALF), F32),
+        vmem((npx, 1, HALF), F32),
         vmem((npy, 2, HALF), F32),
         vmem((npy, 2, HALF), F32),
         vmem((2 * npy, HALF), F32),

time: 95.9 us -> 94.3 us (0.983)
  Pallas kernels: 91.4 us -> 89.8 us
    pallas_call x1, Pallas kernels: 91.4 us -> 89.8 us  [main_call(): pl.pallas_call(functools.partial(main_kernel, dims), out_shape=(jax.Shape...]
where the time goes in v9:
time: 94.3 us; the launch traced here: 94.2 us
  Pallas kernels  89.8 us (95%)
  local copies, waits for them, and re-layouts  3.75 us (4%)
    pallas_call x1, Pallas kernels, main_call(): pl.pallas_call(functools.partial(main_kernel, dims), out_shape=(jax.Shape...  89.8 us
    unnamed x4, local copies, waits for them, and re-layouts  3.75 us

profile of v9, /device:TPU:1, one launch (start us, length us, event | category | flops | bytes accessed | tf_op | source)
XLA Modules:
  0.0 94.2 jit_solution(15771256728154410346)
XLA Ops:
  0.6 89.8 %project.1 = (f32[3,32,24,256]{3,2,1,0:T(8,128)}, f32[1,32]{1,0:T(1,128)}) custom-call(f32[3,32,24,256]{3,2,1,0:T(8,128)} %v_hbm.1, bf16[3,768,256]{2,1,0:T(8,128)(2,1)} %bitcast.7, bf16[3,768,256]{2,1,0:T(8,128)(2,1)} %bitcast.8, s32[32,24,256]{2,1,0:T(8,128)} %m_hbm.1, s32[24,32]{1,0:T(8,128)} %bitcast.9, f32[8,8]{1,0:T(8,128)} %resist_hbm.1, ...), custom_call_target="tpu_custom_call" | custom-call | tf_op jit(solution)/shard_map/project/pallas_call | solution.py:943
  90.5 0.0 copy-start
  90.5 3.2 %copy.19 = f32[3,32,24,256]{3,2,1,0:T(8,128)} copy(f32[3,32,24,256]{3,2,1,0:T(8,128)} %get-tuple-element.8) | data formatting | bytes 4718592
  93.7 0.0 copy-done
  93.7 0.5 copy.20
Async XLA Ops:
  90.5 3.2 %copy-start = (f32[1,32]{1,0:T(1,128)S(1)}, f32[1,32]{1,0:T(1,128)}, u32[]{:S(2)}) copy-start(f32[1,32]{1,0:T(1,128)} %get-tuple-element.5) | copy-start | bytes 388

commit v10 on v9

--- a/solution.py
+++ b/solution.py
@@ -140,6 +140,14 @@
 
     def at_y(r):
         return (me_x, lax.rem(me_y + r, npy))
+
+    def by_twos(first, last, body):
+        def step(i, carry):
+            body(first + 2 * i, 0)
+            body(first + 2 * i + 1, 0)
+            return carry
+
+        lax.fori_loop(0, (last - first) // 2, step, 0)
 
     def spread(count, target, src, dst, send, recv):
         def start(n):
@@ -501,7 +509,7 @@
             div[h, pl.ds(x, nyl, stride=nxl), :] = 0.5 * total
         return carry
 
-    lax.fori_loop(0, nxl, diverge, 0)
+    by_twos(0, nxl, diverge)
 
     for copy in load_t:
         copy.wait()
@@ -776,7 +784,7 @@
             sig[h, pl.ds(pl.multiple_of(x * nyl, 8), nyl), :] = total[:, h * HALF:(h + 1) * HALF]
         return carry
 
-    lax.fori_loop(1, nxl - 1, two_parts, 0)
+    by_twos(1, nxl - 1, two_parts)
     outs = [pltpu.make_async_copy(vel.at[b], v_out.at[b], out_sem.at[b]) for b in range(3)]
 
     for copy in halo:
@@ -810,7 +818,7 @@
             sig[h, rows, :] = -ALPHA * (sig[h, rows, :] + part[:, h * HALF:(h + 1) * HALF])
         return carry
 
-    lax.fori_loop(0, nxl, last_part, 0)
+    by_twos(0, nxl, last_part)
     outs[1].start()
 
     picked = None

time: 94.3 us -> 93.2 us (0.988)
  Pallas kernels: 89.8 us -> 88.7 us
    pallas_call x1, Pallas kernels: 89.8 us -> 88.7 us  [main_call(): pl.pallas_call(functools.partial(main_kernel, dims), out_shape=(jax.Shape...]
where the time goes in v10:
time: 93.2 us; the launch traced here: 93.1 us
  Pallas kernels  88.7 us (95%)
  local copies, waits for them, and re-layouts  3.75 us (4%)
    pallas_call x1, Pallas kernels, main_call(): pl.pallas_call(functools.partial(main_kernel, dims), out_shape=(jax.Shape...  88.7 us
    unnamed x4, local copies, waits for them, and re-layouts  3.75 us

profile of v10, /device:TPU:1, one launch (start us, length us, event | category | flops | bytes accessed | tf_op | source)
XLA Modules:
  0.0 93.1 jit_solution(12494591571348731313)
XLA Ops:
  0.6 88.7 %project.1 = (f32[3,32,24,256]{3,2,1,0:T(8,128)}, f32[1,32]{1,0:T(1,128)}) custom-call(f32[3,32,24,256]{3,2,1,0:T(8,128)} %v_hbm.1, bf16[3,768,256]{2,1,0:T(8,128)(2,1)} %bitcast.7, bf16[3,768,256]{2,1,0:T(8,128)(2,1)} %bitcast.8, s32[32,24,256]{2,1,0:T(8,128)} %m_hbm.1, s32[24,32]{1,0:T(8,128)} %bitcast.9, f32[8,8]{1,0:T(8,128)} %resist_hbm.1, ...), custom_call_target="tpu_custom_call" | custom-call | tf_op jit(solution)/shard_map/project/pallas_call | solution.py:951
  89.4 0.0 copy-start
  89.4 3.2 %copy.19 = f32[3,32,24,256]{3,2,1,0:T(8,128)} copy(f32[3,32,24,256]{3,2,1,0:T(8,128)} %get-tuple-element.8) | data formatting | bytes 4718592
  92.6 0.0 copy-done
  92.6 0.5 copy.20
Async XLA Ops:
  89.4 3.2 %copy-start = (f32[1,32]{1,0:T(1,128)S(1)}, f32[1,32]{1,0:T(1,128)}, u32[]{:S(2)}) copy-start(f32[1,32]{1,0:T(1,128)} %get-tuple-element.5) | copy-start | bytes 388
